TPU v7x, 32 devices: a whole 2x2x4 slice. The times are simulated.
32 devices in a mesh: seq: 16 (over z, y, x), head: 2 (over core).
Axes of the slice: x: 2, y: 2, z: 4, core: 2. Of those that a mesh axis runs over, the one named last changes fastest.
Arguments:
- hidden_in: bfloat16 [16384, 768], P('seq'), may hold values from -6 to 6
- norm_gain: float32 [768], replicated, may hold values from 0.5 to 1.5
- gate_proj: bfloat16 [768, 1536], P(None, 'head'), may hold values from -0.21875 to 0.21875
- value_proj: bfloat16 [768, 1536], P(None, 'head'), may hold values from -0.21875 to 0.21875
- state_proj: bfloat16 [768, 256], replicated, may hold values from -0.21875 to 0.21875
- step_proj: bfloat16 [2, 768, 24], P(None, None, 'head'), may hold values from -0.21875 to 0.21875
- conv_value: float32 [4, 1536], P(None, 'head'), may hold values from -3 to 3
- conv_state: float32 [4, 256], replicated, may hold values from -3 to 3
- step_bias: float32 [2, 24], P(None, 'head'), may hold values from -4 to -3
- decay_log: float32 [24], P('head'), may hold values from -12 to 0
- skip_scale: float32 [24], P('head'), may hold values from 0.5 to 2
- gate_gain: float32 [1536], P('head'), may hold values from 0.5 to 1.5
- out_proj: bfloat16 [1536, 768], P('head'), may hold values from -0.15625 to 0.15625
- lengths: int32 [9], replicated, may hold values from 1024 to 4096, as said below
- cotangent: bfloat16 [16384, 768], P('seq'), may hold values from -6 to 6
Outputs:
- block_out: bfloat16 [16384, 768], P('seq')
- grad_hidden: float32 [16384, 768], P('seq')
- grad_norm_gain: float32 [768], replicated
- grad_gate_proj: float32 [768, 1536], P(None, 'head')
- grad_value_proj: float32 [768, 1536], P(None, 'head')
- grad_state_proj: float32 [768, 256], replicated
- grad_step_proj: float32 [2, 768, 24], P(None, None, 'head')
- grad_conv_value: float32 [4, 1536], P(None, 'head')
- grad_conv_state: float32 [4, 256], replicated
- grad_step_bias: float32 [2, 24], P(None, 'head')
- grad_decay_log: float32 [24], P('head')
- grad_skip_scale: float32 [24], P('head')
- grad_gate_gain: float32 [1536], P('head')
- grad_out_proj: float32 [1536, 768], P('head')
Inputs may be any that keep to these rules, and one draw needn't show every extreme that they name: 9 lengths that sum to 16384; exactly one of them is 4096.
All inputs are finite; a program needn't handle non-finite values.
Results may differ from a plain program's by a relative error of at most 0.012.
The roundings to bfloat16 on the way count: a program that leaves them out, or rounds other values in their place, can miss the bound.
Values may be sent and summed in bfloat16 or wider, within the bound.
A program may use at most 320 MiB of HBM per device.

v0:
```python
from functools import partial

import jax
import jax.numpy as jnp
from jax import lax
from jax.sharding import PartitionSpec as P

GROUP = 256


HIGHEST = lax.Precision.HIGHEST
EPSILON = 1e-05


def passed_along(block, axis, distance):
    devices = range(lax.axis_size(axis))
    route = [(i - distance, i) for i in devices if i - distance in devices]
    return lax.ppermute(block, axis, route)


def entering(array, axis, combine, identity, reverse):
    devices, here = (lax.axis_size(axis), lax.axis_index(axis))
    everything = jax.tree.map(
        lambda part, kind: lax.all_gather(part.astype(kind), axis),
        array,
        (jnp.bfloat16, jnp.bfloat16),
    )
    start = jax.tree.map(
        lambda part, zero: jnp.broadcast_to(jnp.asarray(zero, part.dtype), part.shape),
        array,
        identity,
    )

    def turn(k, before):
        at = devices - 1 - k if reverse else k
        reached = at > here if reverse else at < here
        new = combine(
            before, jax.tree.map(lambda part, own: part[at].astype(own.dtype), everything, array)
        )
        return jax.tree.map(lambda a, b: jnp.where(reached, a, b), new, before)

    return lax.fori_loop(0, devices, turn, start)


def prefix(array, axis, join, neutral, backward):
    count = lax.axis_size(axis)
    place = lax.axis_index(axis)
    ahead = count - 1 - place if backward else place
    gathered = jax.tree.map(
        lambda a, kind: lax.all_gather(a.astype(kind), axis),
        array,
        jax.tree.map(lambda a: jnp.bfloat16 if a.dtype == jnp.float32 else a.dtype, array),
    )
    state = jax.tree.map(lambda a, e: jnp.zeros_like(a) + jnp.asarray(e, a.dtype), array, neutral)

    def one(turn, state):
        source = count - 1 - turn if backward else turn
        return join(
            state,
            jax.tree.map(
                lambda a, own: lax.dynamic_index_in_dim(a, source, 0, False).astype(own.dtype),
                gathered,
                array,
            ),
        )

    return lax.fori_loop(0, ahead, one, state)


def round_low(values):
    return lax.optimization_barrier(values.astype(jnp.bfloat16)).astype(jnp.float32)


def silu_grad(values):
    sigmoid = jax.nn.sigmoid(values)
    return sigmoid * (1.0 + values * (1.0 - sigmoid))


def group_step(carry_in, block_data):
    carried, seg_prev = carry_in
    values, step_size, log_decay, entry_map, read_map, segment = block_data
    running = jnp.cumsum(log_decay, axis=0)
    before = running - log_decay
    length = segment.shape[0]
    positions = jnp.arange(length)
    same_seq = (segment[:, None] == segment[None, :]) & (positions[:, None] > positions[None, :])
    chosen = same_seq[:, :, None]
    decay_matrix = jnp.where(
        chosen, jnp.exp(jnp.where(chosen, before[:, None, :] - running[None, :, :], 0.0)), 0.0
    )
    scores = jnp.dot(read_map, entry_map.T, precision=HIGHEST)
    weight = decay_matrix * scores[:, :, None] * step_size[None, :, :]
    inner_y = jnp.einsum("tsh,shp->thp", weight, values, precision=HIGHEST)
    keep_rows = (segment == seg_prev).astype(jnp.float32)
    from_state = jnp.einsum("tn,hpn->thp", read_map, carried, precision=HIGHEST)
    output = inner_y + (keep_rows[:, None] * jnp.exp(before))[:, :, None] * from_state
    last_seg = segment[-1]
    tail_weight = (
        jnp.where((segment == last_seg)[:, None], jnp.exp(running[-1][None, :] - running), 0.0)
        * step_size
    )
    passed = jnp.where(last_seg == seg_prev, jnp.exp(running[-1]), 0.0)
    new_state = passed[:, None, None] * carried + jnp.einsum(
        "sh,shp,sn->hpn", tail_weight, values, entry_map, precision=HIGHEST
    )
    return ((new_state, last_seg), output)


def device_local(values, step_size, decay_log, entry_map, read_map, segment, seg_before):
    length, heads_dev, head_width = values.shape
    log_decay = -jnp.exp(decay_log)[None, :] * step_size
    num_blocks = length // GROUP

    def to_blocks(array):
        return array.reshape((num_blocks, GROUP) + array.shape[1:])

    zero_state = jnp.zeros((heads_dev, head_width, entry_map.shape[1]), jnp.float32)
    carry_out, outputs = lax.scan(
        jax.checkpoint(group_step),
        (zero_state, seg_before),
        (
            to_blocks(values),
            to_blocks(step_size),
            to_blocks(log_decay),
            to_blocks(entry_map),
            to_blocks(read_map),
            to_blocks(segment),
        ),
    )
    passed = jnp.where(segment[-1] == seg_before, jnp.exp(jnp.sum(log_decay, axis=0)), 0.0)
    return (outputs.reshape(length, heads_dev, head_width), carry_out[0], passed)


def carry_term(step_size, decay_log, read_map, incoming, segment, seg_before):
    log_decay = -jnp.exp(decay_log)[None, :] * step_size
    before = jnp.cumsum(log_decay, axis=0) - log_decay
    keep_rows = (segment == seg_before).astype(jnp.float32)
    factor = keep_rows[:, None] * jnp.exp(before)
    return factor[:, :, None] * jnp.einsum("tn,hpn->thp", read_map, incoming, precision=HIGHEST)


def combine_pair(earlier, later):
    return (earlier[0] * later[0], later[0][:, None, None] * earlier[1] + later[1])


def body(
    hidden_in,
    norm_gain,
    gate_proj,
    value_proj,
    state_proj,
    step_proj,
    conv_value,
    conv_state,
    step_bias,
    decay_log,
    skip_scale,
    gate_gain,
    out_proj,
    lengths,
    cotangent,
):
    length = hidden_in.shape[0]
    inner_dev = gate_proj.shape[1]
    heads_dev = decay_log.shape[0]
    head_width = inner_dev // heads_dev
    state_size = state_proj.shape[1] // 4
    inner_all = inner_dev * lax.axis_size("head")
    seq_index = lax.axis_index("seq")
    seq_ends = jnp.cumsum(lengths)
    starts = seq_ends - lengths
    positions = seq_index * length + jnp.arange(length, dtype=jnp.int32)

    def segment_of(places):
        return jnp.sum((places[:, None] >= seq_ends[None, :]).astype(jnp.int32), axis=1)

    segment = segment_of(positions)
    seg_before = segment_of(jnp.reshape(seq_index * length - 1, (1,)))[0]
    seg_after = segment_of(jnp.reshape(seq_index * length + length, (1,)))[0]
    seq_start = jnp.max(
        jnp.where(positions[:, None] >= starts[None, :], starts[None, :], 0), axis=1
    )
    offset = positions - seq_start
    residual = hidden_in.astype(jnp.float32)
    scale_in = lax.rsqrt(jnp.mean(residual * residual, axis=1) + EPSILON)
    normed = (residual * scale_in[:, None] * norm_gain).astype(jnp.bfloat16)
    gate_pre = jnp.dot(normed, gate_proj, preferred_element_type=jnp.float32)
    value_pre = jnp.dot(normed, value_proj, preferred_element_type=jnp.float32).astype(jnp.bfloat16)
    state_pre = jnp.dot(normed, state_proj, preferred_element_type=jnp.float32).astype(jnp.bfloat16)
    step_pre = jnp.einsum("td,kdh->tkh", normed, step_proj, preferred_element_type=jnp.float32)
    conv_in = jnp.concatenate([value_pre, state_pre], axis=1)
    before_rows = passed_along(conv_in[length - 3 :], "seq", 1)
    extended = jnp.concatenate([before_rows, conv_in], axis=0).astype(jnp.float32)
    conv_weight = jnp.concatenate([conv_value, conv_state], axis=1)

    def convolve(padded_rows, tap_weights):
        conv_total = jnp.zeros((length, padded_rows.shape[1]), jnp.float32)
        for shift_tap in range(4):
            valid_rows = (offset >= 3 - shift_tap).astype(jnp.float32)
            conv_total = (
                conv_total
                + padded_rows[shift_tap : shift_tap + length]
                * tap_weights[shift_tap]
                * valid_rows[:, None]
            )
        return jax.nn.silu(conv_total)

    activated, conv_back = jax.vjp(convolve, extended, conv_weight)
    rounded = round_low(activated)
    values = rounded[:, :inner_dev].reshape(length, heads_dev, head_width)
    state_maps = rounded[:, inner_dev:]
    entry_fwd = state_maps[:, :state_size]
    read_fwd = state_maps[:, state_size : 2 * state_size]
    entry_rev = state_maps[:, 2 * state_size : 3 * state_size]
    read_rev = state_maps[:, 3 * state_size :]
    step_size = jax.nn.softplus(step_pre + step_bias[None])
    rev_segment = segment[::-1]
    local_fwd_fn = partial(device_local, segment=segment, seg_before=seg_before)
    local_rev_fn = partial(device_local, segment=rev_segment, seg_before=seg_after)
    (local_fwd, summary_fwd, passed_fwd), back_local_fwd = jax.vjp(
        local_fwd_fn, values, step_size[:, 0], decay_log, entry_fwd, read_fwd
    )
    (local_rev, summary_rev, passed_rev), back_local_rev = jax.vjp(
        local_rev_fn, values[::-1], step_size[::-1, 1], decay_log, entry_rev[::-1], read_rev[::-1]
    )
    identity_pair = (jnp.ones_like(passed_fwd), jnp.zeros_like(summary_fwd))
    incoming_fwd = entering((passed_fwd, summary_fwd), "seq", combine_pair, identity_pair, False)[1]
    incoming_rev = entering((passed_rev, summary_rev), "seq", combine_pair, identity_pair, True)[1]
    carry_fwd_fn = partial(carry_term, segment=segment, seg_before=seg_before)
    carry_rev_fn = partial(carry_term, segment=rev_segment, seg_before=seg_after)
    extra_fwd, back_carry_fwd = jax.vjp(
        carry_fwd_fn, step_size[:, 0], decay_log, read_fwd, incoming_fwd
    )
    extra_rev, back_carry_rev = jax.vjp(
        carry_rev_fn, step_size[::-1, 1], decay_log, read_rev[::-1], incoming_rev
    )
    mixed_heads = (
        local_fwd + extra_fwd + (local_rev + extra_rev)[::-1] + skip_scale[None, :, None] * values
    )
    mixed_flat = mixed_heads.reshape(length, inner_dev)
    gate_act = jax.nn.silu(gate_pre)
    gated = mixed_flat * gate_act
    square_sum = lax.psum(jnp.sum(gated * gated, axis=1), "head")
    scale_gate = lax.rsqrt(square_sum / inner_all + EPSILON)
    normed_gate = (gated * scale_gate[:, None] * gate_gain).astype(jnp.bfloat16)
    branch_part = jnp.dot(normed_gate, out_proj, preferred_element_type=jnp.float32)
    branch = lax.psum(branch_part.astype(jnp.bfloat16), "head").astype(jnp.float32)
    block_out = (residual + branch).astype(jnp.bfloat16)
    out_proj_grad = jnp.einsum(
        "ti,td->id", normed_gate, cotangent, preferred_element_type=jnp.float32
    )
    grad_normed_gate = jnp.einsum(
        "td,id->ti", cotangent, out_proj, preferred_element_type=jnp.float32
    )
    gate_gain_grad = jnp.sum(grad_normed_gate * gated * scale_gate[:, None], axis=0)
    grad_hat = grad_normed_gate * gate_gain
    cross_sum = lax.psum(jnp.sum(gated * grad_hat, axis=1), "head")
    grad_gated = (
        scale_gate[:, None] * grad_hat - gated * (scale_gate**3 * cross_sum / inner_all)[:, None]
    )
    grad_mixed = (grad_gated * gate_act).reshape(length, heads_dev, head_width)
    grad_gate = (grad_gated * mixed_flat * silu_grad(gate_pre)).astype(jnp.bfloat16)
    skip_grad = jnp.sum(grad_mixed * values, axis=(0, 2))
    grad_rev_out = grad_mixed[::-1]
    carry_step_fwd, carry_decay_fwd, carry_read_fwd, grad_in_fwd = back_carry_fwd(grad_mixed)
    carry_step_rev, carry_decay_rev, carry_read_rev, grad_in_rev = back_carry_rev(grad_rev_out)
    later_fwd = prefix((passed_fwd, grad_in_fwd), "seq", combine_pair, identity_pair, True)[1]
    later_rev = prefix((passed_rev, grad_in_rev), "seq", combine_pair, identity_pair, False)[1]
    passed_grad_fwd = jnp.sum(later_fwd * incoming_fwd, axis=(1, 2))
    passed_grad_rev = jnp.sum(later_rev * incoming_rev, axis=(1, 2))
    local_values_fwd, local_step_fwd, local_decay_fwd, local_entry_fwd, local_read_fwd = (
        back_local_fwd((grad_mixed, later_fwd, passed_grad_fwd))
    )
    local_values_rev, local_step_rev, local_decay_rev, local_entry_rev, local_read_rev = (
        back_local_rev((grad_rev_out, later_rev, passed_grad_rev))
    )
    grad_values = grad_mixed * skip_scale[None, :, None] + local_values_fwd + local_values_rev[::-1]
    grad_step = jnp.stack(
        [carry_step_fwd + local_step_fwd, (carry_step_rev + local_step_rev)[::-1]], axis=1
    )
    decay_grad = carry_decay_fwd + local_decay_fwd + carry_decay_rev + local_decay_rev
    grad_maps = jnp.concatenate(
        [
            grad_values.reshape(length, inner_dev),
            local_entry_fwd,
            carry_read_fwd + local_read_fwd,
            local_entry_rev[::-1],
            (carry_read_rev + local_read_rev)[::-1],
        ],
        axis=1,
    )
    grad_extended, conv_grad = conv_back(grad_maps)
    from_next = passed_along(grad_extended[:3], "seq", -1)
    grad_conv_in = grad_extended[3:].at[length - 3 :].add(from_next)
    grad_value = grad_conv_in[:, :inner_dev].astype(jnp.bfloat16)
    grad_state_part = grad_conv_in[:, inner_dev:]
    step_slope = jax.nn.sigmoid(step_pre + step_bias[None])
    grad_step_raw = grad_step * step_slope
    bias_grad = jnp.sum(grad_step_raw, axis=0)
    grad_step_low = grad_step_raw.astype(jnp.bfloat16)
    grad_normed_part = jnp.einsum(
        "ti,di->td", grad_gate, gate_proj, preferred_element_type=jnp.float32
    )
    grad_normed_part = grad_normed_part + jnp.einsum(
        "ti,di->td", grad_value, value_proj, preferred_element_type=jnp.float32
    )
    grad_normed_part = grad_normed_part + jnp.einsum(
        "tkh,kdh->td", grad_step_low, step_proj, preferred_element_type=jnp.float32
    )
    grad_normed_heads, grad_state_sum, conv_state_grad = lax.psum(
        (grad_normed_part, grad_state_part, conv_grad[:, inner_dev:]), "head"
    )
    grad_state = grad_state_sum.astype(jnp.bfloat16)
    grad_normed = grad_normed_heads + jnp.einsum(
        "tc,dc->td", grad_state, state_proj, preferred_element_type=jnp.float32
    )
    state_proj_grad = jnp.einsum(
        "td,tc->dc", normed, grad_state, preferred_element_type=jnp.float32
    )
    gate_proj_grad = jnp.einsum("td,ti->di", normed, grad_gate, preferred_element_type=jnp.float32)
    value_proj_grad = jnp.einsum(
        "td,ti->di", normed, grad_value, preferred_element_type=jnp.float32
    )
    step_proj_grad = jnp.einsum(
        "td,tkh->kdh", normed, grad_step_low, preferred_element_type=jnp.float32
    )
    scaled = grad_normed * norm_gain
    norm_gain_grad = jnp.sum(grad_normed * residual * scale_in[:, None], axis=0)
    grad_hidden = (
        cotangent.astype(jnp.float32)
        + scale_in[:, None] * scaled
        - residual * (scale_in**3 * jnp.mean(residual * scaled, axis=1))[:, None]
    )
    summed = lax.psum(
        (
            norm_gain_grad,
            gate_proj_grad,
            value_proj_grad,
            state_proj_grad,
            step_proj_grad,
            conv_grad[:, :inner_dev],
            conv_state_grad,
            bias_grad,
            decay_grad,
            skip_grad,
            gate_gain_grad,
            out_proj_grad,
        ),
        "seq",
    )
    return (
        block_out,
        grad_hidden,
        summed[0],
        summed[1],
        summed[2],
        summed[3],
        summed[4],
        summed[5],
        summed[6],
        summed[7],
        summed[8],
        summed[9],
        summed[10],
        summed[11],
    )


def solution(mesh):
    in_specs = (
        P("seq", None),
        P(),
        P(None, "head"),
        P(None, "head"),
        P(),
        P(None, None, "head"),
        P(None, "head"),
        P(),
        P(None, "head"),
        P("head"),
        P("head"),
        P("head"),
        P("head", None),
        P(),
        P("seq", None),
    )
    out_specs = (
        P("seq", None),
        P("seq", None),
        P(),
        P(None, "head"),
        P(None, "head"),
        P(),
        P(None, None, "head"),
        P(None, "head"),
        P(),
        P(None, "head"),
        P("head"),
        P("head"),
        P("head"),
        P("head", None),
    )
    return jax.shard_map(body, mesh=mesh, in_specs=in_specs, out_specs=out_specs, check_vma=False)
```

profile of v0, /device:TPU:0, one launch (start us, length us, event | category | flops | bytes accessed | tf_op | source)
XLA Modules:
  0.0 1731.8 jit_solution(14023587805171006555)
XLA Ops:
  15.8 5.5 collective-permute-start
  58.2 40.2 %all-reduce.17 = (bf16[192]{0:T(256)(128)(2,1)}, bf16[192]{0:T(256)(128)(2,1)S(1)}) all-reduce(bf16[192]{0:T(256)(128)(2,1)} %copy-done.144, bf16[192]{0:T(256)(128)(2,1)} %dynamic-update-slice.3), channel_id=4, replica_groups=mesh['seq'=16,'head'=2] {'seq'}, use_global_device_ids=true, to_apply=%add.13 | all-reduce | flops 384 | bytes 1536
  104.2 5.8 multiply_convert_fusion
  118.3 6.7 rev.37
  135.4 148.9 %while.153 = (s32[]{:T(128)}, f32[12,64,64]{2,1,0:T(8,128)S(1)}, s32[]{:T(128)}, f32[4,256,12,64]{1,0,3,2:T(4,128)}, f32[4,12,64,64]{3,2,1,0:T(8,128)}, /*index=...) while((s32[]{:T(128)}, f32[12,64,64]{2,1,0:T(8,128)S(1)}, ...), condition=%wide.region_18.19_spmd.clone, body=%wide.region_15.18_spmd.clone.sunk | while | flops 961675072 | bytes 9541886 | solution.py:118
  153.4 17.9 %dynamic_update_slice.169 = f32[4,256,12,64]{1,0,3,2:T(4,128)} dynamic-update-slice(f32[4,256,12,64]{1,0,3,2:T(4,128)} %get-tuple-element.2798, f32[1,256,12,64]{1,0,3,2:T(1,128)S(1)} %copy.563, s32[]{:T(128)S(6)} %copy.587, s32[]{:T(128)} %constant.378.clone.1..sunk.6, s32[]{:T(128)} %constant.378.clone.1..sunk.6, s32[]{:T(128)} %constant.378.clone.1..sunk.6) | dynamic-update-slice | bytes 1572868 | tf_op jit(solution)/shard_map/jvp()/while/body/jit(dynamic_update_index_in_dim)/dynamic_update_slice | solution.py:118
  190.7 17.9 %dynamic_update_slice.169 = f32[4,256,12,64]{1,0,3,2:T(4,128)} dynamic-update-slice(f32[4,256,12,64]{1,0,3,2:T(4,128)} %get-tuple-element.2798, f32[1,256,12,64]{1,0,3,2:T(1,128)S(1)} %copy.563, s32[]{:T(128)S(6)} %copy.587, s32[]{:T(128)} %constant.378.clone.1..sunk.6, s32[]{:T(128)} %constant.378.clone.1..sunk.6, s32[]{:T(128)} %constant.378.clone.1..sunk.6) | dynamic-update-slice | bytes 1572868 | tf_op jit(solution)/shard_map/jvp()/while/body/jit(dynamic_update_index_in_dim)/dynamic_update_slice | solution.py:118
  227.9 17.9 %dynamic_update_slice.169 = f32[4,256,12,64]{1,0,3,2:T(4,128)} dynamic-update-slice(f32[4,256,12,64]{1,0,3,2:T(4,128)} %get-tuple-element.2798, f32[1,256,12,64]{1,0,3,2:T(1,128)S(1)} %copy.563, s32[]{:T(128)S(6)} %copy.587, s32[]{:T(128)} %constant.378.clone.1..sunk.6, s32[]{:T(128)} %constant.378.clone.1..sunk.6, s32[]{:T(128)} %constant.378.clone.1..sunk.6) | dynamic-update-slice | bytes 1572868 | tf_op jit(solution)/shard_map/jvp()/while/body/jit(dynamic_update_index_in_dim)/dynamic_update_slice | solution.py:118
  265.1 17.9 %dynamic_update_slice.169 = f32[4,256,12,64]{1,0,3,2:T(4,128)} dynamic-update-slice(f32[4,256,12,64]{1,0,3,2:T(4,128)} %get-tuple-element.2798, f32[1,256,12,64]{1,0,3,2:T(1,128)S(1)} %copy.563, s32[]{:T(128)S(6)} %copy.587, s32[]{:T(128)} %constant.378.clone.1..sunk.6, s32[]{:T(128)} %constant.378.clone.1..sunk.6, s32[]{:T(128)} %constant.378.clone.1..sunk.6) | dynamic-update-slice | bytes 1572868 | tf_op jit(solution)/shard_map/jvp()/while/body/jit(dynamic_update_index_in_dim)/dynamic_update_slice | solution.py:118
  294.8 149.2 %while.151 = (s32[]{:T(128)}, f32[12,64,64]{2,1,0:T(8,128)S(1)}, s32[]{:T(128)}, f32[4,256,12,64]{1,0,3,2:T(4,128)}, f32[4,12,64,64]{3,2,1,0:T(8,128)}, /*index=...) while((s32[]{:T(128)}, f32[12,64,64]{2,1,0:T(8,128)S(1)}, ...), condition=%wide.region_8.9_spmd.clone, body=%wide.region_5.8_spmd.clone.sunk | while | flops 961675072 | bytes 9541886 | solution.py:118
  313.0 17.9 %dynamic_update_slice.166 = f32[4,256,12,64]{1,0,3,2:T(4,128)} dynamic-update-slice(f32[4,256,12,64]{1,0,3,2:T(4,128)} %get-tuple-element.2873, f32[1,256,12,64]{1,0,3,2:T(1,128)S(1)} %copy.559, s32[]{:T(128)S(6)} %copy.613, s32[]{:T(128)} %constant.378.clone.1..sunk.4, s32[]{:T(128)} %constant.378.clone.1..sunk.4, s32[]{:T(128)} %constant.378.clone.1..sunk.4) | dynamic-update-slice | bytes 1572868 | tf_op jit(solution)/shard_map/jvp()/while/body/jit(dynamic_update_index_in_dim)/dynamic_update_slice | solution.py:118
  350.3 17.9 %dynamic_update_slice.166 = f32[4,256,12,64]{1,0,3,2:T(4,128)} dynamic-update-slice(f32[4,256,12,64]{1,0,3,2:T(4,128)} %get-tuple-element.2873, f32[1,256,12,64]{1,0,3,2:T(1,128)S(1)} %copy.559, s32[]{:T(128)S(6)} %copy.613, s32[]{:T(128)} %constant.378.clone.1..sunk.4, s32[]{:T(128)} %constant.378.clone.1..sunk.4, s32[]{:T(128)} %constant.378.clone.1..sunk.4) | dynamic-update-slice | bytes 1572868 | tf_op jit(solution)/shard_map/jvp()/while/body/jit(dynamic_update_index_in_dim)/dynamic_update_slice | solution.py:118
  387.6 17.9 %dynamic_update_slice.166 = f32[4,256,12,64]{1,0,3,2:T(4,128)} dynamic-update-slice(f32[4,256,12,64]{1,0,3,2:T(4,128)} %get-tuple-element.2873, f32[1,256,12,64]{1,0,3,2:T(1,128)S(1)} %copy.559, s32[]{:T(128)S(6)} %copy.613, s32[]{:T(128)} %constant.378.clone.1..sunk.4, s32[]{:T(128)} %constant.378.clone.1..sunk.4, s32[]{:T(128)} %constant.378.clone.1..sunk.4) | dynamic-update-slice | bytes 1572868 | tf_op jit(solution)/shard_map/jvp()/while/body/jit(dynamic_update_index_in_dim)/dynamic_update_slice | solution.py:118
  424.9 17.9 %dynamic_update_slice.166 = f32[4,256,12,64]{1,0,3,2:T(4,128)} dynamic-update-slice(f32[4,256,12,64]{1,0,3,2:T(4,128)} %get-tuple-element.2873, f32[1,256,12,64]{1,0,3,2:T(1,128)S(1)} %copy.559, s32[]{:T(128)S(6)} %copy.613, s32[]{:T(128)} %constant.378.clone.1..sunk.4, s32[]{:T(128)} %constant.378.clone.1..sunk.4, s32[]{:T(128)} %constant.378.clone.1..sunk.4) | dynamic-update-slice | bytes 1572868 | tf_op jit(solution)/shard_map/jvp()/while/body/jit(dynamic_update_index_in_dim)/dynamic_update_slice | solution.py:118
  448.0 5.2 reshape.947
  453.3 5.4 reshape.939
  459.6 28.2 %while.154 = (s32[]{:T(128)}, f32[12,64,64]{2,1,0:T(8,128)S(1)}, s32[]{:T(128)}, bf16[16,12]{1,0:T(8,128)(2,1)}, bf16[16,12,64,64]{3,2,1,0:T(8,128)(2,1)}, /*index=5*/s32[]{:T(128)}, s32[]{:T(128)}, s32[]{:T(128)}, s32[]{:T(128)}) while((s32[]{:T(128)}, f32[12,64,64]{2,1,0:T(8,128)S(1)}, s32[]{:T(128)}, ...), condition=%wide.region_23.24_spmd.clone, body=%wide.region_22.23_spmd.clone.sunk | while | flops 245780 | bytes 491815 | solution.py:42
  487.9 6.0 multiply_add_fusion.4
  493.9 6.8 rev.40
  500.6 23.0 %all-gather.11.cloned.1.call-done = bf16[192,64,64]{2,1,0:T(8,128)(2,1)} async-done(((bf16[12,64,64]{2,1,0:T(8,128)(2,1)}), bf16[192,64,64]{2,1,0:T(8,128)(2,1)}) %all-gather.11.cloned.1.call-update) | async-done | bytes 1572880 | tf_op jit(solution)/shard_map/all_gather | solution.py:24
  523.6 28.0 %while.152 = (s32[]{:T(128)}, f32[12,64,64]{2,1,0:T(8,128)S(1)}, s32[]{:T(128)}, bf16[16,12]{1,0:T(8,128)(2,1)}, bf16[16,12,64,64]{3,2,1,0:T(8,128)(2,1)}, /*index=5*/s32[]{:T(128)}, s32[]{:T(128)}) while((s32[]{:T(128)}, f32[12,64,64]{2,1,0:T(8,128)S(1)}, s32[]{:T(128)}, bf16[16,12]{1,0:T(8,128)(2,1)}, ...), condition=%wide.region_13.14_spmd.clone, body=%wide.region_12.13_spmd.clone.sunk | while | flops 245776 | bytes 491753 | solution.py:42
  551.7 7.4 multiply_add_fusion.3
  566.2 6.6 multiply_reduce_fusion.10
  575.3 8.9 multiply_reduce_fusion.11
  584.2 6.8 rev.41
  591.0 5.2 fusion.210
  600.7 5.2 reshape.953
  616.1 16.1 reduce-window.168
  637.9 25.0 %all-gather.17.cloned.1.call-done = bf16[192,64,64]{2,1,0:T(8,128)(2,1)} async-done(((bf16[12,64,64]{2,1,0:T(8,128)(2,1)}), bf16[192,64,64]{2,1,0:T(8,128)(2,1)}) %all-gather.17.cloned.1.call-update) | async-done | bytes 1572880 | tf_op jit(solution)/shard_map/all_gather | solution.py:50
  663.7 68.5 %all-gather.15.cloned.1.call-done = bf16[192,64,64]{2,1,0:T(8,128)(2,1)} async-done(((bf16[12,64,64]{2,1,0:T(8,128)(2,1)}), bf16[192,64,64]{2,1,0:T(8,128)(2,1)}) %all-gather.15.cloned.1.call-update) | async-done | bytes 1572880 | tf_op jit(solution)/shard_map/all_gather | solution.py:50
  732.3 26.5 %while.147 = (s32[]{:T(128)}, f32[12,64,64]{2,1,0:T(8,128)S(1)}, s32[]{:T(128)}, bf16[16,12]{1,0:T(8,128)(2,1)}, bf16[16,12,64,64]{3,2,1,0:T(8,128)(2,1)}, /*index=5*/s32[]{:T(128)}, s32[]{:T(128)}, s32[]{:T(128)}, s32[]{:T(128)}) while((s32[]{:T(128)}, f32[12,64,64]{2,1,0:T(8,128)S(1)}, s32[]{:T(128)}, bf16[16,12]{1,0:T(8,128)(2,1)}, ...), condition=%wide.region_30.31_spmd, body=%wide.region_29.30_spmd.sunk | while | flops 147474 | bytes 491795 | solution.py:67
  764.6 285.3 %while.150 = (s32[]{:T(128)}, f32[12,64,64]{2,1,0:T(8,128)S(1)}, f32[4,256,12,64]{1,0,3,2:T(4,128)}, f32[4,256,12]{1,0,2:T(4,128)}, f32[4,256,12]{1,0,2:T(4,128)...) while((s32[]{:T(128)}, f32[12,64,64]{2,1,0:T(8,128)S(1)}, ...), condition=%wide.region_58.59_spmd, body=%wide.region_46.58_spmd.sunk | while | flops 2132627200 | bytes 24680752 | solution.py:118
  779.3 6.5 fusion.470
  802.5 17.9 %dynamic_update_slice.160 = f32[4,256,12,64]{1,0,3,2:T(4,128)} dynamic-update-slice(f32[4,256,12,64]{1,0,3,2:T(4,128)} %get-tuple-element.2969, f32[1,256,12,64]{1,0,3,2:T(1,128)S(1)} %copy.547, s32[]{:T(128)S(6)} %sub.574, s32[]{:T(128)} %constant.378.clone.1..sunk.3, s32[]{:T(128)} %constant.378.clone.1..sunk.3, s32[]{:T(128)} %constant.378.clone.1..sunk.3) | dynamic-update-slice | bytes 1572868 | tf_op jit(solution)/shard_map/transpose(jvp())/while/body/jit(dynamic_update_index_in_dim)/dynamic_update_slice | solution.py:118
  850.5 6.5 fusion.470
  873.7 17.9 %dynamic_update_slice.160 = f32[4,256,12,64]{1,0,3,2:T(4,128)} dynamic-update-slice(f32[4,256,12,64]{1,0,3,2:T(4,128)} %get-tuple-element.2969, f32[1,256,12,64]{1,0,3,2:T(1,128)S(1)} %copy.547, s32[]{:T(128)S(6)} %sub.574, s32[]{:T(128)} %constant.378.clone.1..sunk.3, s32[]{:T(128)} %constant.378.clone.1..sunk.3, s32[]{:T(128)} %constant.378.clone.1..sunk.3) | dynamic-update-slice | bytes 1572868 | tf_op jit(solution)/shard_map/transpose(jvp())/while/body/jit(dynamic_update_index_in_dim)/dynamic_update_slice | solution.py:118
  921.7 6.5 fusion.470
  944.9 17.9 %dynamic_update_slice.160 = f32[4,256,12,64]{1,0,3,2:T(4,128)} dynamic-update-slice(f32[4,256,12,64]{1,0,3,2:T(4,128)} %get-tuple-element.2969, f32[1,256,12,64]{1,0,3,2:T(1,128)S(1)} %copy.547, s32[]{:T(128)S(6)} %sub.574, s32[]{:T(128)} %constant.378.clone.1..sunk.3, s32[]{:T(128)} %constant.378.clone.1..sunk.3, s32[]{:T(128)} %constant.378.clone.1..sunk.3) | dynamic-update-slice | bytes 1572868 | tf_op jit(solution)/shard_map/transpose(jvp())/while/body/jit(dynamic_update_index_in_dim)/dynamic_update_slice | solution.py:118
  992.9 6.5 fusion.470
  1016.1 17.9 %dynamic_update_slice.160 = f32[4,256,12,64]{1,0,3,2:T(4,128)} dynamic-update-slice(f32[4,256,12,64]{1,0,3,2:T(4,128)} %get-tuple-element.2969, f32[1,256,12,64]{1,0,3,2:T(1,128)S(1)} %copy.547, s32[]{:T(128)S(6)} %sub.574, s32[]{:T(128)} %constant.378.clone.1..sunk.3, s32[]{:T(128)} %constant.378.clone.1..sunk.3, s32[]{:T(128)} %constant.378.clone.1..sunk.3) | dynamic-update-slice | bytes 1572868 | tf_op jit(solution)/shard_map/transpose(jvp())/while/body/jit(dynamic_update_index_in_dim)/dynamic_update_slice | solution.py:118
  1049.8 5.2 reshape.954
  1055.0 6.7 rev.42
  1066.8 243.1 %while.148 = (s32[]{:T(128)}, f32[12,64,64]{2,1,0:T(8,128)S(1)}, f32[4,256,12,64]{1,0,3,2:T(4,128)}, f32[4,256,12]{1,0,2:T(4,128)}, f32[4,256,12]{1,0,2:T(4,128)...) while((s32[]{:T(128)}, f32[12,64,64]{2,1,0:T(8,128)S(1)}, ...), condition=%wide.region_43.44_spmd, body=%wide.region_31.43_spmd.sunk | while | flops 2132627200 | bytes 23982024 | solution.py:118
  1080.0 5.5 fusion.440
  1096.8 17.9 %dynamic_update_slice.155 = f32[4,256,12,64]{1,0,3,2:T(4,128)} dynamic-update-slice(f32[4,256,12,64]{1,0,3,2:T(4,128)} %get-tuple-element.3056, f32[1,256,12,64]{1,0,3,2:T(1,128)S(1)} %copy.533, s32[]{:T(128)S(6)} %sub.567, s32[]{:T(128)} %constant.378.clone.1..sunk.1, s32[]{:T(128)} %constant.378.clone.1..sunk.1, s32[]{:T(128)} %constant.378.clone.1..sunk.1) | dynamic-update-slice | bytes 1572868 | tf_op jit(solution)/shard_map/transpose(jvp())/while/body/jit(dynamic_update_index_in_dim)/dynamic_update_slice | solution.py:118
  1140.7 5.5 fusion.440
  1157.5 17.9 %dynamic_update_slice.155 = f32[4,256,12,64]{1,0,3,2:T(4,128)} dynamic-update-slice(f32[4,256,12,64]{1,0,3,2:T(4,128)} %get-tuple-element.3056, f32[1,256,12,64]{1,0,3,2:T(1,128)S(1)} %copy.533, s32[]{:T(128)S(6)} %sub.567, s32[]{:T(128)} %constant.378.clone.1..sunk.1, s32[]{:T(128)} %constant.378.clone.1..sunk.1, s32[]{:T(128)} %constant.378.clone.1..sunk.1) | dynamic-update-slice | bytes 1572868 | tf_op jit(solution)/shard_map/transpose(jvp())/while/body/jit(dynamic_update_index_in_dim)/dynamic_update_slice | solution.py:118
  1201.4 5.5 fusion.440
  1218.2 17.9 %dynamic_update_slice.155 = f32[4,256,12,64]{1,0,3,2:T(4,128)} dynamic-update-slice(f32[4,256,12,64]{1,0,3,2:T(4,128)} %get-tuple-element.3056, f32[1,256,12,64]{1,0,3,2:T(1,128)S(1)} %copy.533, s32[]{:T(128)S(6)} %sub.567, s32[]{:T(128)} %constant.378.clone.1..sunk.1, s32[]{:T(128)} %constant.378.clone.1..sunk.1, s32[]{:T(128)} %constant.378.clone.1..sunk.1) | dynamic-update-slice | bytes 1572868 | tf_op jit(solution)/shard_map/transpose(jvp())/while/body/jit(dynamic_update_index_in_dim)/dynamic_update_slice | solution.py:118
  1262.1 5.5 fusion.440
  1278.9 17.9 %dynamic_update_slice.155 = f32[4,256,12,64]{1,0,3,2:T(4,128)} dynamic-update-slice(f32[4,256,12,64]{1,0,3,2:T(4,128)} %get-tuple-element.3056, f32[1,256,12,64]{1,0,3,2:T(1,128)S(1)} %copy.533, s32[]{:T(128)S(6)} %sub.567, s32[]{:T(128)} %constant.378.clone.1..sunk.1, s32[]{:T(128)} %constant.378.clone.1..sunk.1, s32[]{:T(128)} %constant.378.clone.1..sunk.1) | dynamic-update-slice | bytes 1572868 | tf_op jit(solution)/shard_map/transpose(jvp())/while/body/jit(dynamic_update_index_in_dim)/dynamic_update_slice | solution.py:118
  1309.9 5.2 reshape.952
  1315.1 6.3 add_add_fusion
  1330.1 5.3 fusion.225
  1336.9 12.0 multiply_reduce_fusion.9
  1353.3 12.5 pad_add_fusion
  1368.8 14.9 reduce-window.166
  1388.4 5.6 slice.358
  1403.8 6.9 bitcast_add_fusion.2
  1419.9 5.2 fusion.264
  1427.9 6.3 all-reduce.28
  1446.8 75.0 %all-reduce.14 = (f32[768]{0:T(1024)}, f32[4,768]{1,0:T(4,128)}, f32[4,256]{1,0:T(4,128)}, f32[2,12]{1,0:T(2,128)}, f32[12]{0:T(128)}, /*index=5*/f32[12]{0:T(128)}, f32[768]{0:T(1024)}) all-reduce(f32[768]{0:T(1024)S(1)} %get-tuple-element.1856, f32[4,768]{1,0:T(4,128)S(1)} %slice.365, ...), channel_id=1, replica_groups=mesh['seq'=16,'head'=2] {'seq'}, use_global_device_ids=true, to_apply=%region_71.72 | all-reduce | flops 5680 | bytes 45440 | tf_op jit(solution)/shard_map/psum | solution.py:334
  1521.8 6.2 fusion.185
  1528.0 187.4 %all-reduce.27.cloned.1.call-done = (f32[768,768]{1,0:T(8,128)}, f32[768,768]{1,0:T(8,128)}, f32[768,256]{1,0:T(8,128)}, f32[2,768,12]{1,2,0:T(8,128)}, f32[768,768]{1,0:T(8,128)}) async-done(((f32[768,768]{1,0:T(8,128)}, f32[768,768]{1,0:T(8,128)}, f32[768,256]{1,0:T(8,128)}, f32[2,768,12]{1,2,0:T(8,128)}, f32[768,768]{1,0:T(8,128)}), (f32[768,768]{1,0:T(8,128)}, f32[768,768]{1,0:T(8,128)}, ...) | async-done | bytes 7938064 | tf_op jit(solution)/shard_map/psum | solution.py:334
  (1415 shorter events, 738.9 us)
Async XLA Ops:
  7.2 552.0 %copy-start = (bf16[768,768]{1,0:T(8,128)(2,1)S(1)}, bf16[768,768]{1,0:T(8,128)(2,1)}, u32[]{:S(2)}) copy-start(bf16[768,768]{1,0:T(8,128)(2,1)} %param.35) | copy-start | bytes 3538948
  7.2 452.4 %all-gather.13.cloned.1.call-start = ((), (), s32[]{:S(2)}) async-start(), calls=%async_computation.3 | async-start | bytes 3342336 | tf_op jit(solution)/shard_map/all_gather | solution.py:24
  15.8 86.1 %collective-permute-start = (bf16[3,1024]{0,1:T(8,128)(2,1)}, bf16[3,1024]{0,1:T(8,128)(2,1)}, u32[]{:S(2)}, u32[]{:S(2)}) collective-permute-start(bf16[3,1024]{0,1:T(8,128)(2,1)} %pad_maximum_fusion), channel_id=1, source_target_pairs={{0,2},{2,4},{4,6},{6,8},{8,10},{10,12},{12,14},{14,16},{16,18},{18... | collective-permute-start | bytes 18440 | tf_op jit(solution)/shard_map/ppermute | solution.py:18
  24.8 77.1 %copy-start.20 = (bf16[1024,768]{0,1:T(8,128)(2,1)S(1)}, bf16[1024,768]{0,1:T(8,128)(2,1)}, u32[]{:S(2)}) copy-start(bf16[1024,768]{0,1:T(8,128)(2,1)} %copy-done.19) | copy-start | bytes 4718596
  26.0 24.0 %copy-start.62 = (f32[1024,1,12]{0,2,1:T(8,128)}, f32[1024,1,12]{0,2,1:T(8,128)S(1)}, u32[]{:S(2)}) copy-start(f32[1024,1,12]{0,2,1:T(8,128)S(1)} %rev.36) | copy-start | bytes 147460
  27.3 76.8 %copy-start.93 = (f32[1024]{0:T(1024)}, f32[1024]{0:T(1024)S(1)}, u32[]{:S(2)}) copy-start(f32[1024]{0:T(1024)S(1)} %get-tuple-element.2126) | copy-start | bytes 12292
  27.3 76.8 %copy-start.95 = (f32[1024]{0:T(1024)}, f32[1024]{0:T(1024)S(1)}, u32[]{:S(2)}) copy-start(f32[1024]{0:T(1024)S(1)} %get-tuple-element.2127) | copy-start | bytes 12292
  27.3 76.8 %copy-start.97 = (f32[1024]{0:T(1024)}, f32[1024]{0:T(1024)S(1)}, u32[]{:S(2)}) copy-start(f32[1024]{0:T(1024)S(1)} %get-tuple-element.2128) | copy-start | bytes 12292
  29.4 20.7 %copy-start.76 = (f32[4,256,12]{1,0,2:T(4,128)}, f32[4,256,12]{1,0,2:T(4,128)S(1)}, u32[]{:S(2)}) copy-start(f32[4,256,12]{1,0,2:T(4,128)S(1)} %reshape_squeeze.6) | copy-start | bytes 147460
  31.2 18.9 %copy-start.58 = (f32[1024,12]{0,1:T(8,128)}, f32[1024,12]{0,1:T(8,128)S(1)}, u32[]{:S(2)}) copy-start(f32[1024,12]{0,1:T(8,128)S(1)} %get-tuple-element.2062) | copy-start | bytes 147460
  31.2 18.9 %copy-start.60 = (f32[1024,12]{0,1:T(8,128)}, f32[1024,12]{0,1:T(8,128)S(1)}, u32[]{:S(2)}) copy-start(f32[1024,12]{0,1:T(8,128)S(1)} %get-tuple-element.2133) | copy-start | bytes 147460
  285.1 238.5 %all-gather.11.cloned.1.call-start = ((), (), s32[]{:S(2)}) async-start(), calls=%async_computation.2 | async-start | bytes 3342336 | tf_op jit(solution)/shard_map/all_gather | solution.py:24
  458.6 29.2 %copy-start.22 = (f32[1024,64]{0,1:T(8,128)S(1)}, f32[1024,64]{0,1:T(8,128)}, u32[]{:S(2)}) copy-start(f32[1024,64]{0,1:T(8,128)} %copy-done.21) | copy-start | bytes 786436
  458.6 29.3 %copy-start.51 = (f32[1024,12]{0,1:T(8,128)S(1)}, f32[1024,12]{0,1:T(8,128)}, u32[]{:S(2)}) copy-start(f32[1024,12]{0,1:T(8,128)} %broadcast_multiply_fusion) | copy-start | bytes 147460
  459.4 203.6 %all-gather.17.cloned.1.call-start = ((), (), s32[]{:S(2)}) async-start(), calls=%async_computation.5 | async-start | bytes 3342336 | tf_op jit(solution)/shard_map/all_gather | solution.py:50
  493.9 29.8 %copy-start.10 = (f32[12,64,64]{2,1,0:T(8,128)S(1)}, f32[12,64,64]{2,1,0:T(8,128)}, u32[]{:S(2)}) copy-start(f32[12,64,64]{2,1,0:T(8,128)} %custom-call.1) | copy-start | bytes 589828
  500.6 51.0 %copy-start.135 = (f32[12]{0:T(128)S(1)}, f32[12]{0:T(128)}, u32[]{:S(2)}) copy-start(f32[12]{0:T(128)} %param.43) | copy-start | bytes 148
  551.6 207.2 %copy-start.11 = (f32[12,64,64]{2,1,0:T(8,128)}, f32[12,64,64]{2,1,0:T(8,128)S(1)}, u32[]{:S(2)}) copy-start(f32[12,64,64]{2,1,0:T(8,128)S(1)} %get-tuple-element.1354) | copy-start | bytes 589828
  596.2 136.1 %all-gather.15.cloned.1.call-start = ((), (), s32[]{:S(2)}) async-start(), calls=%async_computation.4 | async-start | bytes 3342336 | tf_op jit(solution)/shard_map/all_gather | solution.py:50
  600.6 841.2 %all-reduce.25.cloned.1.call-start = ((), (), s32[]{:S(2)}) async-start(), calls=%async_computation.1 | async-start | bytes 6291456 | tf_op jit(solution)/shard_map/psum | solution.py:310
  611.0 23.8 %copy-start.46 = (bf16[1024,768]{0,1:T(8,128)(2,1)S(1)}, bf16[1024,768]{0,1:T(8,128)(2,1)}, u32[]{:S(2)}) copy-start(bf16[1024,768]{0,1:T(8,128)(2,1)} %get-tuple-element.2103) | copy-start | bytes 4718596
  801.7 31.2 %copy-start.25 = (f32[256,12]{0,1:T(8,128)S(1)}, f32[256,12]{0,1:T(8,128)}, u32[]{:S(2)}) copy-start(f32[256,12]{0,1:T(8,128)} %get-tuple-element.2710) | copy-start | bytes 36868 | tf_op jit(solution)/shard_map/transpose(jvp())/while
  872.9 31.2 %copy-start.25 = (f32[256,12]{0,1:T(8,128)S(1)}, f32[256,12]{0,1:T(8,128)}, u32[]{:S(2)}) copy-start(f32[256,12]{0,1:T(8,128)} %get-tuple-element.2710) | copy-start | bytes 36868 | tf_op jit(solution)/shard_map/transpose(jvp())/while
  944.1 31.2 %copy-start.25 = (f32[256,12]{0,1:T(8,128)S(1)}, f32[256,12]{0,1:T(8,128)}, u32[]{:S(2)}) copy-start(f32[256,12]{0,1:T(8,128)} %get-tuple-element.2710) | copy-start | bytes 36868 | tf_op jit(solution)/shard_map/transpose(jvp())/while
  1015.3 31.2 %copy-start.25 = (f32[256,12]{0,1:T(8,128)S(1)}, f32[256,12]{0,1:T(8,128)}, u32[]{:S(2)}) copy-start(f32[256,12]{0,1:T(8,128)} %get-tuple-element.2710) | copy-start | bytes 36868 | tf_op jit(solution)/shard_map/transpose(jvp())/while
  1095.9 18.8 %copy-start.31 = (f32[1,256,12]{1,2,0:T(8,128)S(1)}, f32[1,256,12]{1,2,0:T(8,128)}, u32[]{:S(2)}) copy-start(f32[1,256,12]{1,2,0:T(8,128)} %get-tuple-element.2669) | copy-start | bytes 36868 | tf_op jit(solution)/shard_map/transpose(jvp())/while
  1095.9 20.3 %copy-start.102 = (f32[12]{0:T(128)S(1)}, f32[12]{0:T(128)}, u32[]{:S(2)}) copy-start(f32[12]{0:T(128)} %get-tuple-element.2671) | copy-start | bytes 148 | tf_op jit(solution)/shard_map/transpose(jvp())/while
  1095.9 21.1 %copy-start.40 = (f32[256,12]{0,1:T(8,128)S(1)}, f32[256,12]{0,1:T(8,128)}, u32[]{:S(2)}) copy-start(f32[256,12]{0,1:T(8,128)} %get-tuple-element.2672) | copy-start | bytes 36868 | tf_op jit(solution)/shard_map/transpose(jvp())/while
  1096.0 21.1 %copy-start.45 = (f32[256,12]{0,1:T(8,128)S(1)}, f32[256,12]{0,1:T(8,128)}, u32[]{:S(2)}) copy-start(f32[256,12]{0,1:T(8,128)} %copy-done.43) | copy-start | bytes 36868 | tf_op jit(solution)/shard_map/transpose(jvp())/while
  1096.0 21.1 %copy-start.66 = (f32[1,12]{0,1:T(8,128)S(1)}, f32[1,12]{0,1:T(8,128)}, u32[]{:S(2)}) copy-start(f32[1,12]{0,1:T(8,128)} %get-tuple-element.2673) | copy-start | bytes 148 | tf_op jit(solution)/shard_map/transpose(jvp())/while
  1096.0 21.1 %copy-start.79 = (f32[256,12]{0,1:T(8,128)S(1)}, f32[256,12]{0,1:T(8,128)}, u32[]{:S(2)}) copy-start(f32[256,12]{0,1:T(8,128)} %get-tuple-element.2670) | copy-start | bytes 36868 | tf_op jit(solution)/shard_map/transpose(jvp())/while
  1096.0 21.1 %copy-start.80 = (f32[256,12]{0,1:T(8,128)S(1)}, f32[256,12]{0,1:T(8,128)}, u32[]{:S(2)}) copy-start(f32[256,12]{0,1:T(8,128)} %get-tuple-element.2674) | copy-start | bytes 36868 | tf_op jit(solution)/shard_map/transpose(jvp())/while
  1096.0 21.1 %copy-start.85 = (f32[256]{0:T(256)S(1)}, f32[256]{0:T(256)}, u32[]{:S(2)}) copy-start(f32[256]{0:T(256)} %copy-done.84) | copy-start | bytes 3076 | tf_op jit(solution)/shard_map/transpose(jvp())/while
  1096.0 28.3 %copy-start.26 = (f32[256,12]{0,1:T(8,128)S(1)}, f32[256,12]{0,1:T(8,128)}, u32[]{:S(2)}) copy-start(f32[256,12]{0,1:T(8,128)} %get-tuple-element.2655) | copy-start | bytes 36868 | tf_op jit(solution)/shard_map/transpose(jvp())/while
  1156.6 20.3 %copy-start.102 = (f32[12]{0:T(128)S(1)}, f32[12]{0:T(128)}, u32[]{:S(2)}) copy-start(f32[12]{0:T(128)} %get-tuple-element.2671) | copy-start | bytes 148 | tf_op jit(solution)/shard_map/transpose(jvp())/while
  1156.6 21.1 %copy-start.40 = (f32[256,12]{0,1:T(8,128)S(1)}, f32[256,12]{0,1:T(8,128)}, u32[]{:S(2)}) copy-start(f32[256,12]{0,1:T(8,128)} %get-tuple-element.2672) | copy-start | bytes 36868 | tf_op jit(solution)/shard_map/transpose(jvp())/while
  1156.6 21.1 %copy-start.45 = (f32[256,12]{0,1:T(8,128)S(1)}, f32[256,12]{0,1:T(8,128)}, u32[]{:S(2)}) copy-start(f32[256,12]{0,1:T(8,128)} %copy-done.43) | copy-start | bytes 36868 | tf_op jit(solution)/shard_map/transpose(jvp())/while
  1156.7 21.1 %copy-start.66 = (f32[1,12]{0,1:T(8,128)S(1)}, f32[1,12]{0,1:T(8,128)}, u32[]{:S(2)}) copy-start(f32[1,12]{0,1:T(8,128)} %get-tuple-element.2673) | copy-start | bytes 148 | tf_op jit(solution)/shard_map/transpose(jvp())/while
  1156.7 21.1 %copy-start.79 = (f32[256,12]{0,1:T(8,128)S(1)}, f32[256,12]{0,1:T(8,128)}, u32[]{:S(2)}) copy-start(f32[256,12]{0,1:T(8,128)} %get-tuple-element.2670) | copy-start | bytes 36868 | tf_op jit(solution)/shard_map/transpose(jvp())/while
  1156.7 21.1 %copy-start.80 = (f32[256,12]{0,1:T(8,128)S(1)}, f32[256,12]{0,1:T(8,128)}, u32[]{:S(2)}) copy-start(f32[256,12]{0,1:T(8,128)} %get-tuple-element.2674) | copy-start | bytes 36868 | tf_op jit(solution)/shard_map/transpose(jvp())/while
  1156.7 21.1 %copy-start.85 = (f32[256]{0:T(256)S(1)}, f32[256]{0:T(256)}, u32[]{:S(2)}) copy-start(f32[256]{0:T(256)} %copy-done.84) | copy-start | bytes 3076 | tf_op jit(solution)/shard_map/transpose(jvp())/while
  1156.7 28.3 %copy-start.26 = (f32[256,12]{0,1:T(8,128)S(1)}, f32[256,12]{0,1:T(8,128)}, u32[]{:S(2)}) copy-start(f32[256,12]{0,1:T(8,128)} %get-tuple-element.2655) | copy-start | bytes 36868 | tf_op jit(solution)/shard_map/transpose(jvp())/while
  1217.3 20.3 %copy-start.102 = (f32[12]{0:T(128)S(1)}, f32[12]{0:T(128)}, u32[]{:S(2)}) copy-start(f32[12]{0:T(128)} %get-tuple-element.2671) | copy-start | bytes 148 | tf_op jit(solution)/shard_map/transpose(jvp())/while
  1217.3 21.1 %copy-start.40 = (f32[256,12]{0,1:T(8,128)S(1)}, f32[256,12]{0,1:T(8,128)}, u32[]{:S(2)}) copy-start(f32[256,12]{0,1:T(8,128)} %get-tuple-element.2672) | copy-start | bytes 36868 | tf_op jit(solution)/shard_map/transpose(jvp())/while
  1217.3 21.1 %copy-start.45 = (f32[256,12]{0,1:T(8,128)S(1)}, f32[256,12]{0,1:T(8,128)}, u32[]{:S(2)}) copy-start(f32[256,12]{0,1:T(8,128)} %copy-done.43) | copy-start | bytes 36868 | tf_op jit(solution)/shard_map/transpose(jvp())/while
  1217.4 21.1 %copy-start.66 = (f32[1,12]{0,1:T(8,128)S(1)}, f32[1,12]{0,1:T(8,128)}, u32[]{:S(2)}) copy-start(f32[1,12]{0,1:T(8,128)} %get-tuple-element.2673) | copy-start | bytes 148 | tf_op jit(solution)/shard_map/transpose(jvp())/while
  1217.4 21.1 %copy-start.79 = (f32[256,12]{0,1:T(8,128)S(1)}, f32[256,12]{0,1:T(8,128)}, u32[]{:S(2)}) copy-start(f32[256,12]{0,1:T(8,128)} %get-tuple-element.2670) | copy-start | bytes 36868 | tf_op jit(solution)/shard_map/transpose(jvp())/while
  1217.4 21.1 %copy-start.80 = (f32[256,12]{0,1:T(8,128)S(1)}, f32[256,12]{0,1:T(8,128)}, u32[]{:S(2)}) copy-start(f32[256,12]{0,1:T(8,128)} %get-tuple-element.2674) | copy-start | bytes 36868 | tf_op jit(solution)/shard_map/transpose(jvp())/while
  1217.4 21.1 %copy-start.85 = (f32[256]{0:T(256)S(1)}, f32[256]{0:T(256)}, u32[]{:S(2)}) copy-start(f32[256]{0:T(256)} %copy-done.84) | copy-start | bytes 3076 | tf_op jit(solution)/shard_map/transpose(jvp())/while
  1217.4 28.3 %copy-start.26 = (f32[256,12]{0,1:T(8,128)S(1)}, f32[256,12]{0,1:T(8,128)}, u32[]{:S(2)}) copy-start(f32[256,12]{0,1:T(8,128)} %get-tuple-element.2655) | copy-start | bytes 36868 | tf_op jit(solution)/shard_map/transpose(jvp())/while
  1278.0 20.3 %copy-start.102 = (f32[12]{0:T(128)S(1)}, f32[12]{0:T(128)}, u32[]{:S(2)}) copy-start(f32[12]{0:T(128)} %get-tuple-element.2671) | copy-start | bytes 148 | tf_op jit(solution)/shard_map/transpose(jvp())/while
  1278.0 21.1 %copy-start.40 = (f32[256,12]{0,1:T(8,128)S(1)}, f32[256,12]{0,1:T(8,128)}, u32[]{:S(2)}) copy-start(f32[256,12]{0,1:T(8,128)} %get-tuple-element.2672) | copy-start | bytes 36868 | tf_op jit(solution)/shard_map/transpose(jvp())/while
  1278.0 21.1 %copy-start.45 = (f32[256,12]{0,1:T(8,128)S(1)}, f32[256,12]{0,1:T(8,128)}, u32[]{:S(2)}) copy-start(f32[256,12]{0,1:T(8,128)} %copy-done.43) | copy-start | bytes 36868 | tf_op jit(solution)/shard_map/transpose(jvp())/while
  1278.0 21.1 %copy-start.66 = (f32[1,12]{0,1:T(8,128)S(1)}, f32[1,12]{0,1:T(8,128)}, u32[]{:S(2)}) copy-start(f32[1,12]{0,1:T(8,128)} %get-tuple-element.2673) | copy-start | bytes 148 | tf_op jit(solution)/shard_map/transpose(jvp())/while
  1278.1 21.1 %copy-start.79 = (f32[256,12]{0,1:T(8,128)S(1)}, f32[256,12]{0,1:T(8,128)}, u32[]{:S(2)}) copy-start(f32[256,12]{0,1:T(8,128)} %get-tuple-element.2670) | copy-start | bytes 36868 | tf_op jit(solution)/shard_map/transpose(jvp())/while
  1278.1 21.1 %copy-start.80 = (f32[256,12]{0,1:T(8,128)S(1)}, f32[256,12]{0,1:T(8,128)}, u32[]{:S(2)}) copy-start(f32[256,12]{0,1:T(8,128)} %get-tuple-element.2674) | copy-start | bytes 36868 | tf_op jit(solution)/shard_map/transpose(jvp())/while
  1278.1 21.1 %copy-start.85 = (f32[256]{0:T(256)S(1)}, f32[256]{0:T(256)}, u32[]{:S(2)}) copy-start(f32[256]{0:T(256)} %copy-done.84) | copy-start | bytes 3076 | tf_op jit(solution)/shard_map/transpose(jvp())/while
  1278.1 28.3 %copy-start.26 = (f32[256,12]{0,1:T(8,128)S(1)}, f32[256,12]{0,1:T(8,128)}, u32[]{:S(2)}) copy-start(f32[256,12]{0,1:T(8,128)} %get-tuple-element.2655) | copy-start | bytes 36868 | tf_op jit(solution)/shard_map/transpose(jvp())/while
  1366.0 19.8 %copy-start.75 = (f32[1024,2,12]{0,2,1:T(8,128)S(1)}, f32[1024,2,12]{0,2,1:T(8,128)}, u32[]{:S(2)}) copy-start(f32[1024,2,12]{0,2,1:T(8,128)} %copy-done.74) | copy-start | bytes 294916
  1366.0 20.0 %copy-start.90 = (f32[1024,2,12]{0,2,1:T(8,128)S(1)}, f32[1024,2,12]{0,2,1:T(8,128)}, u32[]{:S(2)}) copy-start(f32[1024,2,12]{0,2,1:T(8,128)} %get-tuple-element.2135) | copy-start | bytes 294916
  1384.2 14.7 collective-permute-start.1
  1410.7 111.1 %all-reduce.23.cloned.1.call-start = ((), (), s32[]{:S(2)}) async-start(), calls=%async_computation | async-start | bytes 3145728 | tf_op jit(solution)/shard_map/psum | solution.py:247
  1425.2 290.2 %all-reduce.27.cloned.1.call-start = ((), (), s32[]{:S(2)}) async-start(), calls=%async_computation.6 | async-start | bytes 15925248 | tf_op jit(solution)/shard_map/psum | solution.py:334
  1441.8 80.0 %copy-start.111 = (f32[1024]{0:T(1024)S(1)}, f32[1024]{0:T(1024)}, u32[]{:S(2)}) copy-start(f32[1024]{0:T(1024)} %copy-done.110) | copy-start | bytes 12292
  (174 other events, 1100.9 us)
Sparse Core Ops, SparseCore 0:
  285.2 64.0 all-gather.12
  459.5 64.1 all-gather.10
  596.3 66.6 all-gather.16
  665.6 66.6 all-gather.14
  1410.8 19.0 all-reduce.24
  1432.8 21.5 all-reduce.22
  1462.0 253.3 all-reduce.26
where the time goes:
time: 1760 us; the launch traced here: 1730 us
  local copies, waits for them, and re-layouts  639 us (36%)
  other arithmetic  312 us (18%)
  waiting for transfers between devices  309 us (18%)
  matrix products  293 us (17%)
  blocking collectives  126 us (7%)
  loops' own time  24.9 us (1%)
  between operations  19.1 us (1%)
    dynamic_update_slice x104, local copies, waits for them, and re-layouts, device_local(): lax.scan(jax.checkpoint(group_step), (zero_state, seg_before), (to_blocks...  378 us
    psum x1, waiting for transfers between devices, body(): lax.psum((norm_gain_grad, gate_proj_grad, value_proj_grad, state_proj_gra...  187 us
    dot_general x24, matrix products, group_step(): inner_y = jnp.einsum('tsh,shp->thp', weight, values, precision=HIGHEST)  111 us
    all_gather x2, waiting for transfers between devices, prefix(): lax.all_gather(a.astype(kind), axis)  93.6 us
    another operation x93, other arithmetic  75.1 us
    psum x1, blocking collectives, body(): lax.psum((norm_gain_grad, gate_proj_grad, value_proj_grad, state_proj_gra...  75 us
    dynamic_slice x32, local copies, waits for them, and re-layouts, device_local(): lax.scan(jax.checkpoint(group_step), (zero_state, seg_before), (to_blocks...  42.7 us
    unnamed x1, blocking collectives  40.2 us
  transfers between devices with their start and end apart: 9, of which 5 were waited for; matrix products, arithmetic and copies ran while one was open for 19% of the time, Pallas kernels for 0%

commit v1 on v0

v1 whole, which is shorter than its diff:
```python
from functools import partial

import jax
import jax.numpy as jnp
from jax import lax
from jax.experimental import pallas as pl
from jax.experimental.pallas import tpu as pltpu
from jax.sharding import PartitionSpec as P

EPSILON = 1e-05
LEN_MOST = 4096
Q = 128
TB = 256
HP = 16
MIB = 1024 * 1024
HIGHEST = lax.Precision.HIGHEST
F32 = jnp.float32
BF16 = jnp.bfloat16
MESH = pl.DeviceIdType.MESH


def nn(a, b, precision=None):
    return jnp.dot(a, b, preferred_element_type=F32, precision=precision)


def nt(a, b, precision=None):
    return lax.dot_general(a, b, (((1,), (1,)), ((), ())), preferred_element_type=F32, precision=precision)


def tn(a, b, precision=None):
    return lax.dot_general(a, b, (((0,), (0,)), ((), ())), preferred_element_type=F32, precision=precision)


def iota(shape, axis):
    return lax.broadcasted_iota(jnp.int32, shape, axis)


def spread_matrix(width, hdim):
    return (iota((HP, width), 1) // hdim == iota((HP, width), 0)).astype(F32)


def split(x):
    hi = x.astype(BF16)
    return hi, (x - hi.astype(F32)).astype(BF16)


def widen(rows, spread2):
    hi, lo = split(rows.T)
    return nn(jnp.concatenate([hi, lo], axis=1), spread2)


def widen_col(col, spread):
    return tn(jnp.broadcast_to(col, (HP, 8)), spread, HIGHEST)[0:1]


def silu(x):
    return x * jax.nn.sigmoid(x)


def softplus(x):
    return jnp.maximum(x, 0.0) + jnp.log1p(jnp.exp(-jnp.abs(x)))


def step_parts(step, bias, dlog):
    dt = softplus(step + bias)
    ld = -jnp.exp(dlog) * dt
    upto = (iota((Q, Q), 0) <= iota((Q, Q), 1)).astype(F32)
    run = nn(ld, upto, HIGHEST)
    return dt, ld, run, run - ld


def state_factors(dt, run, bef, t0, b):
    t1 = t0 + Q
    tok = iota((1, Q), 1) + t0
    ef = jnp.where((tok < b) | (t0 > b), jnp.exp(bef[:HP]), 0.0)
    er = jnp.where((tok >= b) | (t1 < b), jnp.exp(run[HP:, Q - 1 : Q] - run[HP:]), 0.0)
    tf = jnp.where((tok >= b) | (t1 <= b), jnp.exp(run[:HP, Q - 1 : Q] - run[:HP]), 0.0) * dt[:HP]
    tr = jnp.where((tok < b) | (t0 >= b), jnp.exp(bef[HP:]), 0.0) * dt[HP:]
    return ef, er, tf, tr


def conv_mask(tok, shift, b, off0):
    lost = ((tok < b) & (tok + off0 < shift)) | ((tok >= b) & (tok < b + shift))
    return jnp.where(lost, 0.0, 1.0)


def put_message(ref, state, passed):
    hi, lo = split(passed)
    ref[0:64, :] = state.astype(BF16)
    row = iota((16, state.shape[1]), 0)
    tail = jnp.where(row == 0, hi.astype(F32), jnp.where(row == 1, lo.astype(F32), 0.0))
    ref[64:80, :] = tail.astype(BF16)


def chain(ref):
    total = ref[0, 0:64, :].astype(F32)
    passed = None
    for k in range(1, ref.shape[0]):
        tail = ref[k - 1, 64:80, :].astype(F32)
        here = tail[0:1] + tail[1:2]
        passed = here if passed is None else passed * here
        total = total + passed * ref[k, 0:64, :].astype(F32)
    return total


def front_kernel(len_ref, hid_ref, halo_ref, gain_ref, wg_ref, wv_ref, ws_ref, wstep_ref, tapv_ref, taps_ref,
                 bias_ref, dlog_ref,
                 meta_ref, normt_ref, gate_ref, joined_ref, jhalo_ref, act_ref, step_ref, inc_ref, pexp_ref,
                 msgf_ref, msgr_ref,
                 ext, sumf, sumr, prod):
    blk = pl.program_id(0)
    nblk = pl.num_programs(0)
    inner = wv_ref.shape[1]
    both = inner + ws_ref.shape[1]
    base = lax.axis_index("seq") * (TB * nblk)
    length = TB * nblk

    @pl.when(blk == 0)
    def _():
        def one(j, carry):
            start, b, off0, after = carry
            end = start + len_ref[j]
            b = jnp.where((start > base) & (start < base + length), start - base, b)
            off0 = jnp.where((start <= base) & (base < end), base - start, off0)
            after = jnp.where(end == base + length, 0, after)
            return end, b, off0, after

        _, b, off0, after = lax.fori_loop(
            0, len_ref.shape[0], one, (jnp.int32(0), jnp.int32(length + 1), jnp.int32(0), jnp.int32(1)))
        meta_ref[0] = b
        meta_ref[1] = off0
        meta_ref[2] = jnp.where(off0 > 0, 1, 0).astype(jnp.int32)
        meta_ref[3] = after

    b = meta_ref[0]
    off0 = meta_ref[1]

    def norm(x):
        x = x.astype(F32)
        scale = lax.rsqrt(jnp.mean(x * x, axis=1, keepdims=True) + EPSILON)
        return (x * scale * gain_ref[...]).astype(BF16)

    @pl.when(blk == 0)
    def _():
        nh = norm(halo_ref[...])
        pre = jnp.concatenate([nn(nh, wv_ref[...]), nn(nh, ws_ref[...])], axis=1).astype(BF16)
        jhalo_ref[...] = pre
        ext[0:8, :] = pre.astype(F32)[8:16]
        sumf[...] = jnp.zeros_like(sumf)
        sumr[...] = jnp.zeros_like(sumr)
        prod[...] = jnp.ones_like(prod)

    @pl.when(blk > 0)
    def _():
        ext[0:8, :] = ext[TB : TB + 8, :]

    x = hid_ref[...].astype(F32)
    scale = lax.rsqrt(jnp.mean(x * x, axis=1, keepdims=True) + EPSILON)
    normed32 = x * scale * gain_ref[...]
    normed = normed32.astype(BF16)
    normt_ref[...] = normed.T
    gate_ref[...] = nn(normed, wg_ref[...])
    jv = nn(normed, wv_ref[...]).astype(BF16)
    js = nn(normed, ws_ref[...]).astype(BF16)
    joined_ref[:, :inner] = jv
    joined_ref[:, inner:] = js
    ext[8 : 8 + TB, :inner] = jv.astype(F32)
    ext[8 : 8 + TB, inner:] = js.astype(F32)
    step_all = nt(wstep_ref[...], normed)
    step_ref[...] = step_all
    tok = iota((TB, 1), 0) + blk * TB
    masks = [conv_mask(tok, m, b, off0) for m in range(4)]
    for j in range(both // 128):
        cols = slice(j * 128, (j + 1) * 128)
        tap = tapv_ref[:, cols] if j * 128 < inner else taps_ref[:, j * 128 - inner : (j + 1) * 128 - inner]
        total = ext[8 : 8 + TB, cols] * tap[3:4]
        for m in range(1, 4):
            total = total + ext[8 - m : 8 - m + TB, cols] * tap[3 - m : 4 - m] * masks[m]
        act_ref[:, cols] = silu(total).astype(BF16)
    spread = spread_matrix(inner, 64)
    spread2 = jnp.concatenate([spread, spread], axis=0).astype(BF16)
    for q in range(TB // Q):
        rows = slice(q * Q, (q + 1) * Q)
        t0 = blk * TB + q * Q
        dt, ld, run, bef = step_parts(step_all[:, rows], bias_ref[...], dlog_ref[...])
        _, _, tf, tr = state_factors(dt, run, bef, t0, b)
        values = act_ref[rows, :inner].astype(F32)
        maps_t = act_ref[rows, inner:].astype(F32).T.astype(BF16)
        incf = nn(maps_t[0:64], (values * widen(tf, spread2)).astype(BF16))
        incr = nn(maps_t[128:192], (values * widen(tr, spread2)).astype(BF16))
        inc_ref[q, 0:64, :] = incf
        inc_ref[q, 64:128, :] = incr
        gone = jnp.exp(run[:, Q - 1 : Q])
        passf = jnp.where((t0 <= b) & (b < t0 + Q), 0.0, 1.0)
        passr = jnp.where((t0 < b) & (b <= t0 + Q), 0.0, 1.0)
        pf = widen_col(gone[:HP], spread) * passf
        pr = widen_col(gone[HP:], spread) * passr
        pexp_ref[q, 0:1, :] = pf
        pexp_ref[q, 1:2, :] = pr
        sumf[...] = pf * sumf[...] + incf
        sumr[...] = sumr[...] + prod[1:2, :] * incr
        prod[0:1, :] = prod[0:1, :] * pf
        prod[1:2, :] = prod[1:2, :] * pr

    @pl.when(blk == nblk - 1)
    def _():
        put_message(msgf_ref, sumf[...], prod[0:1, :] * meta_ref[2].astype(F32))
        put_message(msgr_ref, sumr[...], prod[1:2, :] * meta_ref[3].astype(F32))


def swap_kernel(reach, up_ref, down_ref, from_low, from_high, up_send, up_recv, down_send, down_recv):
    me = lax.axis_index("seq")
    core = lax.axis_index("head")
    count = lax.axis_size("seq")
    barrier = pltpu.get_barrier_semaphore()
    for k in range(1, reach + 1):
        @pl.when(me + k < count)
        def _():
            pl.semaphore_signal(barrier, inc=1, device_id=(me + k, core), device_id_type=MESH)

        @pl.when(me >= k)
        def _():
            pl.semaphore_signal(barrier, inc=1, device_id=(me - k, core), device_id_type=MESH)

    pl.semaphore_wait(barrier, jnp.minimum(me, reach) + jnp.minimum(count - 1 - me, reach))

    def up(k):
        return pltpu.make_async_remote_copy(
            src_ref=up_ref, dst_ref=from_low.at[k - 1], send_sem=up_send.at[k - 1], recv_sem=up_recv.at[k - 1],
            device_id=(me + k, core), device_id_type=MESH)

    def down(k):
        return pltpu.make_async_remote_copy(
            src_ref=down_ref, dst_ref=from_high.at[k - 1], send_sem=down_send.at[k - 1],
            recv_sem=down_recv.at[k - 1], device_id=(me - k, core), device_id_type=MESH)

    for k in range(1, reach + 1):
        @pl.when(me + k < count)
        def _():
            up(k).start()

        @pl.when(me >= k)
        def _():
            down(k).start()

    for k in range(1, reach + 1):
        @pl.when(me < k)
        def _():
            from_low[k - 1] = jnp.zeros_like(from_low[k - 1])

        @pl.when(me + k >= count)
        def _():
            from_high[k - 1] = jnp.zeros_like(from_high[k - 1])

    for k in range(1, reach + 1):
        @pl.when(me + k < count)
        def _():
            up(k).wait_send()
            down(k).wait_recv()

        @pl.when(me >= k)
        def _():
            down(k).wait_send()
            up(k).wait_recv()


def swap(up, down, reach, ident):
    shape = jax.ShapeDtypeStruct((reach,) + up.shape, up.dtype)
    vm = pl.BlockSpec(memory_space=pltpu.VMEM)
    return pl.pallas_call(
        partial(swap_kernel, reach),
        out_shape=(shape, shape),
        in_specs=[vm, vm],
        out_specs=(vm, vm),
        scratch_shapes=[pltpu.SemaphoreType.DMA((reach,))] * 4,
        compiler_params=pltpu.CompilerParams(
            collective_id=ident, has_side_effects=True, vmem_limit_bytes=16 * MIB),
    )(up, down)


def core_swap_kernel(count, *refs):
    ins, outs, (send, recv) = refs[:count], refs[count : 2 * count], refs[2 * count :]
    me = lax.axis_index("seq")
    other = 1 - lax.axis_index("head")
    barrier = pltpu.get_barrier_semaphore()
    pl.semaphore_signal(barrier, inc=1, device_id=(me, other), device_id_type=MESH)
    pl.semaphore_wait(barrier, 1)
    copies = [
        pltpu.make_async_remote_copy(
            src_ref=ins[i], dst_ref=outs[i], send_sem=send.at[i], recv_sem=recv.at[i],
            device_id=(me, other), device_id_type=MESH)
        for i in range(count)
    ]
    for copy in copies:
        copy.start()
    for copy in copies:
        copy.wait()


def core_swap(arrays, ident):
    count = len(arrays)
    vm = pl.BlockSpec(memory_space=pltpu.VMEM)
    return pl.pallas_call(
        partial(core_swap_kernel, count),
        out_shape=tuple(jax.ShapeDtypeStruct(a.shape, a.dtype) for a in arrays),
        in_specs=[vm] * count,
        out_specs=(vm,) * count,
        scratch_shapes=[pltpu.SemaphoreType.DMA((count,))] * 2,
        compiler_params=pltpu.CompilerParams(
            collective_id=ident, has_side_effects=True, vmem_limit_bytes=32 * MIB),
    )(*arrays)


def chunk_scores(maps, t0, b):
    tr, tc = iota((Q, Q), 0), iota((Q, Q), 1)
    same = (tr + t0 < b) == (tc + t0 < b)
    fwd = nt(maps[:, 64:128], maps[:, 0:64])
    rev = nt(maps[:, 192:256], maps[:, 128:192])
    return jnp.where((tr > tc) & same, fwd, jnp.where((tr < tc) & same, rev, 0.0))


def halves(x):
    left = iota(x.shape, 1) < 64
    zero = jnp.zeros_like(x)
    return jnp.concatenate([jnp.where(left, x, zero), jnp.where(left, zero, x)], axis=0)


def mix_kernel(meta_ref, act_ref, step_ref, bias_ref, dlog_ref, gate_ref, cot_ref, wo_ref, ggain_ref, skip_ref,
               inc_ref, pexp_ref, low_ref, high_ref,
               mixed_ref, state_ref, sums_ref):
    blk = pl.program_id(0)
    inner = wo_ref.shape[0]
    nchunk = inc_ref.shape[0]
    b = meta_ref[0]

    @pl.when(blk == 0)
    def _():
        hf = chain(low_ref) * meta_ref[2].astype(F32)
        hr = chain(high_ref) * meta_ref[3].astype(F32)
        for c in range(nchunk):
            state_ref[c, 0:64, :] = hf.astype(BF16)
            hf = pexp_ref[c, 0:1, :] * hf + inc_ref[c, 0:64, :]
            d = nchunk - 1 - c
            state_ref[d, 64:128, :] = hr.astype(BF16)
            hr = pexp_ref[d, 1:2, :] * hr + inc_ref[d, 64:128, :]

    spread = spread_matrix(inner, 64)
    spread2 = jnp.concatenate([spread, spread], axis=0).astype(BF16)
    skip = widen_col(skip_ref[...], spread)
    lower = iota((Q, Q), 0) > iota((Q, Q), 1)
    u_all = nt(cot_ref[...], wo_ref[...])
    lane = iota((Q, 128), 1)
    for q in range(TB // Q):
        rows = slice(q * Q, (q + 1) * Q)
        t0 = blk * TB + q * Q
        chunk = blk * (TB // Q) + q
        dt, ld, run, bef = step_parts(step_ref[:, rows], bias_ref[...], dlog_ref[...])
        ef, er, _, _ = state_factors(dt, run, bef, t0, b)
        ldt = jnp.log(jnp.maximum(dt, 1e-37))
        rowf = ldt[:HP] - run[:HP]
        rowr = ldt[HP:] + bef[HP:]
        cols = jnp.concatenate([bef[:HP], -run[HP:]], axis=0).T
        maps = act_ref[rows, inner:]
        scores = chunk_scores(maps, t0, b)
        efe, ere = widen(ef, spread2), widen(er, spread2)
        state = state_ref[chunk]
        ys = nn(maps[:, 64:128], state[0:64]) * efe + nn(maps[:, 192:256], state[64:128]) * ere
        square = jnp.zeros((Q, 1), F32)
        cross = jnp.zeros((Q, 1), F32)
        for j in range(inner // 128):
            lanes = slice(j * 128, (j + 1) * 128)
            weights = []
            for h in (2 * j, 2 * j + 1):
                e = jnp.where(lower, cols[:, h : h + 1] + rowf[h : h + 1],
                              cols[:, HP + h : HP + h + 1] + rowr[h : h + 1])
                weights.append((jnp.exp(jnp.minimum(e, 60.0)) * scores).astype(BF16))
            vp = act_ref[rows, lanes]
            y = nn(jnp.concatenate(weights, axis=1), halves(vp))
            y = y + ys[:, lanes] + skip[:, lanes] * vp.astype(F32)
            mixed_ref[rows, lanes] = y
            gated = y * silu(gate_ref[rows, lanes])
            square = square + jnp.sum(gated * gated, axis=1, keepdims=True)
            cross = cross + jnp.sum(gated * (u_all[rows, lanes] * ggain_ref[:, lanes]), axis=1, keepdims=True)
        both = jnp.where(lane == 0, square, jnp.where(lane == 1, cross, 0.0))
        sums_ref[:, rows] = both.T[0:8]


def gate_kernel(meta_ref, mine_ref, other_ref, mixed_ref, gate_ref, cot_ref, wo_ref, ggain_ref, act_ref, step_ref,
                bias_ref, dlog_ref, pexp_ref, normt_ref,
                out_ref, ggate_ref, dy_ref, dhy_ref, msgf_ref, msgr_ref, small_ref, ggw_ref, ngt,
                gsum_f, gsum_r, prod):
    blk = pl.program_id(0)
    nblk = pl.num_programs(0)
    inner = wo_ref.shape[0]
    whole = inner * 2
    b = meta_ref[0]

    @pl.when(blk == 0)
    def _():
        gsum_f[...] = jnp.zeros_like(gsum_f)
        gsum_r[...] = jnp.zeros_like(gsum_r)
        prod[...] = jnp.ones_like(prod)
        small_ref[...] = jnp.zeros_like(small_ref)

    sums = mine_ref[...] + other_ref[...]
    sums = jnp.concatenate([sums, jnp.zeros((120, TB), F32)], axis=0).T
    scale = lax.rsqrt(sums[:, 0:1] / whole + EPSILON)
    back = scale * scale * scale * sums[:, 1:2] / whole
    gng = nt(cot_ref[...], wo_ref[...])
    for j in range(inner // 128):
        lanes = slice(j * 128, (j + 1) * 128)
        mixed = mixed_ref[:, lanes]
        pre = gate_ref[:, lanes]
        sig = jax.nn.sigmoid(pre)
        gated = mixed * (pre * sig)
        ng = gated * scale
        gain = ggain_ref[:, lanes]
        ng_low = (ng * gain).astype(BF16)
        ngt[blk, :, lanes] = ng_low
        g = gng[:, lanes]
        small_ref[0:1, lanes] += jnp.sum(g * ng, axis=0, keepdims=True)
        grad_gated = scale * (g * gain) - gated * back
        dy = grad_gated * (pre * sig)
        small_ref[1:2, lanes] += jnp.sum(dy * act_ref[:, lanes].astype(F32), axis=0, keepdims=True)
        dy_ref[:, lanes] = dy
        ggate_ref[pl.ds(blk * TB, TB), lanes] = (
            grad_gated * mixed * (sig * (1.0 + pre * (1.0 - sig)))).astype(BF16)
    out_ref[...] = nn(ngt[blk], wo_ref[...]).astype(BF16)
    spread = spread_matrix(inner, 64)
    spread2 = jnp.concatenate([spread, spread], axis=0).astype(BF16)
    for q in range(TB // Q):
        rows = slice(q * Q, (q + 1) * Q)
        t0 = blk * TB + q * Q
        chunk = blk * (TB // Q) + q
        dt, ld, run, bef = step_parts(step_ref[:, rows], bias_ref[...], dlog_ref[...])
        ef, er, _, _ = state_factors(dt, run, bef, t0, b)
        maps_t = act_ref[rows, inner:].astype(F32).T.astype(BF16)
        dy = dy_ref[rows, :]
        df = nn(maps_t[64:128], (dy * widen(ef, spread2)).astype(BF16))
        dr = nn(maps_t[192:256], (dy * widen(er, spread2)).astype(BF16))
        dhy_ref[q, 0:64, :] = df
        dhy_ref[q, 64:128, :] = dr
        pf, pr = pexp_ref[chunk, 0:1, :], pexp_ref[chunk, 1:2, :]
        gsum_f[...] = gsum_f[...] + prod[0:1, :] * df
        gsum_r[...] = pr * gsum_r[...] + dr
        prod[0:1, :] = prod[0:1, :] * pf
        prod[1:2, :] = prod[1:2, :] * pr

    @pl.when(blk == nblk - 1)
    def _():
        before = meta_ref[2].astype(F32)
        after = meta_ref[3].astype(F32)
        put_message(msgf_ref, gsum_f[...] * before, prod[0:1, :] * before)
        put_message(msgr_ref, gsum_r[...] * after, prod[1:2, :] * after)
        ggw_ref[...] = nn(normt_ref[...], ggate_ref[...]).astype(BF16)


def outgrad_kernel(ng_ref, cot_ref, gow_ref):
    gow_ref[...] = tn(ng_ref[...], cot_ref[...]).astype(BF16)


def back_kernel(meta_ref, act_ref, step_ref, bias_ref, dlog_ref, dy_ref, skip_ref, state_ref, dhy_ref, pexp_ref,
                low_ref, high_ref, joined_ref, jprev_ref, jhalo_ref, tapv_ref, taps_ref,
                gv_ref, gs_ref, gstep_ref, lent_ref, convg_ref, heads_ref,
                dstate, ext, jext, rowbuf, dact):
    step_no = pl.program_id(0)
    nblk = pl.num_programs(0)
    blk = nblk - 1 - step_no
    inner = tapv_ref.shape[1]
    both = act_ref.shape[1]
    nchunk = state_ref.shape[0]
    b = meta_ref[0]
    off0 = meta_ref[1]

    @pl.when(step_no == 0)
    def _():
        df = chain(high_ref)
        dr = chain(low_ref)
        for c in range(nchunk):
            d = nchunk - 1 - c
            dstate[d, 0:64, :] = df.astype(BF16)
            df = pexp_ref[d, 0:1, :] * df + dhy_ref[d, 0:64, :]
            dstate[c, 64:128, :] = dr.astype(BF16)
            dr = pexp_ref[c, 1:2, :] * dr + dhy_ref[c, 64:128, :]
        ext[TB : TB + 8, :] = jnp.zeros((8, both), F32)
        convg_ref[...] = jnp.zeros_like(convg_ref)
        heads_ref[...] = jnp.zeros_like(heads_ref)
        rowbuf[...] = jnp.zeros_like(rowbuf)

    @pl.when(step_no > 0)
    def _():
        ext[TB : TB + 8, :] = ext[0:8, :]

    spread = spread_matrix(inner, 64)
    spread_low = spread.astype(BF16)
    spread2 = jnp.concatenate([spread_low, spread_low], axis=0)
    skip = widen_col(skip_ref[...], spread)
    i0, i1 = iota((Q, Q), 0), iota((Q, Q), 1)
    after, before = (i0 > i1), (i0 < i1)
    diag = i0 == i1
    sums_low = jnp.concatenate([after, before], axis=1).astype(BF16)
    after32, before32 = after.astype(F32), before.astype(F32)
    for q in reversed(range(TB // Q)):
        rows = slice(q * Q, (q + 1) * Q)
        t0 = blk * TB + q * Q
        chunk = blk * (TB // Q) + q
        dt, ld, run, bef = step_parts(step_ref[:, rows], bias_ref[...], dlog_ref[...])
        ef, er, tf, tr = state_factors(dt, run, bef, t0, b)
        ldt = jnp.log(jnp.maximum(dt, 1e-37))
        cols = jnp.concatenate([ldt[:HP] - run[:HP], ldt[HP:] + bef[HP:]], axis=0).T
        rowf, rowr = bef[:HP], -run[HP:]
        maps = act_ref[rows, inner:]
        entf, readf, entr, readr = maps[:, 0:64], maps[:, 64:128], maps[:, 128:192], maps[:, 192:256]
        same = (i0 + t0 < b) == (i1 + t0 < b)
        okf, okr = before & same, after & same
        scores = jnp.where(okf, nt(entf, readf), jnp.where(okr, nt(entr, readr), 0.0))
        state = state_ref[chunk]
        grad_state = dstate[chunk]
        dscore = jnp.zeros((Q, Q), F32)
        efe, ere = widen(ef, spread2), widen(er, spread2)
        tfe, tre = widen(tf, spread2), widen(tr, spread2)
        dy = dy_ref[rows, :]
        values = act_ref[rows, :inner].astype(F32)
        dyf, dyr = dy * efe, dy * ere
        dyf_low, dyr_low = dyf.astype(BF16), dyr.astype(BF16)
        dreadf = nt(dyf_low, state[0:64])
        dreadr = nt(dyr_low, state[64:128])
        qf = nt(spread_low, (nn(readf, state[0:64]) * dyf).astype(BF16))
        qr = nt(spread_low, (nn(readr, state[64:128]) * dyr).astype(BF16))
        dvf = nn(entf, grad_state[0:64]) * tfe
        dvr = nn(entr, grad_state[64:128]) * tre
        wf = nt(spread_low, (values * dvf).astype(BF16))
        wr = nt(spread_low, (values * dvr).astype(BF16))
        dentf = nt((values * tfe).astype(BF16), grad_state[0:64])
        dentr = nt((values * tre).astype(BF16), grad_state[64:128])
        through = state.astype(F32) * grad_state.astype(F32)
        zf = jnp.sum(through[0:64], axis=0, keepdims=True) * pexp_ref[chunk, 0:1, :]
        zr = jnp.sum(through[64:128], axis=0, keepdims=True) * pexp_ref[chunk, 1:2, :]
        zf = nt(spread, jnp.broadcast_to(zf, (8, inner)), HIGHEST)[:, 0:1]
        zr = nt(spread, jnp.broadcast_to(zr, (8, inner)), HIGHEST)[:, 0:1]
        for j in range(inner // 128):
            lanes = slice(j * 128, (j + 1) * 128)
            vp = act_ref[rows, lanes]
            dyp = dy_ref[rows, lanes].astype(BF16)
            dw = nt(halves(vp), dyp)
            weights = []
            for i, h in enumerate((2 * j, 2 * j + 1)):
                e = jnp.where(before, cols[:, h : h + 1] + rowf[h : h + 1],
                              cols[:, HP + h : HP + h + 1] + rowr[h : h + 1])
                x = jnp.exp(jnp.minimum(e, 60.0))
                weights.append((x * scores).astype(BF16))
                dwx = dw[i * Q : (i + 1) * Q] * x
                dscore = dscore + dwx
                sums = nn((dwx * scores).astype(BF16), sums_low)
                pf, pr = sums[:, :Q], sums[:, Q:]
                rowbuf[h : h + 1, :] = jnp.sum(jnp.where(before, pf, 0.0), axis=0, keepdims=True)
                rowbuf[HP + h : HP + h + 1, :] = jnp.sum(jnp.where(after, pr, 0.0), axis=0, keepdims=True)
                rowbuf[2 * HP + h : 2 * HP + h + 1, :] = jnp.sum(jnp.where(diag, pf, 0.0), axis=0, keepdims=True)
                rowbuf[3 * HP + h : 3 * HP + h + 1, :] = jnp.sum(jnp.where(diag, pr, 0.0), axis=0, keepdims=True)
            dv = nn(jnp.concatenate(weights, axis=1), halves(dyp))
            dact[rows, lanes] = dv + dvf[:, lanes] + dvr[:, lanes] + dy[:, lanes] * skip[:, lanes]
        dsf = jnp.where(okf, dscore, 0.0)
        dsr = jnp.where(okr, dscore, 0.0)
        dsf_low, dsr_low = dsf.astype(BF16), dsr.astype(BF16)
        dentf = dentf + nn(dsf_low, readf)
        dentr = dentr + nn(dsr_low, readr)
        dreadf = dreadf + nn(dsf.T.astype(BF16), entf)
        dreadr = dreadr + nn(dsr.T.astype(BF16), entr)
        dact[rows, inner:] = jnp.concatenate([dentf, dreadf, dentr, dreadr], axis=1)
        late = nn(jnp.concatenate([qf, wr], axis=0), after32, HIGHEST)
        early = nn(jnp.concatenate([wf, qr], axis=0), before32, HIGHEST)
        dld = jnp.concatenate(
            [rowbuf[0:HP] + late[:HP] + early[:HP] + zf, rowbuf[HP : 2 * HP] + late[HP:] + early[HP:] + zr], axis=0)
        dldt = rowbuf[2 * HP : 4 * HP] + jnp.concatenate([wf, wr], axis=0)
        sig = jax.nn.sigmoid(step_ref[:, rows] + bias_ref[...])
        ratio = jnp.where(dt < 1e-30, 1.0, sig / jnp.maximum(dt, 1e-30))
        graw = dldt * ratio - jnp.exp(dlog_ref[...]) * sig * dld
        gstep_ref[:, rows] = graw.astype(BF16)
        heads_ref[:, 0:1] += jnp.sum(graw, axis=1, keepdims=True)
        heads_ref[:, 1:2] += jnp.sum(dld * ld, axis=1, keepdims=True)

    prev = jnp.where(blk == 0, jhalo_ref[...], jprev_ref[...])
    jext[0:16, :] = prev.astype(F32)
    jext[16 : 16 + TB, :] = joined_ref[...].astype(F32)
    tok = iota((TB, 1), 0) + blk * TB
    masks = [conv_mask(tok, m, b, off0) for m in range(4)]
    later_masks = [conv_mask(tok + m, m, b, off0) for m in range(4)]
    edge_masks = [conv_mask(iota((8, 1), 0) - 8 + m, m, b, off0) for m in range(4)]
    for j in range(both // 128):
        cols = slice(j * 128, (j + 1) * 128)
        tap = tapv_ref[:, cols] if j * 128 < inner else taps_ref[:, j * 128 - inner : (j + 1) * 128 - inner]
        shifted = [jext[16 : 16 + TB, cols]]
        total = shifted[0] * tap[3:4]
        for m in range(1, 4):
            shifted.append(jext[16 - m : 16 - m + TB, cols] * masks[m])
            total = total + shifted[m] * tap[3 - m : 4 - m]
        sig = jax.nn.sigmoid(total)
        dconv = dact[:, cols] * (sig * (1.0 + total * (1.0 - sig)))
        ext[0:TB, cols] = dconv
        for m in range(4):
            convg_ref[3 - m : 4 - m, cols] += jnp.sum(dconv * shifted[m], axis=0, keepdims=True)
        grad = dconv * tap[3:4]
        for m in range(1, 4):
            grad = grad + ext[m : m + TB, cols] * later_masks[m] * tap[3 - m : 4 - m]
        if j * 128 < inner:
            gv_ref[:, cols] = grad
        else:
            gs_ref[:, j * 128 - inner : (j + 1) * 128 - inner] = grad

    @pl.when(step_no == nblk - 1)
    def _():
        first = jnp.concatenate([jnp.zeros((8, both), F32), ext[0:8, :]], axis=0)
        tap = jnp.concatenate([tapv_ref[...], taps_ref[...]], axis=1)
        lent = jnp.zeros((8, both), F32)
        for m in range(1, 4):
            lent = lent + first[m : m + 8] * edge_masks[m] * tap[3 - m : 4 - m]
        lent_ref[...] = lent


def down_kernel(gv_ref, gs_ref, next_ref, gstep_ref, ggate_ref, normt_ref, wg_ref, wv_ref, wstep_ref,
                gn_ref, gso_ref, gvw_ref, gstepw_ref,
                gvl):
    blk = pl.program_id(0)
    nblk = pl.num_programs(0)
    inner = wg_ref.shape[1]
    last = (blk == nblk - 1).astype(F32)
    gvl[pl.ds(blk * TB, TB), :] = gv_ref[...].astype(BF16)

    tail = gv_ref[TB - 16 : TB, :] + jnp.concatenate(
        [jnp.zeros((8, inner), F32), next_ref[:, :inner] * last], axis=0)
    gvl[pl.ds(blk * TB + TB - 16, 16), :] = tail.astype(BF16)
    gso_ref[...] = gs_ref[...].astype(BF16)
    tail = gs_ref[TB - 16 : TB, :] + jnp.concatenate(
        [jnp.zeros((8, gs_ref.shape[1]), F32), next_ref[:, inner:] * last], axis=0)
    gso_ref[TB - 16 : TB, :] = tail.astype(BF16)
    gn = nt(ggate_ref[...], wg_ref[...]) + nt(gvl[pl.ds(blk * TB, TB), :], wv_ref[...])
    gn = gn + tn(gstep_ref[:, pl.ds(blk * TB, TB)], wstep_ref[...])
    gn_ref[...] = gn.astype(BF16)

    @pl.when(blk == nblk - 1)
    def _():
        gvw_ref[...] = nn(normt_ref[...], gvl[...]).astype(BF16)
        gstepw_ref[...] = nt(gstep_ref[...], normt_ref[...])


def end_kernel(mine_ref, other_ref, smine_ref, sother_ref, hid_ref, cot_ref, gain_ref, ws_ref, normt_ref,
               omine_ref, oother_ref,
               gh_ref, ngain_ref, gsw_ref, out_ref,
               gsl):
    blk = pl.program_id(0)
    nblk = pl.num_programs(0)

    @pl.when(blk == 0)
    def _():
        ngain_ref[...] = jnp.zeros_like(ngain_ref)

    grad_state = (smine_ref[...].astype(F32) + sother_ref[...].astype(F32)).astype(BF16)
    gsl[pl.ds(blk * TB, TB), :] = grad_state
    gn = mine_ref[...].astype(F32) + other_ref[...].astype(F32) + nt(grad_state, ws_ref[...])
    x = hid_ref[...].astype(F32)
    scale = lax.rsqrt(jnp.mean(x * x, axis=1, keepdims=True) + EPSILON)
    ngain_ref[0:1, :] += jnp.sum(gn * x * scale, axis=0, keepdims=True)
    v = gn * gain_ref[...]
    inner = jnp.mean(x * v, axis=1, keepdims=True)
    gh_ref[...] = cot_ref[...].astype(F32) + scale * v - x * (scale * scale * scale * inner)
    out_ref[...] = (x + (omine_ref[...].astype(F32) + oother_ref[...].astype(F32))).astype(BF16)

    @pl.when(blk == nblk - 1)
    def _():
        gsw_ref[...] = nn(normt_ref[...], gsl[...]).astype(BF16)


def whole_spec(array):
    zeros = (0,) * array.ndim
    return pl.BlockSpec(array.shape, lambda i: zeros)


def rows_spec(array, rows=TB, flip=0):
    rest = (0,) * (array.ndim - 1)
    if flip:
        return pl.BlockSpec((rows,) + array.shape[1:], lambda i: (flip - 1 - i,) + rest)
    return pl.BlockSpec((rows,) + array.shape[1:], lambda i: (i,) + rest)


def cols_spec(array, flip=0):
    if flip:
        return pl.BlockSpec((array.shape[0], TB), lambda i: (0, flip - 1 - i))
    return pl.BlockSpec((array.shape[0], TB), lambda i: (0, i))


SMEM_SPEC = pl.BlockSpec(memory_space=pltpu.SMEM)


def call(kernel, grid, ins, outs, scratch, vmem, flops):
    arrays = [a for a, _ in ins]
    return pl.pallas_call(
        kernel,
        grid=(grid,),
        in_specs=[s for _, s in ins],
        out_specs=[s for _, s in outs],
        out_shape=[jax.ShapeDtypeStruct(a.shape, a.dtype) for a, _ in outs],
        scratch_shapes=scratch,
        compiler_params=pltpu.CompilerParams(
            dimension_semantics=("arbitrary",), vmem_limit_bytes=vmem * MIB),
        cost_estimate=pl.CostEstimate(
            flops=int(flops), transcendentals=0,
            bytes_accessed=sum(a.size * a.dtype.itemsize for a in arrays)
            + sum(a.size * a.dtype.itemsize for a, _ in outs)),
    )(*arrays)


def padded(x, axis):
    pads = [(0, 0)] * x.ndim
    pads[axis] = (0, HP - x.shape[axis])
    return jnp.pad(x, pads)


def shape(dims, dtype):
    return jax.ShapeDtypeStruct(dims, dtype)


def body(
    hidden_in, norm_gain, gate_proj, value_proj, state_proj, step_proj, conv_value, conv_state,
    step_bias, decay_log, skip_scale, gate_gain, out_proj, lengths, cotangent,
):
    length, width = hidden_in.shape
    inner = gate_proj.shape[1]
    heads = decay_log.shape[0]
    maps = state_proj.shape[1]
    both = inner + maps
    nblk = length // TB
    nchunk = length // Q
    count = lax.axis_size("seq")
    reach = min(1 + (LEN_MOST - 2) // length, count - 1)
    mib = MIB

    halo = lax.ppermute(hidden_in[length - 16 :], "seq", [(i, i + 1) for i in range(count - 1)])
    wstep = padded(step_proj.transpose(0, 2, 1), 1).reshape(2 * HP, width)
    bias = padded(step_bias, 1).reshape(2 * HP, 1)
    dlog = padded(decay_log, 0)
    dlog = jnp.concatenate([dlog, dlog]).reshape(2 * HP, 1)
    skip = padded(skip_scale, 0).reshape(HP, 1)
    gain_in = norm_gain.reshape(1, width)
    gain_gate = gate_gain.reshape(1, inner)

    normt = shape((width, length), BF16)
    gate = shape((length, inner), F32)
    joined = shape((length, both), BF16)
    jhalo = shape((16, both), BF16)
    act = shape((length, both), BF16)
    step = shape((2 * HP, length), F32)
    inc = shape((nchunk, 128, inner), F32)
    pexp = shape((nchunk, 2, inner), F32)
    msg = shape((80, inner), BF16)
    meta = shape((8,), jnp.int32)
    cq = TB // Q
    meta, normt, gate, joined, jhalo, act, step, inc, pexp, msgf, msgr = call(
        front_kernel, nblk,
        [(lengths, SMEM_SPEC), (hidden_in, rows_spec(hidden_in)), (halo, whole_spec(halo)),
         (gain_in, whole_spec(gain_in)), (gate_proj, whole_spec(gate_proj)), (value_proj, whole_spec(value_proj)),
         (state_proj, whole_spec(state_proj)), (wstep, whole_spec(wstep)), (conv_value, whole_spec(conv_value)),
         (conv_state, whole_spec(conv_state)), (bias, whole_spec(bias)), (dlog, whole_spec(dlog))],
        [(meta, SMEM_SPEC), (normt, cols_spec(normt)), (gate, rows_spec(gate)), (joined, rows_spec(joined)),
         (jhalo, whole_spec(jhalo)), (act, rows_spec(act)), (step, cols_spec(step)), (inc, rows_spec(inc, cq)),
         (pexp, rows_spec(pexp, cq)), (msg, whole_spec(msg)), (msg, whole_spec(msg))],
        [pltpu.VMEM((TB + 8, both), F32), pltpu.VMEM((64, inner), F32), pltpu.VMEM((64, inner), F32),
         pltpu.VMEM((8, inner), F32)],
        48, 2 * length * width * (2 * inner + maps))
    low, high = swap(msgf, msgr, reach, 1)

    mixed = shape((length, inner), F32)
    state = shape((nchunk, 128, inner), BF16)
    sums = shape((8, length), F32)
    mixed, state, sums = call(
        mix_kernel, nblk,
        [(meta, SMEM_SPEC), (act, rows_spec(act)), (step, cols_spec(step)), (bias, whole_spec(bias)),
         (dlog, whole_spec(dlog)), (gate, rows_spec(gate)), (cotangent, rows_spec(cotangent)),
         (out_proj, whole_spec(out_proj)), (gain_gate, whole_spec(gain_gate)), (skip, whole_spec(skip)),
         (inc, whole_spec(inc)), (pexp, whole_spec(pexp)), (low, whole_spec(low)), (high, whole_spec(high))],
        [(mixed, rows_spec(mixed)), (state, whole_spec(state)), (sums, cols_spec(sums))],
        [], 48, 2 * length * width * inner * 2)
    (sums_other,) = core_swap([sums], 2)

    out_part = shape((length, width), BF16)
    ggate = shape((length, inner), BF16)
    dy = shape((length, inner), F32)
    dhy = shape((nchunk, 128, inner), F32)
    small = shape((8, inner), F32)
    ggw = shape((width, inner), BF16)
    ng = shape((nblk, TB, inner), BF16)
    out_part, ggate, dy, dhy, msgf, msgr, small, ggw, ng = call(
        gate_kernel, nblk,
        [(meta, SMEM_SPEC), (sums, cols_spec(sums)), (sums_other, cols_spec(sums_other)), (mixed, rows_spec(mixed)),
         (gate, rows_spec(gate)), (cotangent, rows_spec(cotangent)), (out_proj, whole_spec(out_proj)),
         (gain_gate, whole_spec(gain_gate)), (act, rows_spec(act)), (step, cols_spec(step)),
         (bias, whole_spec(bias)), (dlog, whole_spec(dlog)), (pexp, whole_spec(pexp)), (normt, whole_spec(normt))],
        [(out_part, rows_spec(out_part)), (ggate, whole_spec(ggate)), (dy, rows_spec(dy)),
         (dhy, rows_spec(dhy, cq)), (msg, whole_spec(msg)), (msg, whole_spec(msg)), (small, whole_spec(small)),
         (ggw, whole_spec(ggw)), (ng, whole_spec(ng))],
        [pltpu.VMEM((64, inner), F32), pltpu.VMEM((64, inner), F32), pltpu.VMEM((8, inner), F32)],
        48, 2 * length * width * inner * 4)
    low, high = swap(msgr, msgf, reach, 3)

    ng = ng.reshape(length, inner)
    gow = shape((inner, width), BF16)
    (gow,) = call(
        outgrad_kernel, 1, [(ng, whole_spec(ng)), (cotangent, whole_spec(cotangent))], [(gow, whole_spec(gow))],
        [], 32, 2 * length * width * inner)
    ggw, gow = lax.psum((ggw, gow), "seq")

    gv = shape((length, inner), F32)
    gs = shape((length, maps), F32)
    gstep = shape((2 * HP, length), BF16)
    lent = shape((8, both), F32)
    convg = shape((8, both), F32)
    hsum = shape((2 * HP, 128), F32)
    prev_spec = pl.BlockSpec((16, both), lambda i: (jnp.maximum((nblk - 1 - i) * (TB // 16) - 1, 0), 0))
    gv, gs, gstep, lent, convg, hsum = call(
        back_kernel, nblk,
        [(meta, SMEM_SPEC), (act, rows_spec(act, TB, nblk)), (step, cols_spec(step, nblk)), (bias, whole_spec(bias)),
         (dlog, whole_spec(dlog)), (dy, rows_spec(dy, TB, nblk)), (skip, whole_spec(skip)),
         (state, whole_spec(state)), (dhy, whole_spec(dhy)), (pexp, whole_spec(pexp)), (low, whole_spec(low)),
         (high, whole_spec(high)), (joined, rows_spec(joined, TB, nblk)), (joined, prev_spec),
         (jhalo, whole_spec(jhalo)), (conv_value, whole_spec(conv_value)), (conv_state, whole_spec(conv_state))],
        [(gv, rows_spec(gv, TB, nblk)), (gs, rows_spec(gs, TB, nblk)), (gstep, cols_spec(gstep, nblk)),
         (lent, whole_spec(lent)), (convg, whole_spec(convg)), (hsum, whole_spec(hsum))],
        [pltpu.VMEM((nchunk, 128, inner), BF16), pltpu.VMEM((TB + 8, both), F32), pltpu.VMEM((TB + 16, both), F32),
         pltpu.VMEM((4 * HP, Q), F32), pltpu.VMEM((TB, both), F32)],
        56, 2 * length * width * inner * 4)
    from_next = lax.ppermute(lent, "seq", [(i + 1, i) for i in range(count - 1)])

    gn = shape((length, width), BF16)
    gso = shape((length, maps), BF16)
    gvw = shape((width, inner), BF16)
    gstepw = shape((2 * HP, width), F32)
    gn, gso, gvw, gstepw = call(
        down_kernel, nblk,
        [(gv, rows_spec(gv)), (gs, rows_spec(gs)), (from_next, whole_spec(from_next)), (gstep, whole_spec(gstep)),
         (ggate, rows_spec(ggate)), (normt, whole_spec(normt)), (gate_proj, whole_spec(gate_proj)),
         (value_proj, whole_spec(value_proj)), (wstep, whole_spec(wstep))],
        [(gn, rows_spec(gn)), (gso, rows_spec(gso)), (gvw, whole_spec(gvw)), (gstepw, whole_spec(gstepw))],
        [pltpu.VMEM((length, inner), BF16)],
        48, 2 * length * width * inner * 3)
    gn_other, gso_other, out_other = core_swap([gn, gso, out_part], 4)

    gh = shape((length, width), F32)
    ngain = shape((8, width), F32)
    gsw = shape((width, maps), BF16)
    out = shape((length, width), BF16)
    gh, ngain, gsw, out = call(
        end_kernel, nblk,
        [(gn, rows_spec(gn)), (gn_other, rows_spec(gn_other)), (gso, rows_spec(gso)),
         (gso_other, rows_spec(gso_other)), (hidden_in, rows_spec(hidden_in)), (cotangent, rows_spec(cotangent)),
         (gain_in, whole_spec(gain_in)), (state_proj, whole_spec(state_proj)), (normt, whole_spec(normt)),
         (out_part, rows_spec(out_part)), (out_other, rows_spec(out_other))],
        [(gh, rows_spec(gh)), (ngain, whole_spec(ngain)), (gsw, whole_spec(gsw)), (out, rows_spec(out))],
        [pltpu.VMEM((length, maps), BF16)],
        48, 2 * length * width * maps * 2)

    gvw, gsw, gstepw = lax.psum((gvw, gsw, gstepw), "seq")
    small, convg, hsum, ngain = lax.psum((small[0:2], convg[0:4], hsum[:, 0:2], ngain[0]), "seq")
    conv_state_grad = lax.psum(convg[:, inner:], "head")
    gstepw = gstepw.reshape(2, HP, width)[:, :heads].transpose(0, 2, 1)
    hsum = hsum.reshape(2, HP, 2)[:, :heads]
    return (
        out,
        gh,
        ngain,
        ggw.astype(F32),
        gvw.astype(F32),
        gsw.astype(F32),
        gstepw,
        convg[:, :inner],
        conv_state_grad,
        hsum[:, :, 0],
        hsum[0, :, 1] + hsum[1, :, 1],
        jnp.sum(small[1].reshape(heads, inner // heads), axis=1),
        small[0],
        gow.astype(F32),
    )


def solution(mesh):
    in_specs = (
        P("seq", None),
        P(),
        P(None, "head"),
        P(None, "head"),
        P(),
        P(None, None, "head"),
        P(None, "head"),
        P(),
        P(None, "head"),
        P("head"),
        P("head"),
        P("head"),
        P("head", None),
        P(),
        P("seq", None),
    )
    out_specs = (
        P("seq", None),
        P("seq", None),
        P(),
        P(None, "head"),
        P(None, "head"),
        P(),
        P(None, None, "head"),
        P(None, "head"),
        P(),
        P(None, "head"),
        P("head"),
        P("head"),
        P("head"),
        P("head", None),
    )
    return jax.shard_map(body, mesh=mesh, in_specs=in_specs, out_specs=out_specs, check_vma=False)
```

time: 1760 us -> 456 us (0.26); the launches traced: 1730 us -> 455 us
  local copies, waits for them, and re-layouts: 639 us -> 26.3 us
  other arithmetic: 312 us -> 7.97 us
  matrix products: 293 us -> 0 us
  Pallas kernels: 0 us -> 145 us
  waiting for transfers between devices: 309 us -> 178 us
  blocking collectives: 126 us -> 76.3 us
  loops' own time: 24.9 us -> 0 us
    dynamic_update_slice x104 -> x0, local copies, waits for them, and re-layouts: 378 us -> none  [device_local(): lax.scan(jax.checkpoint(group_step), (zero_state, seg_before), (to_blocks...]
    dot_general x133 -> x0, matrix products: 293 us -> none  [the longest x24 111 us: group_step(): inner_y = jnp.einsum('tsh,shp->thp', weight, values, precision=HIGHEST)]
    pallas_call x0 -> x11, Pallas kernels: none -> 145 us  [the longest x7 108 us: call(): pl.pallas_call(kernel, grid=(grid,), in_specs=[s for _, s in ins], out_sp...]
    all_gather x4 -> x0, waiting for transfers between devices: 117 us -> none  [the longest x2 93.6 us: prefix(): lax.all_gather(a.astype(kind), axis)]
    another operation x93 -> x0, other arithmetic: 75.1 us -> none
    reduce_sum x29 -> x1, other arithmetic: 49.4 us -> 0.63 us  [body(): jnp.sum(small[1].reshape(heads, inner // heads), axis=1)]
    convert_element_type x63 -> x4, other arithmetic: 54.3 us -> 6.75 us  [the longest x1 2.03 us: body(): gsw.astype(F32)]
    dynamic_slice x32 -> x0, local copies, waits for them, and re-layouts: 42.7 us -> none  [device_local(): lax.scan(jax.checkpoint(group_step), (zero_state, seg_before), (to_blocks...]
  transfers between devices with their start and end apart: 9 -> 4, of which waited for: 5 -> 3; matrix products, arithmetic and copies ran while one was open for 19% -> 2% of each run, Pallas kernels for 0% -> 4%
where the time goes in v1:
time: 456 us; the launch traced here: 455 us
  waiting for transfers between devices  178 us (39%)
  Pallas kernels  145 us (32%)
  blocking collectives  76.3 us (17%)
  local copies, waits for them, and re-layouts  26.3 us (6%)
  between operations  14.3 us (3%)
  other arithmetic  7.97 us (2%)
  starting transfers between devices  6.42 us (1%)
    psum x1, waiting for transfers between devices, body(): ggw, gow = lax.psum((ggw, gow), 'seq')  169 us
    pallas_call x7, Pallas kernels, call(): pl.pallas_call(kernel, grid=(grid,), in_specs=[s for _, s in ins], out_sp...  108 us
    psum x1, blocking collectives, body(): lax.psum((small[0:2], convg[0:4], hsum[:, 0:2], ngain[0]), 'seq')  73.2 us
    pallas_call x2, Pallas kernels, swap(): pl.pallas_call(partial(swap_kernel, reach), out_shape=(shape, shape), in_...  30.1 us
    unnamed x75, local copies, waits for them, and re-layouts  17.8 us
  transfers between devices with their start and end apart: 4, of which 3 were waited for; matrix products, arithmetic and copies ran while one was open for 2% of the time, Pallas kernels for 4%

profile of v1, /device:TPU:0, one launch (start us, length us, event | category | flops | bytes accessed | tf_op | source)
XLA Modules:
  0.0 455.0 jit_solution(14055133489895006477)
XLA Ops:
  7.2 0.0 all-reduce.9.cloned.1.call-start
  7.2 0.7 slice.43
  8.0 4.8 %collective-permute-start = (bf16[16,768]{1,0:T(8,128)(2,1)S(1)}, bf16[16,768]{1,0:T(8,128)(2,1)S(1)}, u32[]{:S(2)}, u32[]{:S(2)}) collective-permute-start(bf16[16,768]{1,0:T(8,128)(2,1)S(1)} %slice.43), channel_id=1, source_target_pairs={{0,2},{2,4},{4,6},{6,8},{8,10},{10,12},{12,14},{14,16},{16,18},{18... | collective-permute-start | bytes 73736 | tf_op jit(solution)/shard_map/ppermute | solution.py:737
  12.8 0.7 pad.17
  13.5 0.1 maximum_bitcast_fusion
  13.5 0.7 pad_bitcast_fusion
  14.2 0.7 pad.16
  14.9 0.7 reshape.56.gain_ref
  15.6 0.7 reshape.60.ggain_ref
  16.3 0.1 copy.34.skip_ref
  16.4 0.1 reshape.65.bias_ref
  16.4 0.1 copy.31.dlog_ref
  16.5 0.8 copy.43
  17.4 1.0 copy-done.9
  18.3 1.3 copy-done.18
  19.6 1.3 copy-done.20
  20.9 0.7 copy-done.24
  21.6 0.7 copy-done.25
  22.3 0.7 copy-done.26
  22.9 17.0 %shard_map.254 = (s32[8]{0:T(128)S(1)}, bf16[768,1024]{1,0:T(8,128)(2,1)S(1)}, f32[1024,768]{1,0:T(8,128)}, bf16[1024,1024]{1,0:T(8,128)(2,1)}, bf16[16,1024]{1,...) custom-call(s32[9]{0:T(128)S(1)} %copy-done.26, ...), custom_call_target="tpu_custom_call" | custom-call | flops 2818572288 | bytes 16936260 | tf_op jit(solution)/shard_map/pallas_call | solution.py:696
  39.9 1.1 copy-done.6
  41.1 14.9 %shard_map.255 = (bf16[4,80,768]{2,1,0:T(8,128)(2,1)S(1)}, bf16[4,80,768]{2,1,0:T(8,128)(2,1)S(1)}) custom-call(bf16[80,768]{1,0:T(8,128)(2,1)S(1)} %get-tuple-element.64.up_ref, bf16[80,768]{1,0:T(8,128)(2,1)S(1)} %get-tuple-element.65.down_ref), custom_call_target="tpu_custom_call" | custom-call | tf_op jit(solution)/shard_map/pallas_call | solution.py:270
  56.0 17.5 %shard_map.256 = (f32[1024,768]{1,0:T(8,128)}, bf16[8,128,768]{2,1,0:T(8,128)(2,1)S(1)}, f32[8,1024]{1,0:T(8,128)S(1)}) custom-call(s32[8]{0:T(128)S(1)} %get-tuple-element.58.meta_ref, bf16[1024,1024]{1,0:T(8,128)(2,1)} %get-tuple-element.59.act_ref, f32[32,1024]{1,0:T(8,128)S(1)} %get-tuple-element.60.step_ref, f32[32,1]{1,0:T(8,128)S(1)} %reshape.65.bias_ref, ...), custom_call_target="tpu_custom_call" | custom-call | flops 2415919104 | bytes 17059168 | tf_op jit(solution)/shard_map/pallas_call | solution.py:696
  73.5 1.1 copy-done.17
  74.7 1.2 shard_map.257.other_ref
  76.0 16.8 %shard_map.258 = (bf16[1024,768]{1,0:T(8,128)(2,1)S(1)}, bf16[1024,768]{1,0:T(8,128)(2,1)S(1)}, f32[1024,768]{1,0:T(8,128)}, f32[8,128,768]{2,1,0:T(8,128)}, bf1...) custom-call(s32[8]{0:T(128)S(1)} %get-tuple-element.58.meta_ref, ...), custom_call_target="tpu_custom_call" | custom-call | flops 4831838208 | bytes 25423136 | tf_op jit(solution)/shard_map/pallas_call | solution.py:696
  92.7 1.2 copy-done.29
  94.0 15.2 %shard_map.259 = (bf16[4,80,768]{2,1,0:T(8,128)(2,1)S(1)}, bf16[4,80,768]{2,1,0:T(8,128)(2,1)S(1)}) custom-call(bf16[80,768]{1,0:T(8,128)(2,1)S(1)} %get-tuple-element.74.up_ref, bf16[80,768]{1,0:T(8,128)(2,1)S(1)} %get-tuple-element.75.down_ref), custom_call_target="tpu_custom_call" | custom-call | tf_op jit(solution)/shard_map/pallas_call | solution.py:270
  109.2 0.8 copy-done.22
  109.9 0.8 copy-done.23
  110.7 36.4 %shard_map.260 = (f32[1024,768]{1,0:T(8,128)}, f32[1024,256]{1,0:T(8,128)}, bf16[32,1024]{1,0:T(8,128)(2,1)}, f32[8,1024]{1,0:T(8,128)}, f32[8,1024]{1,0:T(8,128)}, /*index=5*/f32[32,128]{1,0:T(8,128)}) custom-call(s32[8]{0:T(128)} %copy-done.16, bf16[1024,1024]{1,0:T(8,128)(2,1)} %get-tuple-element.59.act_ref, f32[32,1024]{1,0:T(8,128)} %copy-done.11, ...), custom_call_target="tpu_custom_call" | custom-call | flops 4831838208 | bytes 19710304 | tf_op jit(solution)/shard_map/pallas_call | solution.py:696
  147.1 1.3 collective-permute-start.1
  148.4 4.7 %collective-permute-done.1.next_ref = f32[8,1024]{1,0:T(8,128)S(1)} collective-permute-done((f32[8,1024]{1,0:T(8,128)}, f32[8,1024]{1,0:T(8,128)S(1)}, u32[]{:S(2)}, u32[]{:S(2)}) %collective-permute-start.1) | collective-permute-done | bytes 32800 | tf_op jit(solution)/shard_map/ppermute | solution.py:830
  153.1 1.2 copy-done.28
  154.4 0.8 copy-done.30
  155.2 9.3 %shard_map.261 = (bf16[1024,768]{1,0:T(8,128)(2,1)}, bf16[1024,256]{1,0:T(8,128)(2,1)S(1)}, bf16[768,768]{1,0:T(8,128)(2,1)}, f32[32,768]{1,0:T(8,128)S(1)}) custom-call(f32[1024,768]{1,0:T(8,128)} %get-tuple-element.80.gv_ref, f32[1024,256]{1,0:T(8,128)S(1)} %copy-done.28, f32[8,1024]{1,0:T(8,128)S(1)} %collective-permute-done.1.next_ref, ...), custom_call_target="tpu_custom_call" | custom-call | flops 3623878656 | bytes 13221888 | tf_op jit(solution)/shard_map/pallas_call | solution.py:696
  164.5 0.8 copy-done.4
  165.3 0.7 copy.40
  166.0 0.3 all-reduce.11.cloned.1.call-start
  166.3 1.4 copy-done.27
  167.7 2.5 shard_map.264
  170.3 6.5 %shard_map.262 = (bf16[1024,768]{1,0:T(8,128)(2,1)S(1)}, bf16[1024,256]{1,0:T(8,128)(2,1)S(1)}, bf16[1024,768]{1,0:T(8,128)(2,1)S(1)}) custom-call(bf16[1024,768]{1,0:T(8,128)(2,1)S(1)} %copy-done.3, bf16[1024,256]{1,0:T(8,128)(2,1)S(1)} %copy-done.5, bf16[1024,768]{1,0:T(8,128)(2,1)S(1)} %get-tuple-element.87.refs_2_.omine_ref), custom_call_target="tpu_custom_call" | custom-call | tf_op jit(solution)/shard_map/pallas_call | solution.py:303
  176.8 1.1 copy-done.7
  177.9 8.1 %shard_map.263 = (f32[1024,768]{1,0:T(8,128)}, f32[8,768]{1,0:T(8,128)S(1)}, bf16[768,256]{1,0:T(8,128)(2,1)}, bf16[1024,768]{1,0:T(8,128)(2,1)}) custom-call(bf16[1024,768]{1,0:T(8,128)(2,1)S(1)} %copy-done.3, bf16[1024,768]{1,0:T(8,128)(2,1)S(1)} %get-tuple-element.88.other_ref, bf16[1024,256]{1,0:T(8,128)(2,1)S(1)} %copy-done.5, ...), custom_call_target="tpu_custom_call" | custom-call | flops 805306368 | bytes 17591296 | tf_op jit(solution)/shard_map/pallas_call | solution.py:696
  186.0 0.0 all-reduce.11.cloned.1.call-update
  186.1 0.7 copy-done.35
  186.8 0.1 copy.42
  186.9 73.2 %all-reduce.4 = (f32[768]{0:T(1024)}, f32[4,1024]{1,0:T(4,128)S(1)}, f32[2,16,2]{1,0,2:T(2,128)S(1)}, f32[2,768]{1,0:T(2,128)S(1)}) all-reduce(f32[768]{0:T(1024)S(1)} %slice_reduce_fusion.2, f32[4,1024]{1,0:T(4,128)S(1)} %slice.46, f32[2,16,2]{1,0,2:T(2,128)S(1)} %copy.42, ...), channel_id=1, replica_groups=mesh['seq'=16,'head'=2] {'seq'}, use_global_device_ids=true, to_apply=%region_0.1 | all-reduce | flops 6464 | bytes 51712 | tf_op jit(solution)/shard_map/psum | solution.py:861
  260.1 0.6 slice.57
  260.7 0.6 slice_reduce_fusion
  261.3 0.1 reshape_squeeze.3
  261.4 0.6 reduce_sum.9
  262.0 3.0 psum.76
  265.0 0.5 fusion
  265.5 0.6 slice_bitcast_fusion.1
  266.1 4.3 all-reduce.9.cloned.1.call-done
  270.5 1.5 slice_bitcast_fusion
  272.0 169.2 %all-reduce.11.cloned.1.call-done = (bf16[768,768]{1,0:T(8,128)(2,1)}, bf16[768,768]{1,0:T(8,128)(2,1)}, bf16[768,256]{1,0:T(8,128)(2,1)}, bf16[768,768]{1,0:T(8,128)(2,1)}) async-done(((bf16[768,768]{1,0:T(8,128)(2,1)}, bf16[768,768]{1,0:T(8,128)(2,1)}, bf16[768,256]{1,0:T(8,128)(2,1)}, bf16[768,768]{1,0:T(8,128)(2,1)}), (bf16[768,768]{1,0:T(8,128)(2,1)}, bf16[768,768]{1,0:T(8,128)(2,1)}, ...) | async-done | bytes 3932176 | tf_op jit(solution)/shard_map/psum | solution.py:809
  441.2 2.0 convert_element_type.21
  443.2 1.6 convert_element_type.19
  444.8 0.1 copy-done.33
  444.9 1.6 convert_element_type.20
  446.5 0.1 copy-done.32
  446.6 1.6 convert_element_type.22
  (62 shorter events, 0.2 us)
Async XLA Ops:
  7.2 263.3 %all-reduce.9.cloned.1.call-start = ((), (), s32[]{:S(2)}) async-start(), calls=%async_computation | async-start | bytes 196608 | tf_op jit(solution)/shard_map/psum | solution.py:860
  8.0 9.4 %collective-permute-start = (bf16[16,768]{1,0:T(8,128)(2,1)S(1)}, bf16[16,768]{1,0:T(8,128)(2,1)S(1)}, u32[]{:S(2)}, u32[]{:S(2)}) collective-permute-start(bf16[16,768]{1,0:T(8,128)(2,1)S(1)} %slice.43), channel_id=1, source_target_pairs={{0,2},{2,4},{4,6},{6,8},{8,10},{10,12},{12,14},{14,16},{16,18},{18... | collective-permute-start | bytes 73736 | tf_op jit(solution)/shard_map/ppermute | solution.py:737
  16.3 39.7 %copy-start.15 = (f32[16,1]{1,0:T(8,128)}, f32[16,1]{1,0:T(8,128)S(1)}, u32[]{:S(2)}) copy-start(f32[16,1]{1,0:T(8,128)S(1)} %copy.34.skip_ref) | copy-start | bytes 196
  16.4 59.5 %copy-start.12 = (f32[32,1]{1,0:T(8,128)}, f32[32,1]{1,0:T(8,128)S(1)}, u32[]{:S(2)}) copy-start(f32[32,1]{1,0:T(8,128)S(1)} %reshape.65.bias_ref) | copy-start | bytes 388
  16.5 59.4 %copy-start.13 = (f32[32,1]{1,0:T(8,128)}, f32[32,1]{1,0:T(8,128)S(1)}, u32[]{:S(2)}) copy-start(f32[32,1]{1,0:T(8,128)S(1)} %copy.31.dlog_ref) | copy-start | bytes 388
  17.3 1.0 copy-start.9
  18.3 1.3 copy-start.18
  19.6 1.3 copy-start.20
  20.9 0.7 copy-start.24
  21.6 0.7 copy-start.25
  22.3 0.7 copy-start.26
  22.9 33.1 %copy-start = (bf16[1024,768]{1,0:T(8,128)(2,1)S(1)}, bf16[1024,768]{1,0:T(8,128)(2,1)}, u32[]{:S(2)}) copy-start(bf16[1024,768]{1,0:T(8,128)(2,1)} %cot_ref.7) | copy-start | bytes 4718596
  22.9 33.1 %copy-start.8 = (bf16[768,768]{1,0:T(8,128)(2,1)S(1)}, bf16[768,768]{1,0:T(8,128)(2,1)}, u32[]{:S(2)}) copy-start(bf16[768,768]{1,0:T(8,128)(2,1)} %wo_ref.3) | copy-start | bytes 3538948
  39.9 1.1 copy-start.6
  41.1 32.5 %copy-start.31 = (bf16[16,1024]{1,0:T(8,128)(2,1)}, bf16[16,1024]{1,0:T(8,128)(2,1)S(1)}, u32[]{:S(2)}) copy-start(bf16[16,1024]{1,0:T(8,128)(2,1)S(1)} %get-tuple-element.79.jhalo_ref) | copy-start | bytes 98308
  41.1 34.9 %copy-start.11 = (f32[32,1024]{1,0:T(8,128)}, f32[32,1024]{1,0:T(8,128)S(1)}, u32[]{:S(2)}) copy-start(f32[32,1024]{1,0:T(8,128)S(1)} %get-tuple-element.60.step_ref) | copy-start | bytes 393220
  41.1 34.9 %copy-start.14 = (f32[8,2,768]{2,1,0:T(2,128)}, f32[8,2,768]{2,1,0:T(2,128)S(1)}, u32[]{:S(2)}) copy-start(f32[8,2,768]{2,1,0:T(2,128)S(1)} %get-tuple-element.63.pexp_ref) | copy-start | bytes 147460
  41.1 34.9 %copy-start.16 = (s32[8]{0:T(128)}, s32[8]{0:T(128)S(1)}, u32[]{:S(2)}) copy-start(s32[8]{0:T(128)S(1)} %get-tuple-element.58.meta_ref) | copy-start | bytes 100
  73.5 1.2 copy-start.17
  92.7 1.2 copy-start.29
  94.0 76.3 %copy-start.2 = (bf16[1024,768]{1,0:T(8,128)(2,1)}, bf16[1024,768]{1,0:T(8,128)(2,1)S(1)}, u32[]{:S(2)}) copy-start(bf16[1024,768]{1,0:T(8,128)(2,1)S(1)} %get-tuple-element.87.refs_2_.omine_ref) | copy-start | bytes 4718596
  109.2 0.8 copy-start.22
  109.9 0.8 copy-start.23
  110.7 42.4 %copy-start.19 = (bf16[768,768]{1,0:T(8,128)(2,1)S(1)}, bf16[768,768]{1,0:T(8,128)(2,1)}, u32[]{:S(2)}) copy-start(bf16[768,768]{1,0:T(8,128)(2,1)} %wg_ref.3) | copy-start | bytes 3538948
  110.7 42.4 %copy-start.21 = (bf16[768,768]{1,0:T(8,128)(2,1)S(1)}, bf16[768,768]{1,0:T(8,128)(2,1)}, u32[]{:S(2)}) copy-start(bf16[768,768]{1,0:T(8,128)(2,1)} %wv_ref.3) | copy-start | bytes 3538948
  147.1 6.0 %collective-permute-start.1 = (f32[8,1024]{1,0:T(8,128)}, f32[8,1024]{1,0:T(8,128)S(1)}, u32[]{:S(2)}, u32[]{:S(2)}) collective-permute-start(f32[8,1024]{1,0:T(8,128)} %get-tuple-element.82), channel_id=1, source_target_pairs={{2,0},{4,2},{6,4},{8,6},{10,8},{12,10},{14,12},{16,14},{18,16},{20... | collective-permute-start | bytes 98312 | tf_op jit(solution)/shard_map/ppermute | solution.py:830
  153.1 1.2 copy-start.28
  154.4 0.8 copy-start.30
  155.2 11.1 %copy-start.1 = (bf16[1024,768]{1,0:T(8,128)(2,1)S(1)}, bf16[1024,768]{1,0:T(8,128)(2,1)}, u32[]{:S(2)}) copy-start(bf16[1024,768]{1,0:T(8,128)(2,1)} %cot_ref.7) | copy-start | bytes 4718596
  164.5 0.8 copy-start.4
  166.0 275.1 %all-reduce.11.cloned.1.call-start = ((), (), s32[]{:S(2)}) async-start(), calls=%async_computation.1 | async-start | bytes 7864320 | tf_op jit(solution)/shard_map/psum | solution.py:809
  166.3 1.4 copy-start.27
  167.7 2.6 copy-start.3
  167.7 2.6 copy-start.5
  170.3 7.6 %copy-start.10 = (bf16[768,256]{1,0:T(8,128)(2,1)S(1)}, bf16[768,256]{1,0:T(8,128)(2,1)}, u32[]{:S(2)}) copy-start(bf16[768,256]{1,0:T(8,128)(2,1)} %ws_ref.3) | copy-start | bytes 1179652
  176.8 1.1 copy-start.7
  186.0 0.7 copy-start.35
  186.0 0.8 copy-start.36
  441.2 2.0 copy-start.34
  443.2 1.7 copy-start.33
  444.9 1.7 copy-start.32
Sparse Core Ops, SparseCore 0:
  166.2 104.2 all-reduce.8
  277.2 163.9 all-reduce.10

commit v2 on v1

--- a/solution.py
+++ b/solution.py
@@ -309,6 +309,168 @@
         compiler_params=pltpu.CompilerParams(
             collective_id=ident, has_side_effects=True, vmem_limit_bytes=32 * MIB),
     )(*arrays)
+
+
+def pieces_of(arrays, bits):
+    found = []
+    for a, array in enumerate(arrays):
+        rows, cols = array.shape
+        halvings = 0
+        while halvings < bits and (rows >> halvings) % 32 == 0:
+            halvings += 1
+        parts = 2 if rows * cols >= 512 * 512 else 1
+        for p in range(parts):
+            order = list(range(bits))
+            if len(found) % 2 and bits > 1:
+                order[0], order[1] = order[1], order[0]
+            found.append((a, p * (cols // parts), cols // parts, order, halvings))
+    return found
+
+
+def reduce_kernel(count, bits, *refs):
+    ins, tiny_ref = refs[:count], refs[count]
+    outs, tiny_out = refs[count + 1 : 2 * count + 1], refs[2 * count + 1]
+    works, recvs = refs[2 * count + 2 : 3 * count + 2], refs[3 * count + 2 : 4 * count + 2]
+    tiny_work, tiny_recv, rs_send, rs_recv, ag_send, ag_recv, t_send, t_recv = refs[4 * count + 2 :]
+    me = lax.axis_index("seq")
+    core = lax.axis_index("head")
+    bit = [lax.rem(me // (1 << k), 2) for k in range(bits)]
+    partner = [me + (1 - 2 * bit[k]) * (1 << k) for k in range(bits)]
+    pieces = pieces_of(ins, bits)
+
+    barrier = pltpu.get_barrier_semaphore()
+    for k in range(bits):
+        pl.semaphore_signal(barrier, inc=1, device_id=(partner[k], core), device_id_type=MESH)
+    pl.semaphore_wait(barrier, bits)
+
+    def remote(src, dst, send, recv, k):
+        return pltpu.make_async_remote_copy(
+            src_ref=src, dst_ref=dst, send_sem=send, recv_sem=recv, device_id=(partner[k], core),
+            device_id_type=MESH)
+
+    state = []
+    for p, (a, c0, cols, order, halvings) in enumerate(pieces):
+        state.append({"off": jnp.int32(0), "size": ins[a].shape[0], "slot": 0, "copy": None})
+
+    def rs_start(p, s):
+        a, c0, cols, order, halvings = pieces[p]
+        st = state[p]
+        k = order[s]
+        src = ins[a] if s == 0 else works[a]
+        half = st["size"] // 2 if s < halvings else st["size"]
+        if s < halvings:
+            st["keep"] = pl.multiple_of(st["off"] + bit[k] * half, 16)
+            st["give"] = pl.multiple_of(st["off"] + (1 - bit[k]) * half, 16)
+        else:
+            st["keep"] = st["give"] = st["off"]
+        st["half"] = half
+        st["copy"] = remote(
+            src.at[pl.ds(st["give"], half), pl.ds(c0, cols)],
+            recvs[a].at[pl.ds(st["slot"], half), pl.ds(c0, cols)],
+            rs_send.at[p, s], rs_recv.at[p, s], k)
+        st["copy"].start()
+
+    def rs_finish(p, s):
+        a, c0, cols, order, halvings = pieces[p]
+        st = state[p]
+        half, keep, slot = st["half"], st["keep"], st["slot"]
+        if s < halvings:
+            st["copy"].wait_recv()
+            st.setdefault("sends", []).append(st["copy"])
+        else:
+            st["copy"].wait()
+        src = ins[a] if s == 0 else works[a]
+        dst = outs[a] if s == bits - 1 else works[a]
+        step = 48 if half % 48 == 0 else 16
+
+        def add(i, _):
+            r = pl.multiple_of(keep + i * step, 16)
+            q = pl.multiple_of(slot + i * step, 16)
+            total = src[pl.ds(r, step), pl.ds(c0, cols)].astype(F32) + recvs[a][pl.ds(q, step), pl.ds(c0, cols)].astype(F32)
+            dst[pl.ds(r, step), pl.ds(c0, cols)] = total.astype(BF16)
+            return 0
+
+        lax.fori_loop(0, half // step, add, 0)
+        st["off"], st["size"], st["slot"] = keep, half, slot + half
+
+    def ag_start(p, s):
+        a, c0, cols, order, halvings = pieces[p]
+        st = state[p]
+        k = order[s]
+        where = outs[a].at[pl.ds(st["off"], st["size"]), pl.ds(c0, cols)]
+        st["copy"] = remote(where, where, ag_send.at[p, s], ag_recv.at[p, s], k)
+        st["copy"].start()
+
+    def ag_finish(p, s):
+        a, c0, cols, order, halvings = pieces[p]
+        st = state[p]
+        st["copy"].wait_recv()
+        st["sends"].append(st["copy"])
+        st["off"] = pl.multiple_of(st["off"] - bit[order[s]] * st["size"], 16)
+        st["size"] = 2 * st["size"]
+
+    def tiny_copy(s):
+        src = tiny_ref if s == 0 else tiny_work.at[s - 1]
+        return remote(src, tiny_recv.at[s], t_send.at[s], t_recv.at[s], s)
+
+    every = range(len(pieces))
+    for p in every:
+        rs_start(p, 0)
+    tiny_copy(0).start()
+    for s in range(bits):
+        for p in every:
+            rs_finish(p, s)
+            if s + 1 < bits:
+                rs_start(p, s + 1)
+            elif pieces[p][4]:
+                ag_start(p, pieces[p][4] - 1)
+        tiny_copy(s).wait()
+        total = (tiny_ref[...] if s == 0 else tiny_work[s - 1]) + tiny_recv[s]
+        if s + 1 < bits:
+            tiny_work[s] = total
+            tiny_copy(s + 1).start()
+        else:
+            tiny_out[...] = total
+    for back in range(bits):
+        for p in every:
+            s = pieces[p][4] - 1 - back
+            if s >= 0:
+                ag_finish(p, s)
+                if s > 0:
+                    ag_start(p, s - 1)
+    for p in every:
+        for copy in state[p].get("sends", []):
+            copy.wait_send()
+
+
+def reduce_all(arrays, tiny, devices, ident):
+    count = len(arrays)
+    bits = devices.bit_length() - 1
+    assert devices == 1 << bits
+    npieces = len(pieces_of(arrays, bits))
+    vm = pl.BlockSpec(memory_space=pltpu.VMEM)
+    received = []
+    for array in arrays:
+        rows, halvings = array.shape[0], pieces_of([array], bits)[0][4]
+        total = 0
+        for s in range(bits):
+            rows = rows // 2 if s < halvings else rows
+            total += rows
+        received.append(total)
+    outs = pl.pallas_call(
+        partial(reduce_kernel, count, bits),
+        out_shape=[jax.ShapeDtypeStruct(a.shape, a.dtype) for a in arrays + [tiny]],
+        in_specs=[vm] * (count + 1),
+        out_specs=[vm] * (count + 1),
+        scratch_shapes=[pltpu.VMEM(a.shape, a.dtype) for a in arrays]
+        + [pltpu.VMEM((r, a.shape[1]), a.dtype) for r, a in zip(received, arrays)]
+        + [pltpu.VMEM((bits,) + tiny.shape, F32), pltpu.VMEM((bits,) + tiny.shape, F32)]
+        + [pltpu.SemaphoreType.DMA((npieces, bits))] * 4
+        + [pltpu.SemaphoreType.DMA((bits,))] * 2,
+        compiler_params=pltpu.CompilerParams(
+            collective_id=ident, has_side_effects=True, vmem_limit_bytes=48 * MIB),
+    )(*arrays, tiny)
+    return outs[:count], outs[count]
 
 
 def chunk_scores(maps, t0, b):
@@ -640,26 +802,32 @@
     @pl.when(blk == nblk - 1)
     def _():
         gvw_ref[...] = nn(normt_ref[...], gvl[...]).astype(BF16)
-        gstepw_ref[...] = nt(gstep_ref[...], normt_ref[...])
+        gstepw_ref[...] = nt(gstep_ref[...], normt_ref[...]).astype(BF16)
 
 
 def end_kernel(mine_ref, other_ref, smine_ref, sother_ref, hid_ref, cot_ref, gain_ref, ws_ref, normt_ref,
-               omine_ref, oother_ref,
-               gh_ref, ngain_ref, gsw_ref, out_ref,
+               omine_ref, oother_ref, small_ref, hsum_ref, cmine_ref, cother_ref,
+               gh_ref, tiny_ref, gsw_ref, out_ref,
                gsl):
     blk = pl.program_id(0)
     nblk = pl.num_programs(0)
+    width = hid_ref.shape[1]
+    inner_dev = small_ref.shape[1]
 
     @pl.when(blk == 0)
     def _():
-        ngain_ref[...] = jnp.zeros_like(ngain_ref)
+        tiny_ref[...] = jnp.zeros_like(tiny_ref)
+        tiny_ref[0:2, :inner_dev] = small_ref[0:2, :]
+        tiny_ref[4:6, 0 : 2 * HP] = hsum_ref[...].T[0:2]
+        tiny_ref[8:16, :inner_dev] = cmine_ref[:, :inner_dev]
+        tiny_ref[8:16, inner_dev:] = cmine_ref[:, inner_dev:] + cother_ref[:, inner_dev:]
 
     grad_state = (smine_ref[...].astype(F32) + sother_ref[...].astype(F32)).astype(BF16)
     gsl[pl.ds(blk * TB, TB), :] = grad_state
     gn = mine_ref[...].astype(F32) + other_ref[...].astype(F32) + nt(grad_state, ws_ref[...])
     x = hid_ref[...].astype(F32)
     scale = lax.rsqrt(jnp.mean(x * x, axis=1, keepdims=True) + EPSILON)
-    ngain_ref[0:1, :] += jnp.sum(gn * x * scale, axis=0, keepdims=True)
+    tiny_ref[2:3, :width] += jnp.sum(gn * x * scale, axis=0, keepdims=True)
     v = gn * gain_ref[...]
     inner = jnp.mean(x * v, axis=1, keepdims=True)
     gh_ref[...] = cot_ref[...].astype(F32) + scale * v - x * (scale * scale * scale * inner)
@@ -806,7 +974,6 @@
     (gow,) = call(
         outgrad_kernel, 1, [(ng, whole_spec(ng)), (cotangent, whole_spec(cotangent))], [(gow, whole_spec(gow))],
         [], 32, 2 * length * width * inner)
-    ggw, gow = lax.psum((ggw, gow), "seq")
 
     gv = shape((length, inner), F32)
     gs = shape((length, maps), F32)
@@ -832,7 +999,7 @@
     gn = shape((length, width), BF16)
     gso = shape((length, maps), BF16)
     gvw = shape((width, inner), BF16)
-    gstepw = shape((2 * HP, width), F32)
+    gstepw = shape((2 * HP, width), BF16)
     gn, gso, gvw, gstepw = call(
         down_kernel, nblk,
         [(gv, rows_spec(gv)), (gs, rows_spec(gs)), (from_next, whole_spec(from_next)), (gstep, whole_spec(gstep)),
@@ -841,41 +1008,40 @@
         [(gn, rows_spec(gn)), (gso, rows_spec(gso)), (gvw, whole_spec(gvw)), (gstepw, whole_spec(gstepw))],
         [pltpu.VMEM((length, inner), BF16)],
         48, 2 * length * width * inner * 3)
-    gn_other, gso_other, out_other = core_swap([gn, gso, out_part], 4)
+    gn_other, gso_other, out_other, convg_other = core_swap([gn, gso, out_part, convg], 4)
 
     gh = shape((length, width), F32)
-    ngain = shape((8, width), F32)
+    tiny = shape((16, both), F32)
     gsw = shape((width, maps), BF16)
     out = shape((length, width), BF16)
-    gh, ngain, gsw, out = call(
+    gh, tiny, gsw, out = call(
         end_kernel, nblk,
         [(gn, rows_spec(gn)), (gn_other, rows_spec(gn_other)), (gso, rows_spec(gso)),
          (gso_other, rows_spec(gso_other)), (hidden_in, rows_spec(hidden_in)), (cotangent, rows_spec(cotangent)),
          (gain_in, whole_spec(gain_in)), (state_proj, whole_spec(state_proj)), (normt, whole_spec(normt)),
-         (out_part, rows_spec(out_part)), (out_other, rows_spec(out_other))],
-        [(gh, rows_spec(gh)), (ngain, whole_spec(ngain)), (gsw, whole_spec(gsw)), (out, rows_spec(out))],
+         (out_part, rows_spec(out_part)), (out_other, rows_spec(out_other)), (small, whole_spec(small)),
+         (hsum, whole_spec(hsum)), (convg, whole_spec(convg)), (convg_other, whole_spec(convg_other))],
+        [(gh, rows_spec(gh)), (tiny, whole_spec(tiny)), (gsw, whole_spec(gsw)), (out, rows_spec(out))],
         [pltpu.VMEM((length, maps), BF16)],
         48, 2 * length * width * maps * 2)
 
-    gvw, gsw, gstepw = lax.psum((gvw, gsw, gstepw), "seq")
-    small, convg, hsum, ngain = lax.psum((small[0:2], convg[0:4], hsum[:, 0:2], ngain[0]), "seq")
-    conv_state_grad = lax.psum(convg[:, inner:], "head")
-    gstepw = gstepw.reshape(2, HP, width)[:, :heads].transpose(0, 2, 1)
-    hsum = hsum.reshape(2, HP, 2)[:, :heads]
+    (ggw, gow, gvw, gsw, gstepw), tiny = reduce_all([ggw, gow, gvw, gsw, gstepw], tiny, count, 5)
+    gstepw = gstepw.astype(F32).reshape(2, HP, width)[:, :heads].transpose(0, 2, 1)
+    hsum = tiny[4:6, : 2 * HP].reshape(2, 2, HP)[:, :, :heads]
     return (
         out,
         gh,
-        ngain,
+        tiny[2, :width],
         ggw.astype(F32),
         gvw.astype(F32),
         gsw.astype(F32),
         gstepw,
-        convg[:, :inner],
-        conv_state_grad,
-        hsum[:, :, 0],
-        hsum[0, :, 1] + hsum[1, :, 1],
-        jnp.sum(small[1].reshape(heads, inner // heads), axis=1),
-        small[0],
+        tiny[8:12, :inner],
+        tiny[8:12, inner:],
+        hsum[0],
+        hsum[1, 0] + hsum[1, 1],
+        jnp.sum(tiny[1, :inner].reshape(heads, inner // heads), axis=1),
+        tiny[0, :inner],
         gow.astype(F32),
     )
 

time: 456 us -> 298 us (0.65)
  waiting for transfers between devices: 178 us -> 1.97 us
  Pallas kernels: 145 us -> 251 us
  blocking collectives: 76.3 us -> 0 us
  between operations: 14.3 us -> 0.96 us
    psum x2 -> x0, waiting for transfers between devices: 174 us -> none  [the longest x1 169 us: body(): ggw, gow = lax.psum((ggw, gow), 'seq')]
    pallas_call x0 -> x1, Pallas kernels: none -> 107 us  [reduce_all(): pl.pallas_call(partial(reduce_kernel, count, bits), out_shape=[jax.ShapeD...]
    psum x2 -> x0, blocking collectives: 76.3 us -> none  [the longest x1 73.2 us: body(): lax.psum((small[0:2], convg[0:4], hsum[:, 0:2], ngain[0]), 'seq')]
    unnamed x75 -> x78, local copies, waits for them, and re-layouts: 17.8 us -> 18.8 us
  transfers between devices with their start and end apart: 4 -> 2, of which waited for: 3 -> 1; matrix products, arithmetic and copies ran while one was open for 2% -> 2% of each run, Pallas kernels for 4% -> 0%
where the time goes in v2:
time: 298 us; the launch traced here: 297 us
  Pallas kernels  251 us (84%)
  local copies, waits for them, and re-layouts  28 us (9%)
  other arithmetic  8.69 us (3%)
  starting transfers between devices  6.34 us (2%)
    pallas_call x1, Pallas kernels, reduce_all(): pl.pallas_call(partial(reduce_kernel, count, bits), out_shape=[jax.ShapeD...  107 us
    pallas_call x7, Pallas kernels, call(): pl.pallas_call(kernel, grid=(grid,), in_specs=[s for _, s in ins], out_sp...  106 us
    pallas_call x2, Pallas kernels, swap(): pl.pallas_call(partial(swap_kernel, reach), out_shape=(shape, shape), in_...  30.1 us
    unnamed x78, local copies, waits for them, and re-layouts  18.8 us
    pallas_call x2, Pallas kernels, core_swap(): pl.pallas_call(partial(core_swap_kernel, count), out_shape=tuple((jax.Sha...  7.75 us
  transfers between devices with their start and end apart: 2, of which 1 were waited for; matrix products, arithmetic and copies ran while one was open for 2% of the time, Pallas kernels for 0%

profile of v2, /device:TPU:0, one launch (start us, length us, event | category | flops | bytes accessed | tf_op | source)
XLA Modules:
  0.0 296.7 jit_solution(14665384697208006269)
XLA Ops:
  0.6 0.7 slice.38
  1.4 4.8 %collective-permute-start = (bf16[16,768]{1,0:T(8,128)(2,1)S(1)}, bf16[16,768]{1,0:T(8,128)(2,1)S(1)}, u32[]{:S(2)}, u32[]{:S(2)}) collective-permute-start(bf16[16,768]{1,0:T(8,128)(2,1)S(1)} %slice.38), channel_id=1, source_target_pairs={{0,2},{2,4},{4,6},{6,8},{8,10},{10,12},{12,14},{14,16},{16,18},{18... | collective-permute-start | bytes 73736 | tf_op jit(solution)/shard_map/ppermute | solution.py:905
  6.2 0.7 pad.17
  6.9 0.1 maximum_bitcast_fusion
  7.0 0.7 pad_bitcast_fusion
  7.6 0.7 pad.16
  8.3 0.7 reshape.57.gain_ref
  9.0 0.7 reshape.61.ggain_ref
  9.7 0.1 copy.34.skip_ref
  9.8 0.1 reshape.66.bias_ref
  9.9 0.1 copy.31.dlog_ref
  9.9 0.8 copy.42
  10.8 0.0 copy-start.10
  10.8 1.0 copy-done.10
  11.8 1.3 copy-done.24
  13.0 1.3 copy-done.26
  14.3 0.7 copy-done.30
  15.0 0.7 copy-done.31
  15.7 0.7 copy-done.32
  16.4 16.9 %shard_map.254 = (s32[8]{0:T(128)S(1)}, bf16[768,1024]{1,0:T(8,128)(2,1)S(1)}, f32[1024,768]{1,0:T(8,128)}, bf16[1024,1024]{1,0:T(8,128)(2,1)}, bf16[16,1024]{1,...) custom-call(s32[9]{0:T(128)S(1)} %copy-done.32, ...), custom_call_target="tpu_custom_call" | custom-call | flops 2818572288 | bytes 16936260 | tf_op jit(solution)/shard_map/pallas_call | solution.py:864
  33.3 1.1 copy-done.5
  34.4 14.9 %shard_map.255 = (bf16[4,80,768]{2,1,0:T(8,128)(2,1)S(1)}, bf16[4,80,768]{2,1,0:T(8,128)(2,1)S(1)}) custom-call(bf16[80,768]{1,0:T(8,128)(2,1)S(1)} %get-tuple-element.71.up_ref, bf16[80,768]{1,0:T(8,128)(2,1)S(1)} %get-tuple-element.72.down_ref), custom_call_target="tpu_custom_call" | custom-call | tf_op jit(solution)/shard_map/pallas_call | solution.py:270
  49.4 17.4 %shard_map.256 = (f32[1024,768]{1,0:T(8,128)}, bf16[8,128,768]{2,1,0:T(8,128)(2,1)S(1)}, f32[8,1024]{1,0:T(8,128)S(1)}) custom-call(s32[8]{0:T(128)S(1)} %get-tuple-element.65.meta_ref, bf16[1024,1024]{1,0:T(8,128)(2,1)} %get-tuple-element.66.act_ref, f32[32,1024]{1,0:T(8,128)S(1)} %get-tuple-element.67.step_ref, f32[32,1]{1,0:T(8,128)S(1)} %reshape.66.bias_ref, ...), custom_call_target="tpu_custom_call" | custom-call | flops 2415919104 | bytes 17059168 | tf_op jit(solution)/shard_map/pallas_call | solution.py:864
  66.8 1.1 copy-done.23
  68.0 1.2 shard_map.257.other_ref
  69.2 16.5 %shard_map.258 = (bf16[1024,768]{1,0:T(8,128)(2,1)S(1)}, bf16[1024,768]{1,0:T(8,128)(2,1)S(1)}, f32[1024,768]{1,0:T(8,128)}, f32[8,128,768]{2,1,0:T(8,128)}, bf1...) custom-call(s32[8]{0:T(128)S(1)} %get-tuple-element.65.meta_ref, ...), custom_call_target="tpu_custom_call" | custom-call | flops 4831838208 | bytes 25423136 | tf_op jit(solution)/shard_map/pallas_call | solution.py:864
  85.7 1.2 copy-done.35
  86.9 15.2 %shard_map.259 = (bf16[4,80,768]{2,1,0:T(8,128)(2,1)S(1)}, bf16[4,80,768]{2,1,0:T(8,128)(2,1)S(1)}) custom-call(bf16[80,768]{1,0:T(8,128)(2,1)S(1)} %get-tuple-element.81.up_ref, bf16[80,768]{1,0:T(8,128)(2,1)S(1)} %get-tuple-element.82.down_ref), custom_call_target="tpu_custom_call" | custom-call | tf_op jit(solution)/shard_map/pallas_call | solution.py:270
  102.1 0.0 copy-start.28
  102.1 0.8 copy-done.28
  102.9 0.8 copy-done.29
  103.7 36.4 %shard_map.260 = (f32[1024,768]{1,0:T(8,128)}, f32[1024,256]{1,0:T(8,128)}, bf16[32,1024]{1,0:T(8,128)(2,1)}, f32[8,1024]{1,0:T(8,128)}, f32[8,1024]{1,0:T(8,128)}, /*index=5*/f32[32,128]{1,0:T(8,128)}) custom-call(s32[8]{0:T(128)} %copy-done.22, bf16[1024,1024]{1,0:T(8,128)(2,1)} %get-tuple-element.66.act_ref, f32[32,1024]{1,0:T(8,128)} %copy-done.13, ...), custom_call_target="tpu_custom_call" | custom-call | flops 4831838208 | bytes 19710304 | tf_op jit(solution)/shard_map/pallas_call | solution.py:864
  140.1 1.5 collective-permute-start.1
  141.6 0.0 copy-start.25
  141.6 0.0 copy-start.27
  141.7 0.0 copy-start.36
  141.7 1.4 shard_map.264.refs_1_
  143.1 1.0 copy-done.8
  144.1 2.0 collective-permute-done.1.next_ref
  146.1 8.8 %shard_map.261 = (bf16[1024,768]{1,0:T(8,128)(2,1)}, bf16[1024,256]{1,0:T(8,128)(2,1)S(1)}, bf16[768,768]{1,0:T(8,128)(2,1)S(1)}, bf16[32,768]{1,0:T(8,128)(2,1)S(1)}) custom-call(f32[1024,768]{1,0:T(8,128)} %get-tuple-element.87.gv_ref, f32[1024,256]{1,0:T(8,128)S(1)} %copy-done.34, f32[8,1024]{1,0:T(8,128)S(1)} %collective-permute-done.1.next_ref, ...), custom_call_target="tpu_custom_call" | custom-call | flops 3623878656 | bytes 13172736 | tf_op jit(solution)/shard_map/pallas_call | solution.py:864
  155.0 1.0 copy-done.9
  156.0 1.4 copy-done.3
  157.4 6.5 %shard_map.262 = (bf16[1024,768]{1,0:T(8,128)(2,1)S(1)}, bf16[1024,256]{1,0:T(8,128)(2,1)S(1)}, bf16[1024,768]{1,0:T(8,128)(2,1)S(1)}, f32[8,1024]{1,0:T(8,128)S(1)}) custom-call(bf16[1024,768]{1,0:T(8,128)(2,1)S(1)} %copy-done.3, bf16[1024,256]{1,0:T(8,128)(2,1)S(1)} %get-tuple-element.93.refs_1_.smine_ref, ...), custom_call_target="tpu_custom_call" | custom-call | tf_op jit(solution)/shard_map/pallas_call | solution.py:303
  164.0 1.1 copy-done.6
  165.1 8.1 %shard_map.263 = (f32[1024,768]{1,0:T(8,128)}, f32[16,1024]{1,0:T(8,128)S(1)}, bf16[768,256]{1,0:T(8,128)(2,1)S(1)}, bf16[1024,768]{1,0:T(8,128)(2,1)}) custom-call(bf16[1024,768]{1,0:T(8,128)(2,1)S(1)} %copy-done.4, bf16[1024,768]{1,0:T(8,128)(2,1)S(1)} %get-tuple-element.96.other_ref, bf16[1024,256]{1,0:T(8,128)(2,1)S(1)} %get-tuple-element.93.refs_1_.smine_ref, ...), custom_call_target="tpu_custom_call" | custom-call | flops 805306368 | bytes 17738752 | tf_op jit(solution)/shard_map/pallas_call | solution.py:864
  173.3 107.3 %shard_map.265 = (bf16[768,768]{1,0:T(8,128)(2,1)S(1)}, bf16[768,768]{1,0:T(8,128)(2,1)S(1)}, bf16[768,768]{1,0:T(8,128)(2,1)S(1)}, bf16[768,256]{1,0:T(8,128)(2...) custom-call(bf16[768,768]{1,0:T(8,128)(2,1)S(1)} %get-tuple-element.104.refs_0_, ...), custom_call_target="tpu_custom_call" | custom-call | tf_op jit(solution)/shard_map/pallas_call | solution.py:460
  280.5 0.0 copy-start.12
  280.6 0.7 copy-done.12
  281.3 0.6 copy-done.18
  281.9 0.6 copy-done.21
  282.5 0.1 reshape.65
  282.6 0.5 fusion
  283.1 0.6 slice_bitcast_fusion
  283.7 1.3 slice.42
  285.0 1.3 slice.41
  286.3 1.5 slice_reduce_fusion
  287.8 0.1 reshape_squeeze.3
  287.9 0.6 reduce_sum.9
  288.5 0.8 slice_convert_fusion
  289.3 0.7 copy.45
  290.0 1.9 convert_element_type.22
  291.9 1.6 convert_element_type.20
  293.5 1.6 convert_element_type.21
  295.1 1.6 convert_element_type.23
  (55 shorter events, 0.1 us)
Async XLA Ops:
  1.4 9.4 %collective-permute-start = (bf16[16,768]{1,0:T(8,128)(2,1)S(1)}, bf16[16,768]{1,0:T(8,128)(2,1)S(1)}, u32[]{:S(2)}, u32[]{:S(2)}) collective-permute-start(bf16[16,768]{1,0:T(8,128)(2,1)S(1)} %slice.38), channel_id=1, source_target_pairs={{0,2},{2,4},{4,6},{6,8},{8,10},{10,12},{12,14},{14,16},{16,18},{18... | collective-permute-start | bytes 73736 | tf_op jit(solution)/shard_map/ppermute | solution.py:905
  9.8 39.6 %copy-start.19 = (f32[16,1]{1,0:T(8,128)}, f32[16,1]{1,0:T(8,128)S(1)}, u32[]{:S(2)}) copy-start(f32[16,1]{1,0:T(8,128)S(1)} %copy.34.skip_ref) | copy-start | bytes 196
  9.9 59.3 %copy-start.15 = (f32[32,1]{1,0:T(8,128)}, f32[32,1]{1,0:T(8,128)S(1)}, u32[]{:S(2)}) copy-start(f32[32,1]{1,0:T(8,128)S(1)} %reshape.66.bias_ref) | copy-start | bytes 388
  9.9 59.3 %copy-start.16 = (f32[32,1]{1,0:T(8,128)}, f32[32,1]{1,0:T(8,128)S(1)}, u32[]{:S(2)}) copy-start(f32[32,1]{1,0:T(8,128)S(1)} %copy.31.dlog_ref) | copy-start | bytes 388
  10.8 1.0 copy-start.10
  11.8 1.3 copy-start.24
  13.0 1.3 copy-start.26
  14.3 0.7 copy-start.30
  15.0 0.7 copy-start.31
  15.7 0.7 copy-start.32
  16.4 33.0 %copy-start = (bf16[1024,768]{1,0:T(8,128)(2,1)S(1)}, bf16[1024,768]{1,0:T(8,128)(2,1)}, u32[]{:S(2)}) copy-start(bf16[1024,768]{1,0:T(8,128)(2,1)} %cot_ref.7) | copy-start | bytes 4718596
  16.4 33.0 %copy-start.7 = (bf16[768,768]{1,0:T(8,128)(2,1)S(1)}, bf16[768,768]{1,0:T(8,128)(2,1)}, u32[]{:S(2)}) copy-start(bf16[768,768]{1,0:T(8,128)(2,1)} %wo_ref.3) | copy-start | bytes 3538948
  33.3 1.1 copy-start.5
  34.4 32.4 %copy-start.37 = (bf16[16,1024]{1,0:T(8,128)(2,1)}, bf16[16,1024]{1,0:T(8,128)(2,1)S(1)}, u32[]{:S(2)}) copy-start(bf16[16,1024]{1,0:T(8,128)(2,1)S(1)} %get-tuple-element.86.jhalo_ref) | copy-start | bytes 98308
  34.4 34.8 %copy-start.13 = (f32[32,1024]{1,0:T(8,128)}, f32[32,1024]{1,0:T(8,128)S(1)}, u32[]{:S(2)}) copy-start(f32[32,1024]{1,0:T(8,128)S(1)} %get-tuple-element.67.step_ref) | copy-start | bytes 393220
  34.4 34.8 %copy-start.17 = (f32[8,2,768]{2,1,0:T(2,128)}, f32[8,2,768]{2,1,0:T(2,128)S(1)}, u32[]{:S(2)}) copy-start(f32[8,2,768]{2,1,0:T(2,128)S(1)} %get-tuple-element.70.pexp_ref) | copy-start | bytes 147460
  34.4 34.8 %copy-start.22 = (s32[8]{0:T(128)}, s32[8]{0:T(128)S(1)}, u32[]{:S(2)}) copy-start(s32[8]{0:T(128)S(1)} %get-tuple-element.65.meta_ref) | copy-start | bytes 100
  66.8 1.1 copy-start.23
  85.7 1.2 copy-start.35
  86.9 69.1 %copy-start.2 = (bf16[1024,768]{1,0:T(8,128)(2,1)}, bf16[1024,768]{1,0:T(8,128)(2,1)S(1)}, u32[]{:S(2)}) copy-start(bf16[1024,768]{1,0:T(8,128)(2,1)S(1)} %get-tuple-element.94.refs_2_.omine_ref) | copy-start | bytes 4718596
  102.1 0.8 copy-start.28
  102.9 0.8 copy-start.29
  103.7 37.9 %copy-start.1 = (bf16[1024,768]{1,0:T(8,128)(2,1)S(1)}, bf16[1024,768]{1,0:T(8,128)(2,1)}, u32[]{:S(2)}) copy-start(bf16[1024,768]{1,0:T(8,128)(2,1)} %cot_ref.7) | copy-start | bytes 4718596
  103.7 37.9 %copy-start.33 = (bf16[4,256,768]{2,1,0:T(8,128)(2,1)S(1)}, bf16[4,256,768]{2,1,0:T(8,128)(2,1)}, u32[]{:S(2)}) copy-start(bf16[4,256,768]{2,1,0:T(8,128)(2,1)} %get-tuple-element.105) | copy-start | bytes 4718596
  140.1 6.0 %collective-permute-start.1 = (f32[8,1024]{1,0:T(8,128)}, f32[8,1024]{1,0:T(8,128)S(1)}, u32[]{:S(2)}, u32[]{:S(2)}) collective-permute-start(f32[8,1024]{1,0:T(8,128)} %get-tuple-element.89), channel_id=1, source_target_pairs={{2,0},{4,2},{6,4},{8,6},{10,8},{12,10},{14,12},{16,14},{18,16},{20... | collective-permute-start | bytes 98312 | tf_op jit(solution)/shard_map/ppermute | solution.py:997
  141.6 4.5 %copy-start.25 = (bf16[768,768]{1,0:T(8,128)(2,1)S(1)}, bf16[768,768]{1,0:T(8,128)(2,1)}, u32[]{:S(2)}) copy-start(bf16[768,768]{1,0:T(8,128)(2,1)} %wg_ref.3) | copy-start | bytes 3538948
  141.6 4.5 %copy-start.27 = (bf16[768,768]{1,0:T(8,128)(2,1)S(1)}, bf16[768,768]{1,0:T(8,128)(2,1)}, u32[]{:S(2)}) copy-start(bf16[768,768]{1,0:T(8,128)(2,1)} %wv_ref.3) | copy-start | bytes 3538948
  141.6 4.5 %copy-start.34 = (f32[1024,256]{1,0:T(8,128)S(1)}, f32[1024,256]{1,0:T(8,128)}, u32[]{:S(2)}) copy-start(f32[1024,256]{1,0:T(8,128)} %get-tuple-element.88.gs_ref) | copy-start | bytes 3145732
  141.7 4.5 %copy-start.36 = (bf16[32,1024]{1,0:T(8,128)(2,1)S(1)}, bf16[32,1024]{1,0:T(8,128)(2,1)}, u32[]{:S(2)}) copy-start(bf16[32,1024]{1,0:T(8,128)(2,1)} %get-tuple-element.90.gstep_ref) | copy-start | bytes 196612
  143.1 1.0 copy-start.8
  146.1 9.9 %copy-start.14 = (f32[8,1024]{1,0:T(8,128)S(1)}, f32[8,1024]{1,0:T(8,128)}, u32[]{:S(2)}) copy-start(f32[8,1024]{1,0:T(8,128)} %get-tuple-element.95.refs_3_.cmine_ref) | copy-start | bytes 98308
  155.0 1.0 copy-start.9
  156.0 1.4 copy-start.3
  157.4 7.7 %copy-start.4 = (bf16[1024,768]{1,0:T(8,128)(2,1)S(1)}, bf16[1024,768]{1,0:T(8,128)(2,1)}, u32[]{:S(2)}) copy-start(bf16[1024,768]{1,0:T(8,128)(2,1)} %get-tuple-element.92.refs_0_.mine_ref) | copy-start | bytes 4718596
  157.4 7.7 %copy-start.11 = (bf16[768,256]{1,0:T(8,128)(2,1)S(1)}, bf16[768,256]{1,0:T(8,128)(2,1)}, u32[]{:S(2)}) copy-start(bf16[768,256]{1,0:T(8,128)(2,1)} %ws_ref.3) | copy-start | bytes 1179652
  157.4 7.7 %copy-start.20 = (f32[32,128]{1,0:T(8,128)S(1)}, f32[32,128]{1,0:T(8,128)}, u32[]{:S(2)}) copy-start(f32[32,128]{1,0:T(8,128)} %get-tuple-element.100.hsum_ref) | copy-start | bytes 49156
  164.0 1.1 copy-start.6
  280.5 0.7 copy-start.12
  281.3 0.6 copy-start.18
  281.9 0.6 copy-start.21

commit v3 on v2

--- a/solution.py
+++ b/solution.py
@@ -208,74 +208,69 @@
         put_message(msgr_ref, sumr[...], prod[1:2, :] * meta_ref[3].astype(F32))
 
 
-def swap_kernel(reach, up_ref, down_ref, from_low, from_high, up_send, up_recv, down_send, down_recv):
-    me = lax.axis_index("seq")
-    core = lax.axis_index("head")
-    count = lax.axis_size("seq")
-    barrier = pltpu.get_barrier_semaphore()
-    for k in range(1, reach + 1):
-        @pl.when(me + k < count)
-        def _():
-            pl.semaphore_signal(barrier, inc=1, device_id=(me + k, core), device_id_type=MESH)
-
-        @pl.when(me >= k)
-        def _():
-            pl.semaphore_signal(barrier, inc=1, device_id=(me - k, core), device_id_type=MESH)
-
-    pl.semaphore_wait(barrier, jnp.minimum(me, reach) + jnp.minimum(count - 1 - me, reach))
-
-    def up(k):
+class Swap:
+    def __init__(self, reach, up_ref, down_ref, from_low, from_high, up_send, up_recv, down_send, down_recv):
+        self.me, self.core, self.count = lax.axis_index("seq"), lax.axis_index("head"), lax.axis_size("seq")
+        self.reach, self.up_ref, self.down_ref, self.from_low, self.from_high = reach, up_ref, down_ref, from_low, from_high
+        self.sems = up_send, up_recv, down_send, down_recv
+
+    def up(self, k):
         return pltpu.make_async_remote_copy(
-            src_ref=up_ref, dst_ref=from_low.at[k - 1], send_sem=up_send.at[k - 1], recv_sem=up_recv.at[k - 1],
-            device_id=(me + k, core), device_id_type=MESH)
-
-    def down(k):
+            src_ref=self.up_ref, dst_ref=self.from_low.at[k - 1], send_sem=self.sems[0].at[k - 1],
+            recv_sem=self.sems[1].at[k - 1], device_id=(self.me + k, self.core), device_id_type=MESH)
+
+    def down(self, k):
         return pltpu.make_async_remote_copy(
-            src_ref=down_ref, dst_ref=from_high.at[k - 1], send_sem=down_send.at[k - 1],
-            recv_sem=down_recv.at[k - 1], device_id=(me - k, core), device_id_type=MESH)
-
-    for k in range(1, reach + 1):
-        @pl.when(me + k < count)
-        def _():
-            up(k).start()
-
-        @pl.when(me >= k)
-        def _():
-            down(k).start()
-
-    for k in range(1, reach + 1):
-        @pl.when(me < k)
-        def _():
-            from_low[k - 1] = jnp.zeros_like(from_low[k - 1])
-
-        @pl.when(me + k >= count)
-        def _():
-            from_high[k - 1] = jnp.zeros_like(from_high[k - 1])
-
-    for k in range(1, reach + 1):
-        @pl.when(me + k < count)
-        def _():
-            up(k).wait_send()
-            down(k).wait_recv()
-
-        @pl.when(me >= k)
-        def _():
-            down(k).wait_send()
-            up(k).wait_recv()
-
-
-def swap(up, down, reach, ident):
-    shape = jax.ShapeDtypeStruct((reach,) + up.shape, up.dtype)
-    vm = pl.BlockSpec(memory_space=pltpu.VMEM)
-    return pl.pallas_call(
-        partial(swap_kernel, reach),
-        out_shape=(shape, shape),
-        in_specs=[vm, vm],
-        out_specs=(vm, vm),
-        scratch_shapes=[pltpu.SemaphoreType.DMA((reach,))] * 4,
-        compiler_params=pltpu.CompilerParams(
-            collective_id=ident, has_side_effects=True, vmem_limit_bytes=16 * MIB),
-    )(up, down)
+            src_ref=self.down_ref, dst_ref=self.from_high.at[k - 1], send_sem=self.sems[2].at[k - 1],
+            recv_sem=self.sems[3].at[k - 1], device_id=(self.me - k, self.core), device_id_type=MESH)
+
+    def greet(self, barrier):
+        me, core, count = self.me, self.core, self.count
+        for k in range(1, self.reach + 1):
+            @pl.when(me + k < count)
+            def _():
+                pl.semaphore_signal(barrier, inc=1, device_id=(me + k, core), device_id_type=MESH)
+
+            @pl.when(me >= k)
+            def _():
+                pl.semaphore_signal(barrier, inc=1, device_id=(me - k, core), device_id_type=MESH)
+        return jnp.minimum(me, self.reach) + jnp.minimum(count - 1 - me, self.reach)
+
+    def start(self):
+        me, count = self.me, self.count
+        for k in range(1, self.reach + 1):
+            @pl.when(me + k < count)
+            def _():
+                self.up(k).start()
+
+            @pl.when(me >= k)
+            def _():
+                self.down(k).start()
+
+            @pl.when(me < k)
+            def _():
+                self.from_low[k - 1] = jnp.zeros_like(self.from_low[k - 1])
+
+            @pl.when(me + k >= count)
+            def _():
+                self.from_high[k - 1] = jnp.zeros_like(self.from_high[k - 1])
+
+    def finish(self):
+        me, count = self.me, self.count
+        for k in range(1, self.reach + 1):
+            @pl.when(me + k < count)
+            def _():
+                self.up(k).wait_send()
+                self.down(k).wait_recv()
+
+            @pl.when(me >= k)
+            def _():
+                self.down(k).wait_send()
+                self.up(k).wait_recv()
+
+
+def swap_scratch(reach, inner):
+    return [pltpu.VMEM((reach, 80, inner), BF16)] * 2 + [pltpu.SemaphoreType.DMA((reach,))] * 4
 
 
 def core_swap_kernel(count, *refs):
@@ -487,18 +482,72 @@
     return jnp.concatenate([jnp.where(left, x, zero), jnp.where(left, zero, x)], axis=0)
 
 
-def mix_kernel(meta_ref, act_ref, step_ref, bias_ref, dlog_ref, gate_ref, cot_ref, wo_ref, ggain_ref, skip_ref,
-               inc_ref, pexp_ref, low_ref, high_ref,
-               mixed_ref, state_ref, sums_ref):
-    blk = pl.program_id(0)
+def mix_kernel(reach, meta_ref, act_ref, step_ref, bias_ref, dlog_ref, gate_ref, cot_ref, wo_ref, ggain_ref, skip_ref,
+               inc_ref, pexp_ref, msgf_ref, msgr_ref, normt_ref,
+               state_ref, out_ref, ggate_ref, dy_ref, dhy_ref, gmsgf_ref, gmsgr_ref, small_ref, ggw_ref, gow_ref,
+               mixed_ref, ngt, mine, other, gsum_f, gsum_r, prod, s_send, s_recv,
+               from_low, from_high, up_send, up_recv, down_send, down_recv):
+    turn = pl.program_id(0)
+    nblk = pl.num_programs(0) // 3
+    blk = lax.rem(turn, nblk)
     inner = wo_ref.shape[0]
+    whole = inner * 2
     nchunk = inc_ref.shape[0]
     b = meta_ref[0]
-
-    @pl.when(blk == 0)
-    def _():
-        hf = chain(low_ref) * meta_ref[2].astype(F32)
-        hr = chain(high_ref) * meta_ref[3].astype(F32)
+    swap = Swap(reach, msgf_ref, msgr_ref, from_low, from_high, up_send, up_recv, down_send, down_recv)
+    me, partner = lax.axis_index("seq"), 1 - lax.axis_index("head")
+    place = pl.ds(pl.multiple_of(blk * TB, TB), TB)
+
+    def sums_copy(k):
+        return pltpu.make_async_remote_copy(
+            src_ref=mine.at[k], dst_ref=other.at[k], send_sem=s_send.at[k], recv_sem=s_recv.at[k],
+            device_id=(me, partner), device_id_type=MESH)
+
+    @pl.when(turn == 0)
+    def _():
+        barrier = pltpu.get_barrier_semaphore()
+        near = swap.greet(barrier)
+        pl.semaphore_signal(barrier, inc=1, device_id=(me, partner), device_id_type=MESH)
+        pl.semaphore_wait(barrier, near + 1)
+        swap.start()
+        gsum_f[...] = jnp.zeros_like(gsum_f)
+        gsum_r[...] = jnp.zeros_like(gsum_r)
+        prod[...] = jnp.ones_like(prod)
+        small_ref[...] = jnp.zeros_like(small_ref)
+
+    spread = spread_matrix(inner, 64)
+    spread2 = jnp.concatenate([spread, spread], axis=0).astype(BF16)
+
+    @pl.when(turn < nblk)
+    def _():
+        skip = widen_col(skip_ref[...], spread)
+        lower = iota((Q, Q), 0) > iota((Q, Q), 1)
+        for q in range(TB // Q):
+            rows = slice(q * Q, (q + 1) * Q)
+            dest = pl.ds(pl.multiple_of(blk * TB + q * Q, Q), Q)
+            t0 = blk * TB + q * Q
+            dt, ld, run, bef = step_parts(step_ref[:, rows], bias_ref[...], dlog_ref[...])
+            ldt = jnp.log(jnp.maximum(dt, 1e-37))
+            rowf = ldt[:HP] - run[:HP]
+            rowr = ldt[HP:] + bef[HP:]
+            cols = jnp.concatenate([bef[:HP], -run[HP:]], axis=0).T
+            scores = chunk_scores(act_ref[rows, inner:], t0, b)
+            for j in range(inner // 128):
+                lanes = slice(j * 128, (j + 1) * 128)
+                weights = []
+                for h in (2 * j, 2 * j + 1):
+                    e = jnp.where(lower, cols[:, h : h + 1] + rowf[h : h + 1],
+                                  cols[:, HP + h : HP + h + 1] + rowr[h : h + 1])
+                    weights.append((jnp.exp(jnp.minimum(e, 60.0)) * scores).astype(BF16))
+                vp = act_ref[rows, lanes]
+                y = nn(jnp.concatenate(weights, axis=1), halves(vp))
+                mixed_ref[dest, lanes] = y + skip[:, lanes] * vp.astype(F32)
+
+    @pl.when(turn == nblk)
+    def _():
+        swap.finish()
+        hf = chain(from_low) * meta_ref[2].astype(F32)
+        hr = chain(from_high) * meta_ref[3].astype(F32)
         for c in range(nchunk):
             state_ref[c, 0:64, :] = hf.astype(BF16)
             hf = pexp_ref[c, 0:1, :] * hf + inc_ref[c, 0:64, :]
@@ -506,273 +555,262 @@
             state_ref[d, 64:128, :] = hr.astype(BF16)
             hr = pexp_ref[d, 1:2, :] * hr + inc_ref[d, 64:128, :]
 
-    spread = spread_matrix(inner, 64)
-    spread2 = jnp.concatenate([spread, spread], axis=0).astype(BF16)
-    skip = widen_col(skip_ref[...], spread)
-    lower = iota((Q, Q), 0) > iota((Q, Q), 1)
-    u_all = nt(cot_ref[...], wo_ref[...])
-    lane = iota((Q, 128), 1)
-    for q in range(TB // Q):
-        rows = slice(q * Q, (q + 1) * Q)
-        t0 = blk * TB + q * Q
-        chunk = blk * (TB // Q) + q
-        dt, ld, run, bef = step_parts(step_ref[:, rows], bias_ref[...], dlog_ref[...])
-        ef, er, _, _ = state_factors(dt, run, bef, t0, b)
-        ldt = jnp.log(jnp.maximum(dt, 1e-37))
-        rowf = ldt[:HP] - run[:HP]
-        rowr = ldt[HP:] + bef[HP:]
-        cols = jnp.concatenate([bef[:HP], -run[HP:]], axis=0).T
-        maps = act_ref[rows, inner:]
-        scores = chunk_scores(maps, t0, b)
-        efe, ere = widen(ef, spread2), widen(er, spread2)
-        state = state_ref[chunk]
-        ys = nn(maps[:, 64:128], state[0:64]) * efe + nn(maps[:, 192:256], state[64:128]) * ere
-        square = jnp.zeros((Q, 1), F32)
-        cross = jnp.zeros((Q, 1), F32)
+    @pl.when((turn >= nblk) & (turn < 2 * nblk))
+    def _():
+        lane = iota((Q, 128), 1)
+        u_all = nt(cot_ref[place, :], wo_ref[...])
+        for q in range(TB // Q):
+            rows = slice(q * Q, (q + 1) * Q)
+            dest = pl.ds(pl.multiple_of(blk * TB + q * Q, Q), Q)
+            t0 = blk * TB + q * Q
+            dt, ld, run, bef = step_parts(step_ref[:, rows], bias_ref[...], dlog_ref[...])
+            ef, er, _, _ = state_factors(dt, run, bef, t0, b)
+            maps = act_ref[rows, inner:]
+            state = state_ref[blk * (TB // Q) + q]
+            ys = nn(maps[:, 64:128], state[0:64]) * widen(ef, spread2)
+            ys = ys + nn(maps[:, 192:256], state[64:128]) * widen(er, spread2)
+            square = jnp.zeros((Q, 1), F32)
+            cross = jnp.zeros((Q, 1), F32)
+            for j in range(inner // 128):
+                lanes = slice(j * 128, (j + 1) * 128)
+                y = mixed_ref[dest, lanes] + ys[:, lanes]
+                mixed_ref[dest, lanes] = y
+                gated = y * silu(gate_ref[rows, lanes])
+                square = square + jnp.sum(gated * gated, axis=1, keepdims=True)
+                cross = cross + jnp.sum(gated * (u_all[rows, lanes] * ggain_ref[:, lanes]), axis=1, keepdims=True)
+            both = jnp.where(lane == 0, square, jnp.where(lane == 1, cross, 0.0))
+            mine[blk, :, rows] = both.T[0:8]
+        sums_copy(blk).start()
+
+    @pl.when(turn >= 2 * nblk)
+    def _():
+        sums_copy(blk).wait()
+        sums = mine[blk] + other[blk]
+        sums = jnp.concatenate([sums, jnp.zeros((120, TB), F32)], axis=0).T
+        scale = lax.rsqrt(sums[:, 0:1] / whole + EPSILON)
+        back = scale * scale * scale * sums[:, 1:2] / whole
+        gng = nt(cot_ref[place, :], wo_ref[...])
         for j in range(inner // 128):
             lanes = slice(j * 128, (j + 1) * 128)
-            weights = []
-            for h in (2 * j, 2 * j + 1):
-                e = jnp.where(lower, cols[:, h : h + 1] + rowf[h : h + 1],
-                              cols[:, HP + h : HP + h + 1] + rowr[h : h + 1])
-                weights.append((jnp.exp(jnp.minimum(e, 60.0)) * scores).astype(BF16))
-            vp = act_ref[rows, lanes]
-            y = nn(jnp.concatenate(weights, axis=1), halves(vp))
-            y = y + ys[:, lanes] + skip[:, lanes] * vp.astype(F32)
-            mixed_ref[rows, lanes] = y
-            gated = y * silu(gate_ref[rows, lanes])
-            square = square + jnp.sum(gated * gated, axis=1, keepdims=True)
-            cross = cross + jnp.sum(gated * (u_all[rows, lanes] * ggain_ref[:, lanes]), axis=1, keepdims=True)
-        both = jnp.where(lane == 0, square, jnp.where(lane == 1, cross, 0.0))
-        sums_ref[:, rows] = both.T[0:8]
-
-
-def gate_kernel(meta_ref, mine_ref, other_ref, mixed_ref, gate_ref, cot_ref, wo_ref, ggain_ref, act_ref, step_ref,
-                bias_ref, dlog_ref, pexp_ref, normt_ref,
-                out_ref, ggate_ref, dy_ref, dhy_ref, msgf_ref, msgr_ref, small_ref, ggw_ref, ngt,
-                gsum_f, gsum_r, prod):
-    blk = pl.program_id(0)
-    nblk = pl.num_programs(0)
-    inner = wo_ref.shape[0]
-    whole = inner * 2
-    b = meta_ref[0]
-
-    @pl.when(blk == 0)
-    def _():
-        gsum_f[...] = jnp.zeros_like(gsum_f)
-        gsum_r[...] = jnp.zeros_like(gsum_r)
-        prod[...] = jnp.ones_like(prod)
-        small_ref[...] = jnp.zeros_like(small_ref)
-
-    sums = mine_ref[...] + other_ref[...]
-    sums = jnp.concatenate([sums, jnp.zeros((120, TB), F32)], axis=0).T
-    scale = lax.rsqrt(sums[:, 0:1] / whole + EPSILON)
-    back = scale * scale * scale * sums[:, 1:2] / whole
-    gng = nt(cot_ref[...], wo_ref[...])
-    for j in range(inner // 128):
-        lanes = slice(j * 128, (j + 1) * 128)
-        mixed = mixed_ref[:, lanes]
-        pre = gate_ref[:, lanes]
-        sig = jax.nn.sigmoid(pre)
-        gated = mixed * (pre * sig)
-        ng = gated * scale
-        gain = ggain_ref[:, lanes]
-        ng_low = (ng * gain).astype(BF16)
-        ngt[blk, :, lanes] = ng_low
-        g = gng[:, lanes]
-        small_ref[0:1, lanes] += jnp.sum(g * ng, axis=0, keepdims=True)
-        grad_gated = scale * (g * gain) - gated * back
-        dy = grad_gated * (pre * sig)
-        small_ref[1:2, lanes] += jnp.sum(dy * act_ref[:, lanes].astype(F32), axis=0, keepdims=True)
-        dy_ref[:, lanes] = dy
-        ggate_ref[pl.ds(blk * TB, TB), lanes] = (
-            grad_gated * mixed * (sig * (1.0 + pre * (1.0 - sig)))).astype(BF16)
-    out_ref[...] = nn(ngt[blk], wo_ref[...]).astype(BF16)
-    spread = spread_matrix(inner, 64)
-    spread2 = jnp.concatenate([spread, spread], axis=0).astype(BF16)
-    for q in range(TB // Q):
-        rows = slice(q * Q, (q + 1) * Q)
-        t0 = blk * TB + q * Q
-        chunk = blk * (TB // Q) + q
-        dt, ld, run, bef = step_parts(step_ref[:, rows], bias_ref[...], dlog_ref[...])
-        ef, er, _, _ = state_factors(dt, run, bef, t0, b)
-        maps_t = act_ref[rows, inner:].astype(F32).T.astype(BF16)
-        dy = dy_ref[rows, :]
-        df = nn(maps_t[64:128], (dy * widen(ef, spread2)).astype(BF16))
-        dr = nn(maps_t[192:256], (dy * widen(er, spread2)).astype(BF16))
-        dhy_ref[q, 0:64, :] = df
-        dhy_ref[q, 64:128, :] = dr
-        pf, pr = pexp_ref[chunk, 0:1, :], pexp_ref[chunk, 1:2, :]
-        gsum_f[...] = gsum_f[...] + prod[0:1, :] * df
-        gsum_r[...] = pr * gsum_r[...] + dr
-        prod[0:1, :] = prod[0:1, :] * pf
-        prod[1:2, :] = prod[1:2, :] * pr
-
-    @pl.when(blk == nblk - 1)
+            mixed = mixed_ref[place, lanes]
+            pre = gate_ref[:, lanes]
+            sig = jax.nn.sigmoid(pre)
+            gated = mixed * (pre * sig)
+            ng = gated * scale
+            gain = ggain_ref[:, lanes]
+            ngt[place, lanes] = (ng * gain).astype(BF16)
+            g = gng[:, lanes]
+            small_ref[0:1, lanes] += jnp.sum(g * ng, axis=0, keepdims=True)
+            grad_gated = scale * (g * gain) - gated * back
+            dy = grad_gated * (pre * sig)
+            small_ref[1:2, lanes] += jnp.sum(dy * act_ref[:, lanes].astype(F32), axis=0, keepdims=True)
+            dy_ref[:, lanes] = dy
+            ggate_ref[place, lanes] = (grad_gated * mixed * (sig * (1.0 + pre * (1.0 - sig)))).astype(BF16)
+        out_ref[...] = nn(ngt[place, :], wo_ref[...]).astype(BF16)
+        for q in range(TB // Q):
+            rows = slice(q * Q, (q + 1) * Q)
+            t0 = blk * TB + q * Q
+            chunk = blk * (TB // Q) + q
+            dt, ld, run, bef = step_parts(step_ref[:, rows], bias_ref[...], dlog_ref[...])
+            ef, er, _, _ = state_factors(dt, run, bef, t0, b)
+            maps_t = act_ref[rows, inner:].astype(F32).T.astype(BF16)
+            dy = dy_ref[rows, :]
+            df = nn(maps_t[64:128], (dy * widen(ef, spread2)).astype(BF16))
+            dr = nn(maps_t[192:256], (dy * widen(er, spread2)).astype(BF16))
+            dhy_ref[q, 0:64, :] = df
+            dhy_ref[q, 64:128, :] = dr
+            pf, pr = pexp_ref[chunk, 0:1, :], pexp_ref[chunk, 1:2, :]
+            gsum_f[...] = gsum_f[...] + prod[0:1, :] * df
+            gsum_r[...] = pr * gsum_r[...] + dr
+            prod[0:1, :] = prod[0:1, :] * pf
+            prod[1:2, :] = prod[1:2, :] * pr
+
+    @pl.when(turn == 3 * nblk - 1)
     def _():
         before = meta_ref[2].astype(F32)
         after = meta_ref[3].astype(F32)
-        put_message(msgf_ref, gsum_f[...] * before, prod[0:1, :] * before)
-        put_message(msgr_ref, gsum_r[...] * after, prod[1:2, :] * after)
+        put_message(gmsgf_ref, gsum_f[...] * before, prod[0:1, :] * before)
+        put_message(gmsgr_ref, gsum_r[...] * after, prod[1:2, :] * after)
         ggw_ref[...] = nn(normt_ref[...], ggate_ref[...]).astype(BF16)
-
-
-def outgrad_kernel(ng_ref, cot_ref, gow_ref):
-    gow_ref[...] = tn(ng_ref[...], cot_ref[...]).astype(BF16)
-
-
-def back_kernel(meta_ref, act_ref, step_ref, bias_ref, dlog_ref, dy_ref, skip_ref, state_ref, dhy_ref, pexp_ref,
-                low_ref, high_ref, joined_ref, jprev_ref, jhalo_ref, tapv_ref, taps_ref,
+        gow_ref[...] = tn(ngt[...], cot_ref[...]).astype(BF16)
+
+
+def back_kernel(reach, meta_ref, act_ref, step_ref, bias_ref, dlog_ref, dy_ref, skip_ref, state_ref, dhy_ref, pexp_ref,
+                msgf_ref, msgr_ref, joined_ref, jprev_ref, jhalo_ref, tapv_ref, taps_ref,
                 gv_ref, gs_ref, gstep_ref, lent_ref, convg_ref, heads_ref,
-                dstate, ext, jext, rowbuf, dact):
-    step_no = pl.program_id(0)
-    nblk = pl.num_programs(0)
-    blk = nblk - 1 - step_no
+                dstate, ext, jext, rowbuf, dact,
+                from_low, from_high, up_send, up_recv, down_send, down_recv):
+    turn = pl.program_id(0)
+    nblk = pl.num_programs(0) // 2
+    blk = nblk - 1 - lax.rem(turn, nblk)
     inner = tapv_ref.shape[1]
     both = act_ref.shape[1]
     nchunk = state_ref.shape[0]
     b = meta_ref[0]
     off0 = meta_ref[1]
-
-    @pl.when(step_no == 0)
-    def _():
-        df = chain(high_ref)
-        dr = chain(low_ref)
+    swap = Swap(reach, msgr_ref, msgf_ref, from_low, from_high, up_send, up_recv, down_send, down_recv)
+
+    @pl.when(turn == 0)
+    def _():
+        barrier = pltpu.get_barrier_semaphore()
+        pl.semaphore_wait(barrier, swap.greet(barrier))
+        swap.start()
+        ext[TB : TB + 8, :] = jnp.zeros((8, both), F32)
+        convg_ref[...] = jnp.zeros_like(convg_ref)
+        heads_ref[...] = jnp.zeros_like(heads_ref)
+        rowbuf[...] = jnp.zeros_like(rowbuf)
+
+    spread = spread_matrix(inner, 64)
+    spread_low = spread.astype(BF16)
+    spread2 = jnp.concatenate([spread_low, spread_low], axis=0)
+    i0, i1 = iota((Q, Q), 0), iota((Q, Q), 1)
+    after, before = (i0 > i1), (i0 < i1)
+
+    @pl.when(turn < nblk)
+    def _():
+        skip = widen_col(skip_ref[...], spread)
+        diag = i0 == i1
+        sums_low = jnp.concatenate([after, before], axis=1).astype(BF16)
+        for q in range(TB // Q):
+            rows = slice(q * Q, (q + 1) * Q)
+            t0 = blk * TB + q * Q
+            chunk = blk * (TB // Q) + q
+            dest = pl.ds(pl.multiple_of(blk * TB + q * Q, Q), Q)
+            dt, ld, run, bef = step_parts(step_ref[:, rows], bias_ref[...], dlog_ref[...])
+            ldt = jnp.log(jnp.maximum(dt, 1e-37))
+            cols = jnp.concatenate([ldt[:HP] - run[:HP], ldt[HP:] + bef[HP:]], axis=0).T
+            rowf, rowr = bef[:HP], -run[HP:]
+            maps = act_ref[rows, inner:]
+            entf, readf, entr, readr = maps[:, 0:64], maps[:, 64:128], maps[:, 128:192], maps[:, 192:256]
+            same = (i0 + t0 < b) == (i1 + t0 < b)
+            okf, okr = before & same, after & same
+            scores = jnp.where(okf, nt(entf, readf), jnp.where(okr, nt(entr, readr), 0.0))
+            dscore = jnp.zeros((Q, Q), F32)
+            for j in range(inner // 128):
+                lanes = slice(j * 128, (j + 1) * 128)
+                vp = act_ref[rows, lanes]
+                dyp32 = dy_ref[rows, lanes]
+                dyp = dyp32.astype(BF16)
+                dw = nt(halves(vp), dyp)
+                weights = []
+                for i, h in enumerate((2 * j, 2 * j + 1)):
+                    e = jnp.where(before, cols[:, h : h + 1] + rowf[h : h + 1],
+                                  cols[:, HP + h : HP + h + 1] + rowr[h : h + 1])
+                    x = jnp.exp(jnp.minimum(e, 60.0))
+                    weights.append((x * scores).astype(BF16))
+                    dwx = dw[i * Q : (i + 1) * Q] * x
+                    dscore = dscore + dwx
+                    sums = nn((dwx * scores).astype(BF16), sums_low)
+                    pf, pr = sums[:, :Q], sums[:, Q:]
+                    for place, part in enumerate((jnp.where(before, pf, 0.0), jnp.where(after, pr, 0.0),
+                                                  jnp.where(diag, pf, 0.0), jnp.where(diag, pr, 0.0))):
+                        rowbuf[chunk, place * HP + h : place * HP + h + 1, :] = jnp.sum(part, axis=0, keepdims=True)
+                dv = nn(jnp.concatenate(weights, axis=1), halves(dyp))
+                dact[dest, lanes] = dv + dyp32 * skip[:, lanes]
+            dsf = jnp.where(okf, dscore, 0.0)
+            dsr = jnp.where(okr, dscore, 0.0)
+            dsf_low, dsr_low = dsf.astype(BF16), dsr.astype(BF16)
+            dact[dest, inner:] = jnp.concatenate(
+                [nn(dsf_low, readf), nn(dsf.T.astype(BF16), entf), nn(dsr_low, readr), nn(dsr.T.astype(BF16), entr)],
+                axis=1)
+
+    @pl.when(turn == nblk)
+    def _():
+        swap.finish()
+        df = chain(from_high)
+        dr = chain(from_low)
         for c in range(nchunk):
             d = nchunk - 1 - c
             dstate[d, 0:64, :] = df.astype(BF16)
             df = pexp_ref[d, 0:1, :] * df + dhy_ref[d, 0:64, :]
             dstate[c, 64:128, :] = dr.astype(BF16)
             dr = pexp_ref[c, 1:2, :] * dr + dhy_ref[c, 64:128, :]
-        ext[TB : TB + 8, :] = jnp.zeros((8, both), F32)
-        convg_ref[...] = jnp.zeros_like(convg_ref)
-        heads_ref[...] = jnp.zeros_like(heads_ref)
-        rowbuf[...] = jnp.zeros_like(rowbuf)
-
-    @pl.when(step_no > 0)
+
+    @pl.when(turn > nblk)
     def _():
         ext[TB : TB + 8, :] = ext[0:8, :]
 
-    spread = spread_matrix(inner, 64)
-    spread_low = spread.astype(BF16)
-    spread2 = jnp.concatenate([spread_low, spread_low], axis=0)
-    skip = widen_col(skip_ref[...], spread)
-    i0, i1 = iota((Q, Q), 0), iota((Q, Q), 1)
-    after, before = (i0 > i1), (i0 < i1)
-    diag = i0 == i1
-    sums_low = jnp.concatenate([after, before], axis=1).astype(BF16)
-    after32, before32 = after.astype(F32), before.astype(F32)
-    for q in reversed(range(TB // Q)):
-        rows = slice(q * Q, (q + 1) * Q)
-        t0 = blk * TB + q * Q
-        chunk = blk * (TB // Q) + q
-        dt, ld, run, bef = step_parts(step_ref[:, rows], bias_ref[...], dlog_ref[...])
-        ef, er, tf, tr = state_factors(dt, run, bef, t0, b)
-        ldt = jnp.log(jnp.maximum(dt, 1e-37))
-        cols = jnp.concatenate([ldt[:HP] - run[:HP], ldt[HP:] + bef[HP:]], axis=0).T
-        rowf, rowr = bef[:HP], -run[HP:]
-        maps = act_ref[rows, inner:]
-        entf, readf, entr, readr = maps[:, 0:64], maps[:, 64:128], maps[:, 128:192], maps[:, 192:256]
-        same = (i0 + t0 < b) == (i1 + t0 < b)
-        okf, okr = before & same, after & same
-        scores = jnp.where(okf, nt(entf, readf), jnp.where(okr, nt(entr, readr), 0.0))
-        state = state_ref[chunk]
-        grad_state = dstate[chunk]
-        dscore = jnp.zeros((Q, Q), F32)
-        efe, ere = widen(ef, spread2), widen(er, spread2)
-        tfe, tre = widen(tf, spread2), widen(tr, spread2)
-        dy = dy_ref[rows, :]
-        values = act_ref[rows, :inner].astype(F32)
-        dyf, dyr = dy * efe, dy * ere
-        dyf_low, dyr_low = dyf.astype(BF16), dyr.astype(BF16)
-        dreadf = nt(dyf_low, state[0:64])
-        dreadr = nt(dyr_low, state[64:128])
-        qf = nt(spread_low, (nn(readf, state[0:64]) * dyf).astype(BF16))
-        qr = nt(spread_low, (nn(readr, state[64:128]) * dyr).astype(BF16))
-        dvf = nn(entf, grad_state[0:64]) * tfe
-        dvr = nn(entr, grad_state[64:128]) * tre
-        wf = nt(spread_low, (values * dvf).astype(BF16))
-        wr = nt(spread_low, (values * dvr).astype(BF16))
-        dentf = nt((values * tfe).astype(BF16), grad_state[0:64])
-        dentr = nt((values * tre).astype(BF16), grad_state[64:128])
-        through = state.astype(F32) * grad_state.astype(F32)
-        zf = jnp.sum(through[0:64], axis=0, keepdims=True) * pexp_ref[chunk, 0:1, :]
-        zr = jnp.sum(through[64:128], axis=0, keepdims=True) * pexp_ref[chunk, 1:2, :]
-        zf = nt(spread, jnp.broadcast_to(zf, (8, inner)), HIGHEST)[:, 0:1]
-        zr = nt(spread, jnp.broadcast_to(zr, (8, inner)), HIGHEST)[:, 0:1]
-        for j in range(inner // 128):
-            lanes = slice(j * 128, (j + 1) * 128)
-            vp = act_ref[rows, lanes]
-            dyp = dy_ref[rows, lanes].astype(BF16)
-            dw = nt(halves(vp), dyp)
-            weights = []
-            for i, h in enumerate((2 * j, 2 * j + 1)):
-                e = jnp.where(before, cols[:, h : h + 1] + rowf[h : h + 1],
-                              cols[:, HP + h : HP + h + 1] + rowr[h : h + 1])
-                x = jnp.exp(jnp.minimum(e, 60.0))
-                weights.append((x * scores).astype(BF16))
-                dwx = dw[i * Q : (i + 1) * Q] * x
-                dscore = dscore + dwx
-                sums = nn((dwx * scores).astype(BF16), sums_low)
-                pf, pr = sums[:, :Q], sums[:, Q:]
-                rowbuf[h : h + 1, :] = jnp.sum(jnp.where(before, pf, 0.0), axis=0, keepdims=True)
-                rowbuf[HP + h : HP + h + 1, :] = jnp.sum(jnp.where(after, pr, 0.0), axis=0, keepdims=True)
-                rowbuf[2 * HP + h : 2 * HP + h + 1, :] = jnp.sum(jnp.where(diag, pf, 0.0), axis=0, keepdims=True)
-                rowbuf[3 * HP + h : 3 * HP + h + 1, :] = jnp.sum(jnp.where(diag, pr, 0.0), axis=0, keepdims=True)
-            dv = nn(jnp.concatenate(weights, axis=1), halves(dyp))
-            dact[rows, lanes] = dv + dvf[:, lanes] + dvr[:, lanes] + dy[:, lanes] * skip[:, lanes]
-        dsf = jnp.where(okf, dscore, 0.0)
-        dsr = jnp.where(okr, dscore, 0.0)
-        dsf_low, dsr_low = dsf.astype(BF16), dsr.astype(BF16)
-        dentf = dentf + nn(dsf_low, readf)
-        dentr = dentr + nn(dsr_low, readr)
-        dreadf = dreadf + nn(dsf.T.astype(BF16), entf)
-        dreadr = dreadr + nn(dsr.T.astype(BF16), entr)
-        dact[rows, inner:] = jnp.concatenate([dentf, dreadf, dentr, dreadr], axis=1)
-        late = nn(jnp.concatenate([qf, wr], axis=0), after32, HIGHEST)
-        early = nn(jnp.concatenate([wf, qr], axis=0), before32, HIGHEST)
-        dld = jnp.concatenate(
-            [rowbuf[0:HP] + late[:HP] + early[:HP] + zf, rowbuf[HP : 2 * HP] + late[HP:] + early[HP:] + zr], axis=0)
-        dldt = rowbuf[2 * HP : 4 * HP] + jnp.concatenate([wf, wr], axis=0)
-        sig = jax.nn.sigmoid(step_ref[:, rows] + bias_ref[...])
-        ratio = jnp.where(dt < 1e-30, 1.0, sig / jnp.maximum(dt, 1e-30))
-        graw = dldt * ratio - jnp.exp(dlog_ref[...]) * sig * dld
-        gstep_ref[:, rows] = graw.astype(BF16)
-        heads_ref[:, 0:1] += jnp.sum(graw, axis=1, keepdims=True)
-        heads_ref[:, 1:2] += jnp.sum(dld * ld, axis=1, keepdims=True)
-
-    prev = jnp.where(blk == 0, jhalo_ref[...], jprev_ref[...])
-    jext[0:16, :] = prev.astype(F32)
-    jext[16 : 16 + TB, :] = joined_ref[...].astype(F32)
-    tok = iota((TB, 1), 0) + blk * TB
-    masks = [conv_mask(tok, m, b, off0) for m in range(4)]
-    later_masks = [conv_mask(tok + m, m, b, off0) for m in range(4)]
-    edge_masks = [conv_mask(iota((8, 1), 0) - 8 + m, m, b, off0) for m in range(4)]
-    for j in range(both // 128):
-        cols = slice(j * 128, (j + 1) * 128)
-        tap = tapv_ref[:, cols] if j * 128 < inner else taps_ref[:, j * 128 - inner : (j + 1) * 128 - inner]
-        shifted = [jext[16 : 16 + TB, cols]]
-        total = shifted[0] * tap[3:4]
-        for m in range(1, 4):
-            shifted.append(jext[16 - m : 16 - m + TB, cols] * masks[m])
-            total = total + shifted[m] * tap[3 - m : 4 - m]
-        sig = jax.nn.sigmoid(total)
-        dconv = dact[:, cols] * (sig * (1.0 + total * (1.0 - sig)))
-        ext[0:TB, cols] = dconv
-        for m in range(4):
-            convg_ref[3 - m : 4 - m, cols] += jnp.sum(dconv * shifted[m], axis=0, keepdims=True)
-        grad = dconv * tap[3:4]
-        for m in range(1, 4):
-            grad = grad + ext[m : m + TB, cols] * later_masks[m] * tap[3 - m : 4 - m]
-        if j * 128 < inner:
-            gv_ref[:, cols] = grad
-        else:
-            gs_ref[:, j * 128 - inner : (j + 1) * 128 - inner] = grad
-
-    @pl.when(step_no == nblk - 1)
+    @pl.when(turn >= nblk)
+    def _():
+        after32, before32 = after.astype(F32), before.astype(F32)
+        for q in range(TB // Q):
+            rows = slice(q * Q, (q + 1) * Q)
+            t0 = blk * TB + q * Q
+            chunk = blk * (TB // Q) + q
+            dest = pl.ds(pl.multiple_of(blk * TB + q * Q, Q), Q)
+            dt, ld, run, bef = step_parts(step_ref[:, rows], bias_ref[...], dlog_ref[...])
+            ef, er, tf, tr = state_factors(dt, run, bef, t0, b)
+            maps = act_ref[rows, inner:]
+            entf, readf, entr, readr = maps[:, 0:64], maps[:, 64:128], maps[:, 128:192], maps[:, 192:256]
+            state = state_ref[chunk]
+            grad_state = dstate[chunk]
+            efe, ere = widen(ef, spread2), widen(er, spread2)
+            tfe, tre = widen(tf, spread2), widen(tr, spread2)
+            dy = dy_ref[rows, :]
+            values = act_ref[rows, :inner].astype(F32)
+            dyf, dyr = dy * efe, dy * ere
+            dreadf = nt(dyf.astype(BF16), state[0:64])
+            dreadr = nt(dyr.astype(BF16), state[64:128])
+            qf = nt(spread_low, (nn(readf, state[0:64]) * dyf).astype(BF16))
+            qr = nt(spread_low, (nn(readr, state[64:128]) * dyr).astype(BF16))
+            dvf = nn(entf, grad_state[0:64]) * tfe
+            dvr = nn(entr, grad_state[64:128]) * tre
+            wf = nt(spread_low, (values * dvf).astype(BF16))
+            wr = nt(spread_low, (values * dvr).astype(BF16))
+            dentf = nt((values * tfe).astype(BF16), grad_state[0:64])
+            dentr = nt((values * tre).astype(BF16), grad_state[64:128])
+            through = state.astype(F32) * grad_state.astype(F32)
+            zf = jnp.sum(through[0:64], axis=0, keepdims=True) * pexp_ref[chunk, 0:1, :]
+            zr = jnp.sum(through[64:128], axis=0, keepdims=True) * pexp_ref[chunk, 1:2, :]
+            zf = nt(spread, jnp.broadcast_to(zf, (8, inner)), HIGHEST)[:, 0:1]
+            zr = nt(spread, jnp.broadcast_to(zr, (8, inner)), HIGHEST)[:, 0:1]
+            dact[dest, :inner] = dact[dest, :inner] + dvf + dvr
+            dact[dest, inner:] = dact[dest, inner:] + jnp.concatenate([dentf, dreadf, dentr, dreadr], axis=1)
+            late = nn(jnp.concatenate([qf, wr], axis=0), after32, HIGHEST)
+            early = nn(jnp.concatenate([wf, qr], axis=0), before32, HIGHEST)
+            rowsum = rowbuf[chunk]
+            dld = jnp.concatenate(
+                [rowsum[0:HP] + late[:HP] + early[:HP] + zf, rowsum[HP : 2 * HP] + late[HP:] + early[HP:] + zr], axis=0)
+            dldt = rowsum[2 * HP : 4 * HP] + jnp.concatenate([wf, wr], axis=0)
+            sig = jax.nn.sigmoid(step_ref[:, rows] + bias_ref[...])
+            ratio = jnp.where(dt < 1e-30, 1.0, sig / jnp.maximum(dt, 1e-30))
+            graw = dldt * ratio - jnp.exp(dlog_ref[...]) * sig * dld
+            gstep_ref[:, rows] = graw.astype(BF16)
+            heads_ref[:, 0:1] += jnp.sum(graw, axis=1, keepdims=True)
+            heads_ref[:, 1:2] += jnp.sum(dld * ld, axis=1, keepdims=True)
+
+        prev = jnp.where(blk == 0, jhalo_ref[...], jprev_ref[...])
+        jext[0:16, :] = prev.astype(F32)
+        jext[16 : 16 + TB, :] = joined_ref[...].astype(F32)
+        tok = iota((TB, 1), 0) + blk * TB
+        masks = [conv_mask(tok, m, b, off0) for m in range(4)]
+        later_masks = [conv_mask(tok + m, m, b, off0) for m in range(4)]
+        for j in range(both // 128):
+            cols = slice(j * 128, (j + 1) * 128)
+            tap = tapv_ref[:, cols] if j * 128 < inner else taps_ref[:, j * 128 - inner : (j + 1) * 128 - inner]
+            shifted = [jext[16 : 16 + TB, cols]]
+            total = shifted[0] * tap[3:4]
+            for m in range(1, 4):
+                shifted.append(jext[16 - m : 16 - m + TB, cols] * masks[m])
+                total = total + shifted[m] * tap[3 - m : 4 - m]
+            sig = jax.nn.sigmoid(total)
+            dconv = dact[pl.ds(pl.multiple_of(blk * TB, TB), TB), cols] * (sig * (1.0 + total * (1.0 - sig)))
+            ext[0:TB, cols] = dconv
+            for m in range(4):
+                convg_ref[3 - m : 4 - m, cols] += jnp.sum(dconv * shifted[m], axis=0, keepdims=True)
+            grad = dconv * tap[3:4]
+            for m in range(1, 4):
+                grad = grad + ext[m : m + TB, cols] * later_masks[m] * tap[3 - m : 4 - m]
+            if j * 128 < inner:
+                gv_ref[:, cols] = grad
+            else:
+                gs_ref[:, j * 128 - inner : (j + 1) * 128 - inner] = grad
+
+    @pl.when(turn == 2 * nblk - 1)
     def _():
         first = jnp.concatenate([jnp.zeros((8, both), F32), ext[0:8, :]], axis=0)
         tap = jnp.concatenate([tapv_ref[...], taps_ref[...]], axis=1)
+        edge_masks = [conv_mask(iota((8, 1), 0) - 8 + m, m, b, off0) for m in range(4)]
         lent = jnp.zeros((8, both), F32)
         for m in range(1, 4):
             lent = lent + first[m : m + 8] * edge_masks[m] * tap[3 - m : 4 - m]
@@ -859,7 +897,7 @@
 SMEM_SPEC = pl.BlockSpec(memory_space=pltpu.SMEM)
 
 
-def call(kernel, grid, ins, outs, scratch, vmem, flops):
+def call(kernel, grid, ins, outs, scratch, vmem, flops, ident=None):
     arrays = [a for a, _ in ins]
     return pl.pallas_call(
         kernel,
@@ -869,7 +907,8 @@
         out_shape=[jax.ShapeDtypeStruct(a.shape, a.dtype) for a, _ in outs],
         scratch_shapes=scratch,
         compiler_params=pltpu.CompilerParams(
-            dimension_semantics=("arbitrary",), vmem_limit_bytes=vmem * MIB),
+            dimension_semantics=("arbitrary",), vmem_limit_bytes=vmem * MIB, collective_id=ident,
+            has_side_effects=ident is not None),
         cost_estimate=pl.CostEstimate(
             flops=int(flops), transcendentals=0,
             bytes_accessed=sum(a.size * a.dtype.itemsize for a in arrays)
@@ -934,46 +973,41 @@
         [pltpu.VMEM((TB + 8, both), F32), pltpu.VMEM((64, inner), F32), pltpu.VMEM((64, inner), F32),
          pltpu.VMEM((8, inner), F32)],
         48, 2 * length * width * (2 * inner + maps))
-    low, high = swap(msgf, msgr, reach, 1)
-
-    mixed = shape((length, inner), F32)
+
+    def turned(array):
+        rest = (0,) * (array.ndim - 1)
+        return pl.BlockSpec((TB,) + array.shape[1:], lambda i: (lax.rem(i, nblk),) + rest)
+
+    def turned_cols(array):
+        return pl.BlockSpec((array.shape[0], TB), lambda i: (0, lax.rem(i, nblk)))
+
+    def final(array, rows=TB):
+        rest = (0,) * (array.ndim - 1)
+        return pl.BlockSpec((rows,) + array.shape[1:], lambda i: (jnp.maximum(i - 2 * nblk, 0),) + rest)
+
     state = shape((nchunk, 128, inner), BF16)
-    sums = shape((8, length), F32)
-    mixed, state, sums = call(
-        mix_kernel, nblk,
-        [(meta, SMEM_SPEC), (act, rows_spec(act)), (step, cols_spec(step)), (bias, whole_spec(bias)),
-         (dlog, whole_spec(dlog)), (gate, rows_spec(gate)), (cotangent, rows_spec(cotangent)),
-         (out_proj, whole_spec(out_proj)), (gain_gate, whole_spec(gain_gate)), (skip, whole_spec(skip)),
-         (inc, whole_spec(inc)), (pexp, whole_spec(pexp)), (low, whole_spec(low)), (high, whole_spec(high))],
-        [(mixed, rows_spec(mixed)), (state, whole_spec(state)), (sums, cols_spec(sums))],
-        [], 48, 2 * length * width * inner * 2)
-    (sums_other,) = core_swap([sums], 2)
-
     out_part = shape((length, width), BF16)
     ggate = shape((length, inner), BF16)
     dy = shape((length, inner), F32)
     dhy = shape((nchunk, 128, inner), F32)
     small = shape((8, inner), F32)
     ggw = shape((width, inner), BF16)
-    ng = shape((nblk, TB, inner), BF16)
-    out_part, ggate, dy, dhy, msgf, msgr, small, ggw, ng = call(
-        gate_kernel, nblk,
-        [(meta, SMEM_SPEC), (sums, cols_spec(sums)), (sums_other, cols_spec(sums_other)), (mixed, rows_spec(mixed)),
-         (gate, rows_spec(gate)), (cotangent, rows_spec(cotangent)), (out_proj, whole_spec(out_proj)),
-         (gain_gate, whole_spec(gain_gate)), (act, rows_spec(act)), (step, cols_spec(step)),
-         (bias, whole_spec(bias)), (dlog, whole_spec(dlog)), (pexp, whole_spec(pexp)), (normt, whole_spec(normt))],
-        [(out_part, rows_spec(out_part)), (ggate, whole_spec(ggate)), (dy, rows_spec(dy)),
-         (dhy, rows_spec(dhy, cq)), (msg, whole_spec(msg)), (msg, whole_spec(msg)), (small, whole_spec(small)),
-         (ggw, whole_spec(ggw)), (ng, whole_spec(ng))],
-        [pltpu.VMEM((64, inner), F32), pltpu.VMEM((64, inner), F32), pltpu.VMEM((8, inner), F32)],
-        48, 2 * length * width * inner * 4)
-    low, high = swap(msgr, msgf, reach, 3)
-
-    ng = ng.reshape(length, inner)
     gow = shape((inner, width), BF16)
-    (gow,) = call(
-        outgrad_kernel, 1, [(ng, whole_spec(ng)), (cotangent, whole_spec(cotangent))], [(gow, whole_spec(gow))],
-        [], 32, 2 * length * width * inner)
+    state, out_part, ggate, dy, dhy, gmsgf, gmsgr, small, ggw, gow = call(
+        partial(mix_kernel, reach), 3 * nblk,
+        [(meta, SMEM_SPEC), (act, turned(act)), (step, turned_cols(step)), (bias, whole_spec(bias)),
+         (dlog, whole_spec(dlog)), (gate, turned(gate)), (cotangent, whole_spec(cotangent)),
+         (out_proj, whole_spec(out_proj)), (gain_gate, whole_spec(gain_gate)), (skip, whole_spec(skip)),
+         (inc, whole_spec(inc)), (pexp, whole_spec(pexp)), (msgf, whole_spec(msgf)), (msgr, whole_spec(msgr)),
+         (normt, whole_spec(normt))],
+        [(state, whole_spec(state)), (out_part, final(out_part)), (ggate, whole_spec(ggate)), (dy, final(dy)),
+         (dhy, final(dhy, cq)), (msg, whole_spec(msg)), (msg, whole_spec(msg)), (small, whole_spec(small)),
+         (ggw, whole_spec(ggw)), (gow, whole_spec(gow))],
+        [pltpu.VMEM((length, inner), F32), pltpu.VMEM((length, inner), BF16), pltpu.VMEM((nblk, 8, TB), F32),
+         pltpu.VMEM((nblk, 8, TB), F32), pltpu.VMEM((64, inner), F32), pltpu.VMEM((64, inner), F32),
+         pltpu.VMEM((8, inner), F32), pltpu.SemaphoreType.DMA((nblk,)), pltpu.SemaphoreType.DMA((nblk,))]
+        + swap_scratch(reach, inner),
+        56, 2 * length * width * inner * 6, 1)
 
     gv = shape((length, inner), F32)
     gs = shape((length, maps), F32)
@@ -981,19 +1015,31 @@
     lent = shape((8, both), F32)
     convg = shape((8, both), F32)
     hsum = shape((2 * HP, 128), F32)
-    prev_spec = pl.BlockSpec((16, both), lambda i: (jnp.maximum((nblk - 1 - i) * (TB // 16) - 1, 0), 0))
+
+    def flipped(array):
+        rest = (0,) * (array.ndim - 1)
+        return pl.BlockSpec((TB,) + array.shape[1:], lambda i: (nblk - 1 - lax.rem(i, nblk),) + rest)
+
+    def flipped_late(array):
+        rest = (0,) * (array.ndim - 1)
+        return pl.BlockSpec((TB,) + array.shape[1:], lambda i: (jnp.minimum(2 * nblk - 1 - i, nblk - 1),) + rest)
+
+    step_spec = pl.BlockSpec((2 * HP, TB), lambda i: (0, nblk - 1 - lax.rem(i, nblk)))
+    gstep_spec = pl.BlockSpec((2 * HP, TB), lambda i: (0, jnp.minimum(2 * nblk - 1 - i, nblk - 1)))
+    prev_spec = pl.BlockSpec(
+        (16, both), lambda i: (jnp.maximum(jnp.minimum(2 * nblk - 1 - i, nblk - 1) * (TB // 16) - 1, 0), 0))
     gv, gs, gstep, lent, convg, hsum = call(
-        back_kernel, nblk,
-        [(meta, SMEM_SPEC), (act, rows_spec(act, TB, nblk)), (step, cols_spec(step, nblk)), (bias, whole_spec(bias)),
-         (dlog, whole_spec(dlog)), (dy, rows_spec(dy, TB, nblk)), (skip, whole_spec(skip)),
-         (state, whole_spec(state)), (dhy, whole_spec(dhy)), (pexp, whole_spec(pexp)), (low, whole_spec(low)),
-         (high, whole_spec(high)), (joined, rows_spec(joined, TB, nblk)), (joined, prev_spec),
+        partial(back_kernel, reach), 2 * nblk,
+        [(meta, SMEM_SPEC), (act, flipped(act)), (step, step_spec), (bias, whole_spec(bias)),
+         (dlog, whole_spec(dlog)), (dy, flipped(dy)), (skip, whole_spec(skip)),
+         (state, whole_spec(state)), (dhy, whole_spec(dhy)), (pexp, whole_spec(pexp)), (gmsgf, whole_spec(gmsgf)),
+         (gmsgr, whole_spec(gmsgr)), (joined, flipped_late(joined)), (joined, prev_spec),
          (jhalo, whole_spec(jhalo)), (conv_value, whole_spec(conv_value)), (conv_state, whole_spec(conv_state))],
-        [(gv, rows_spec(gv, TB, nblk)), (gs, rows_spec(gs, TB, nblk)), (gstep, cols_spec(gstep, nblk)),
+        [(gv, flipped_late(gv)), (gs, flipped_late(gs)), (gstep, gstep_spec),
          (lent, whole_spec(lent)), (convg, whole_spec(convg)), (hsum, whole_spec(hsum))],
         [pltpu.VMEM((nchunk, 128, inner), BF16), pltpu.VMEM((TB + 8, both), F32), pltpu.VMEM((TB + 16, both), F32),
-         pltpu.VMEM((4 * HP, Q), F32), pltpu.VMEM((TB, both), F32)],
-        56, 2 * length * width * inner * 4)
+         pltpu.VMEM((nchunk, 4 * HP, Q), F32), pltpu.VMEM((length, both), F32)] + swap_scratch(reach, inner),
+        56, 2 * length * width * inner * 4, 3)
     from_next = lax.ppermute(lent, "seq", [(i + 1, i) for i in range(count - 1)])
 
     gn = shape((length, width), BF16)

time: 298 us -> 291 us (0.977)
  Pallas kernels: 251 us -> 239 us
    pallas_call x2 -> x0, Pallas kernels: 30.1 us -> none  [swap(): pl.pallas_call(partial(swap_kernel, reach), out_shape=(shape, shape), in_...]
    pallas_call x7 -> x5, Pallas kernels: 106 us -> 126 us  [call(): pl.pallas_call(kernel, grid=(grid,), in_specs=[s for _, s in ins], out_sp...]
    pallas_call x2 -> x1, Pallas kernels: 7.75 us -> 6.54 us  [core_swap(): pl.pallas_call(partial(core_swap_kernel, count), out_shape=tuple((jax.Sha...]
    unnamed x78 -> x62, local copies, waits for them, and re-layouts: 18.8 us -> 19.5 us
where the time goes in v3:
time: 291 us; the launch traced here: 289 us
  Pallas kernels  239 us (82%)
  local copies, waits for them, and re-layouts  29.9 us (10%)
  other arithmetic  8.69 us (3%)
  starting transfers between devices  6.12 us (2%)
  waiting for transfers between devices  4.72 us (2%)
    pallas_call x5, Pallas kernels, call(): pl.pallas_call(kernel, grid=(grid,), in_specs=[s for _, s in ins], out_sp...  126 us
    pallas_call x1, Pallas kernels, reduce_all(): pl.pallas_call(partial(reduce_kernel, count, bits), out_shape=[jax.ShapeD...  106 us
    unnamed x62, local copies, waits for them, and re-layouts  19.5 us
    pallas_call x1, Pallas kernels, core_swap(): pl.pallas_call(partial(core_swap_kernel, count), out_shape=tuple((jax.Sha...  6.54 us
  transfers between devices with their start and end apart: 2, of which 1 were waited for; matrix products, arithmetic and copies ran while one was open for 2% of the time, Pallas kernels for 0%

profile of v3, /device:TPU:0, one launch (start us, length us, event | category | flops | bytes accessed | tf_op | source)
XLA Modules:
  0.0 289.4 jit_solution(14153329085587351216)
XLA Ops:
  0.6 0.7 slice.38
  1.4 4.8 %collective-permute-start = (bf16[16,768]{1,0:T(8,128)(2,1)S(1)}, bf16[16,768]{1,0:T(8,128)(2,1)S(1)}, u32[]{:S(2)}, u32[]{:S(2)}) collective-permute-start(bf16[16,768]{1,0:T(8,128)(2,1)S(1)} %slice.38), channel_id=1, source_target_pairs={{0,2},{2,4},{4,6},{6,8},{8,10},{10,12},{12,14},{14,16},{16,18},{18... | collective-permute-start | bytes 73736 | tf_op jit(solution)/shard_map/ppermute | solution.py:944
  6.2 0.7 pad.17
  6.9 0.1 maximum_bitcast_fusion
  7.0 0.7 pad_bitcast_fusion
  7.6 0.7 pad.16
  8.3 0.7 reshape.54.gain_ref
  9.0 1.3 reshape.58.ggain_ref
  10.3 0.7 copy.34.skip_ref
  10.9 0.1 reshape.62.bias_ref
  11.0 0.1 copy.31.dlog_ref
  11.1 0.8 copy.40
  11.9 0.0 collective-permute-done.halo_ref
  11.9 0.0 copy-start.7
  11.9 1.0 copy-done.7
  12.9 1.3 copy-done.17
  14.2 1.3 copy-done.18
  15.5 0.7 copy-done.19
  16.2 0.7 copy-done.20
  16.9 0.7 copy-done.21
  17.5 16.9 %shard_map.254 = (s32[8]{0:T(128)S(1)}, bf16[768,1024]{1,0:T(8,128)(2,1)S(1)}, f32[1024,768]{1,0:T(8,128)}, bf16[1024,1024]{1,0:T(8,128)(2,1)}, bf16[16,1024]{1,...) custom-call(s32[9]{0:T(128)S(1)} %copy-done.21, ...), custom_call_target="tpu_custom_call" | custom-call | flops 2818572288 | bytes 16936260 | tf_op jit(solution)/shard_map/pallas_call | solution.py:902
  34.5 0.0 copy-done.15
  34.5 0.0 copy-start.3
  34.5 1.1 copy-done.3
  35.6 0.7 copy-done.23
  36.3 0.6 copy-done.25
  36.9 0.6 copy-done.26
  37.5 0.7 copy-done.27
  38.2 0.6 copy-done.28
  38.8 0.5 copy-done.29
  39.3 45.8 %shard_map.255 = (bf16[8,128,768]{2,1,0:T(8,128)(2,1)}, bf16[1024,768]{1,0:T(8,128)(2,1)}, bf16[1024,768]{1,0:T(8,128)(2,1)}, f32[1024,768]{1,0:T(8,128)}, f32[8...) custom-call(s32[8]{0:T(128)} %copy-done.29, ...), custom_call_target="tpu_custom_call" | custom-call | flops 7247757312 | bytes 26783072 | tf_op jit(solution)/shard_map/pallas_call | solution.py:902
  85.1 46.2 %shard_map.256 = (f32[1024,768]{1,0:T(8,128)}, f32[1024,256]{1,0:T(8,128)}, bf16[32,1024]{1,0:T(8,128)(2,1)}, f32[8,1024]{1,0:T(8,128)}, f32[8,1024]{1,0:T(8,128)}, /*index=5*/f32[32,128]{1,0:T(8,128)}) custom-call(s32[8]{0:T(128)} %copy-done.29, bf16[1024,1024]{1,0:T(8,128)(2,1)} %get-tuple-element.60.act_ref, f32[32,1024]{1,0:T(8,128)} %copy-done.23, ...), custom_call_target="tpu_custom_call" | custom-call | flops 4831838208 | bytes 18973024 | tf_op jit(solution)/shard_map/pallas_call | solution.py:902
  131.3 1.3 collective-permute-start.1
  132.6 4.7 %collective-permute-done.1.next_ref = f32[8,1024]{1,0:T(8,128)S(1)} collective-permute-done((f32[8,1024]{1,0:T(8,128)}, f32[8,1024]{1,0:T(8,128)S(1)}, u32[]{:S(2)}, u32[]{:S(2)}) %collective-permute-start.1) | collective-permute-done | bytes 32800 | tf_op jit(solution)/shard_map/ppermute | solution.py:1043
  137.4 1.2 copy-done.22
  138.6 0.8 copy-done.24
  139.4 9.2 %shard_map.257 = (bf16[1024,768]{1,0:T(8,128)(2,1)}, bf16[1024,256]{1,0:T(8,128)(2,1)S(1)}, bf16[768,768]{1,0:T(8,128)(2,1)S(1)}, bf16[32,768]{1,0:T(8,128)(2,1)S(1)}) custom-call(f32[1024,768]{1,0:T(8,128)} %get-tuple-element.75.gv_ref, f32[1024,256]{1,0:T(8,128)S(1)} %copy-done.22, f32[8,1024]{1,0:T(8,128)S(1)} %collective-permute-done.1.next_ref, ...), custom_call_target="tpu_custom_call" | custom-call | flops 3623878656 | bytes 13172736 | tf_op jit(solution)/shard_map/pallas_call | solution.py:902
  148.6 1.0 copy-done.6
  149.6 1.4 copy-done.1
  151.1 6.5 %shard_map.258 = (bf16[1024,768]{1,0:T(8,128)(2,1)S(1)}, bf16[1024,256]{1,0:T(8,128)(2,1)S(1)}, bf16[1024,768]{1,0:T(8,128)(2,1)S(1)}, f32[8,1024]{1,0:T(8,128)S(1)}) custom-call(bf16[1024,768]{1,0:T(8,128)(2,1)S(1)} %copy-done.1, bf16[1024,256]{1,0:T(8,128)(2,1)S(1)} %get-tuple-element.81.refs_1_.smine_ref, bf16[1024,768]{1,0:T(8,128)(2,1)S(1)} %copy-done, ...), custom_call_target="tpu_custom_call" | custom-call | tf_op jit(solution)/shard_map/pallas_call | solution.py:298
  157.6 0.0 copy-start.4
  157.6 1.1 copy-done.4
  158.8 0.0 copy-done.13
  158.8 0.0 copy-start.5
  158.8 8.2 %shard_map.259 = (f32[1024,768]{1,0:T(8,128)}, f32[16,1024]{1,0:T(8,128)S(1)}, bf16[768,256]{1,0:T(8,128)(2,1)S(1)}, bf16[1024,768]{1,0:T(8,128)(2,1)}) custom-call(bf16[1024,768]{1,0:T(8,128)(2,1)S(1)} %copy-done.2, bf16[1024,768]{1,0:T(8,128)(2,1)S(1)} %get-tuple-element.84.other_ref, bf16[1024,256]{1,0:T(8,128)(2,1)S(1)} %get-tuple-element.81.refs_1_.smine_ref, ...), custom_call_target="tpu_custom_call" | custom-call | flops 805306368 | bytes 17738752 | tf_op jit(solution)/shard_map/pallas_call | solution.py:902
  167.0 106.3 %shard_map.260 = (bf16[768,768]{1,0:T(8,128)(2,1)S(1)}, bf16[768,768]{1,0:T(8,128)(2,1)S(1)}, bf16[768,768]{1,0:T(8,128)(2,1)S(1)}, bf16[768,256]{1,0:T(8,128)(2...) custom-call(bf16[768,768]{1,0:T(8,128)(2,1)S(1)} %copy-done.5, bf16[768,768]{1,0:T(8,128)(2,1)} %get-tuple-element.93.refs_1_, ...), custom_call_target="tpu_custom_call" | custom-call | tf_op jit(solution)/shard_map/pallas_call | solution.py:455
  273.3 0.0 copy-start.9
  273.3 0.7 copy-done.9
  274.0 0.6 copy-done.11
  274.7 0.6 copy-done.16
  275.3 0.1 reshape.61
  275.4 0.5 fusion
  275.9 0.6 slice_bitcast_fusion
  276.5 1.3 slice.42
  277.7 1.3 slice.41
  279.1 1.5 slice_reduce_fusion
  280.6 0.1 reshape_squeeze.3
  280.6 0.6 reduce_sum.9
  281.3 0.8 slice_convert_fusion
  282.1 0.7 copy.43
  282.7 1.9 convert_element_type.22
  284.7 1.6 convert_element_type.20
  286.3 1.6 convert_element_type.21
  287.8 1.6 convert_element_type.23
  (34 shorter events, 0.1 us)
Async XLA Ops:
  1.4 10.5 %collective-permute-start = (bf16[16,768]{1,0:T(8,128)(2,1)S(1)}, bf16[16,768]{1,0:T(8,128)(2,1)S(1)}, u32[]{:S(2)}, u32[]{:S(2)}) collective-permute-start(bf16[16,768]{1,0:T(8,128)(2,1)S(1)} %slice.38), channel_id=1, source_target_pairs={{0,2},{2,4},{4,6},{6,8},{8,10},{10,12},{12,14},{14,16},{16,18},{18... | collective-permute-start | bytes 73736 | tf_op jit(solution)/shard_map/ppermute | solution.py:944
  11.0 23.4 %copy-start.14 = (f32[32,1]{1,0:T(8,128)}, f32[32,1]{1,0:T(8,128)S(1)}, u32[]{:S(2)}) copy-start(f32[32,1]{1,0:T(8,128)S(1)} %reshape.62.bias_ref) | copy-start | bytes 388
  11.1 23.3 %copy-start.15 = (f32[32,1]{1,0:T(8,128)}, f32[32,1]{1,0:T(8,128)S(1)}, u32[]{:S(2)}) copy-start(f32[32,1]{1,0:T(8,128)S(1)} %copy.31.dlog_ref) | copy-start | bytes 388
  11.9 1.0 copy-start.7
  12.9 1.3 copy-start.17
  14.2 1.3 copy-start.18
  15.5 0.7 copy-start.19
  16.2 0.7 copy-start.20
  16.9 0.7 copy-start.21
  34.5 1.1 copy-start.3
  35.6 0.7 copy-start.23
  36.3 0.6 copy-start.25
  36.9 0.6 copy-start.26
  37.5 0.7 copy-start.27
  38.2 0.6 copy-start.28
  38.8 0.5 copy-start.29
  131.3 6.0 %collective-permute-start.1 = (f32[8,1024]{1,0:T(8,128)}, f32[8,1024]{1,0:T(8,128)S(1)}, u32[]{:S(2)}, u32[]{:S(2)}) collective-permute-start(f32[8,1024]{1,0:T(8,128)} %get-tuple-element.77), channel_id=1, source_target_pairs={{2,0},{4,2},{6,4},{8,6},{10,8},{12,10},{14,12},{16,14},{18,16},{20... | collective-permute-start | bytes 98312 | tf_op jit(solution)/shard_map/ppermute | solution.py:1043
  137.4 1.2 copy-start.22
  138.6 0.8 copy-start.24
  139.4 10.2 %copy-start = (bf16[1024,768]{1,0:T(8,128)(2,1)S(1)}, bf16[1024,768]{1,0:T(8,128)(2,1)}, u32[]{:S(2)}) copy-start(bf16[1024,768]{1,0:T(8,128)(2,1)} %get-tuple-element.82.refs_2_.omine_ref) | copy-start | bytes 4718596
  139.4 10.2 %copy-start.10 = (f32[8,1024]{1,0:T(8,128)S(1)}, f32[8,1024]{1,0:T(8,128)}, u32[]{:S(2)}) copy-start(f32[8,1024]{1,0:T(8,128)} %get-tuple-element.83.refs_3_.cmine_ref) | copy-start | bytes 98308
  148.6 1.0 copy-start.6
  149.6 1.4 copy-start.1
  151.0 7.7 %copy-start.2 = (bf16[1024,768]{1,0:T(8,128)(2,1)S(1)}, bf16[1024,768]{1,0:T(8,128)(2,1)}, u32[]{:S(2)}) copy-start(bf16[1024,768]{1,0:T(8,128)(2,1)} %get-tuple-element.80.refs_0_.mine_ref) | copy-start | bytes 4718596
  151.0 7.7 %copy-start.8 = (bf16[768,256]{1,0:T(8,128)(2,1)S(1)}, bf16[768,256]{1,0:T(8,128)(2,1)}, u32[]{:S(2)}) copy-start(bf16[768,256]{1,0:T(8,128)(2,1)} %ws_ref.3) | copy-start | bytes 1179652
  151.0 7.7 %copy-start.12 = (f32[8,768]{1,0:T(8,128)S(1)}, f32[8,768]{1,0:T(8,128)}, u32[]{:S(2)}) copy-start(f32[8,768]{1,0:T(8,128)} %get-tuple-element.87.small_ref) | copy-start | bytes 73732
  151.0 7.7 %copy-start.13 = (f32[32,128]{1,0:T(8,128)S(1)}, f32[32,128]{1,0:T(8,128)}, u32[]{:S(2)}) copy-start(f32[32,128]{1,0:T(8,128)} %get-tuple-element.88.hsum_ref) | copy-start | bytes 49156
  157.6 1.1 copy-start.4
  158.8 8.2 %copy-start.5 = (bf16[768,768]{1,0:T(8,128)(2,1)S(1)}, bf16[768,768]{1,0:T(8,128)(2,1)}, u32[]{:S(2)}) copy-start(bf16[768,768]{1,0:T(8,128)(2,1)} %get-tuple-element.92.refs_0_) | copy-start | bytes 3538948
  273.3 0.7 copy-start.9
  274.0 0.6 copy-start.11
  274.7 0.6 copy-start.16

commit v4 on v0

v4 whole, which is shorter than its diff:
```python
from functools import partial

import jax
import jax.numpy as jnp
from jax import lax
from jax.experimental import pallas as pl
from jax.experimental.pallas import tpu as pltpu
from jax.sharding import PartitionSpec as P

EPSILON = 1e-05
LEN_MOST = 4096
Q = 128
TB = 256
HP = 16
MIB = 1024 * 1024
VMEM_LIMIT = 63 * MIB
HIGHEST = lax.Precision.HIGHEST
F32 = jnp.float32
BF16 = jnp.bfloat16
MESH = pl.DeviceIdType.MESH


def nn(a, b, precision=None):
    return jnp.dot(a, b, preferred_element_type=F32, precision=precision)


def nt(a, b, precision=None):
    return lax.dot_general(a, b, (((1,), (1,)), ((), ())), preferred_element_type=F32, precision=precision)


def tn(a, b, precision=None):
    return lax.dot_general(a, b, (((0,), (0,)), ((), ())), preferred_element_type=F32, precision=precision)


def iota(shape, axis):
    return lax.broadcasted_iota(jnp.int32, shape, axis)


def spread_matrix(width, hdim):
    return (iota((HP, width), 1) // hdim == iota((HP, width), 0)).astype(F32)


def split(x):
    hi = x.astype(BF16)
    return hi, (x - hi.astype(F32)).astype(BF16)


def widen(rows, spread2):
    hi, lo = split(rows.T)
    return nn(jnp.concatenate([hi, lo], axis=1), spread2)


def widen_col(col, spread):
    return tn(jnp.broadcast_to(col, (HP, 8)), spread, HIGHEST)[0:1]


def silu(x):
    return x * jax.nn.sigmoid(x)


def softplus(x):
    return jnp.maximum(x, 0.0) + jnp.log1p(jnp.exp(-jnp.abs(x)))


def step_parts(step, bias, dlog):
    dt = softplus(step + bias)
    ld = -jnp.exp(dlog) * dt
    upto = (iota((Q, Q), 0) <= iota((Q, Q), 1)).astype(F32)
    run = nn(ld, upto, HIGHEST)
    return dt, ld, run, run - ld


def state_factors(dt, run, bef, t0, b):
    t1 = t0 + Q
    tok = iota((1, Q), 1) + t0
    ef = jnp.where((tok < b) | (t0 > b), jnp.exp(bef[:HP]), 0.0)
    er = jnp.where((tok >= b) | (t1 < b), jnp.exp(run[HP:, Q - 1 : Q] - run[HP:]), 0.0)
    tf = jnp.where((tok >= b) | (t1 <= b), jnp.exp(run[:HP, Q - 1 : Q] - run[:HP]), 0.0) * dt[:HP]
    tr = jnp.where((tok < b) | (t0 >= b), jnp.exp(bef[HP:]), 0.0) * dt[HP:]
    return ef, er, tf, tr


def conv_mask(tok, shift, b, off0):
    lost = ((tok < b) & (tok + off0 < shift)) | ((tok >= b) & (tok < b + shift))
    return jnp.where(lost, 0.0, 1.0)


def put_message(ref, state, passed):
    hi, lo = split(passed)
    ref[0:64, :] = state.astype(BF16)
    row = iota((16, state.shape[1]), 0)
    tail = jnp.where(row == 0, hi.astype(F32), jnp.where(row == 1, lo.astype(F32), 0.0))
    ref[64:80, :] = tail.astype(BF16)


def chain(ref):
    total = ref[0, 0:64, :].astype(F32)
    passed = None
    for k in range(1, ref.shape[0]):
        tail = ref[k - 1, 64:80, :].astype(F32)
        here = tail[0:1] + tail[1:2]
        passed = here if passed is None else passed * here
        total = total + passed * ref[k, 0:64, :].astype(F32)
    return total


class Swap:
    def __init__(self, reach, up_ref, down_ref, from_low, from_high, up_send, up_recv, down_send, down_recv):
        self.me, self.core, self.count = lax.axis_index("seq"), lax.axis_index("head"), lax.axis_size("seq")
        self.reach, self.up_ref, self.down_ref, self.from_low, self.from_high = reach, up_ref, down_ref, from_low, from_high
        self.sems = up_send, up_recv, down_send, down_recv

    def up(self, k):
        return pltpu.make_async_remote_copy(
            src_ref=self.up_ref, dst_ref=self.from_low.at[k - 1], send_sem=self.sems[0].at[k - 1],
            recv_sem=self.sems[1].at[k - 1], device_id=(self.me + k, self.core), device_id_type=MESH)

    def down(self, k):
        return pltpu.make_async_remote_copy(
            src_ref=self.down_ref, dst_ref=self.from_high.at[k - 1], send_sem=self.sems[2].at[k - 1],
            recv_sem=self.sems[3].at[k - 1], device_id=(self.me - k, self.core), device_id_type=MESH)

    def greet(self, barrier):
        me, core, count = self.me, self.core, self.count
        for k in range(1, self.reach + 1):
            @pl.when(me + k < count)
            def _():
                pl.semaphore_signal(barrier, inc=1, device_id=(me + k, core), device_id_type=MESH)

            @pl.when(me >= k)
            def _():
                pl.semaphore_signal(barrier, inc=1, device_id=(me - k, core), device_id_type=MESH)
        return jnp.minimum(me, self.reach) + jnp.minimum(count - 1 - me, self.reach)

    def start(self):
        me, count = self.me, self.count
        for k in range(1, self.reach + 1):
            @pl.when(me + k < count)
            def _():
                self.up(k).start()

            @pl.when(me >= k)
            def _():
                self.down(k).start()

            @pl.when(me < k)
            def _():
                self.from_low[k - 1] = jnp.zeros_like(self.from_low[k - 1])

            @pl.when(me + k >= count)
            def _():
                self.from_high[k - 1] = jnp.zeros_like(self.from_high[k - 1])

    def finish(self):
        me, count = self.me, self.count
        for k in range(1, self.reach + 1):
            @pl.when(me + k < count)
            def _():
                self.up(k).wait_send()
                self.down(k).wait_recv()

            @pl.when(me >= k)
            def _():
                self.down(k).wait_send()
                self.up(k).wait_recv()


def chunk_scores(maps, t0, b):
    tr, tc = iota((Q, Q), 0), iota((Q, Q), 1)
    same = (tr + t0 < b) == (tc + t0 < b)
    fwd = nt(maps[:, 64:128], maps[:, 0:64])
    rev = nt(maps[:, 192:256], maps[:, 128:192])
    return jnp.where((tr > tc) & same, fwd, jnp.where((tr < tc) & same, rev, 0.0))


def halves(x):
    left = iota(x.shape, 1) < 64
    zero = jnp.zeros_like(x)
    return jnp.concatenate([jnp.where(left, x, zero), jnp.where(left, zero, x)], axis=0)


class Reduce:
    def __init__(self, bits, pieces, rs_send, rs_recv, ag_send, ag_recv):
        me, core = lax.axis_index("seq"), lax.axis_index("head")
        bit = [lax.rem(me // (1 << k), 2) for k in range(bits)]
        mate = [me + (1 - 2 * bit[k]) * (1 << k) for k in range(bits)]
        self.mates = list(mate)
        self.bits, self.bit, self.mate, self.core, self.pieces = bits, bit, mate, core, pieces
        self.sems = rs_send, rs_recv, ag_send, ag_recv
        self.pos = [0] * len(pieces)
        self.steps = []
        for piece in pieces:
            halvings = halvings_of(piece["work"].shape[0], bits)
            self.steps.append([("rs", s) for s in range(bits)] + [("ag", s) for s in reversed(range(halvings))])

    def geometry(self, p, s):
        rows = self.pieces[p]["work"].shape[0]
        halvings = halvings_of(rows, self.bits)
        off, slot = jnp.int32(0), 0
        for t in range(s):
            if t < halvings:
                rows = rows // 2
                off = off + self.bit[self.pieces[p]["order"][t]] * rows
            slot += rows
        return off, rows, slot, s < halvings

    def remote(self, src, dst, send, recv, k):
        return pltpu.make_async_remote_copy(
            src_ref=src, dst_ref=dst, send_sem=send, recv_sem=recv, device_id=(self.mate[k], self.core),
            device_id_type=MESH)

    def first(self, p):
        return self.bit[self.pieces[p]["order"][0]] * (self.pieces[p]["work"].shape[0] // 2)

    def copy(self, p, step):
        kind, s = step
        piece = self.pieces[p]
        k = piece["order"][s]
        if kind == "rs":
            off, rows, slot, halved = self.geometry(p, s)
            source, off = (piece["work"], off) if s == 0 else (piece["kept"], off - self.first(p))
            if halved:
                rows = rows // 2
                off = off + (1 - self.bit[k]) * rows
            return self.remote(
                source.at[pl.ds(pl.multiple_of(off, 16), rows)], piece["recv"].at[pl.ds(slot, rows)],
                self.sems[0].at[p, s], self.sems[1].at[p, s], k)
        off, rows, _, _ = self.geometry(p, s + 1)
        where = piece["out"].at[pl.ds(pl.multiple_of(off, 16), rows)]
        return self.remote(where, where, self.sems[2].at[p, s], self.sems[3].at[p, s], k)

    def arriving(self, p, s):
        off, rows, _, _ = self.geometry(p, s + 1)
        k = self.pieces[p]["order"][s]
        off = off + (1 - 2 * self.bit[k]) * rows
        where = self.pieces[p]["out"].at[pl.ds(pl.multiple_of(off, 16), rows)]
        return self.remote(where, where, self.sems[2].at[p, s], self.sems[3].at[p, s], k)

    def start(self, p):
        self.copy(p, self.steps[p][0]).start()

    def step(self, p, at):
        kind, s = self.steps[p][at]
        if kind == "rs":
            self.add(p, s, self.copy(p, (kind, s)))
        else:
            self.arriving(p, s).wait_recv()
        if at + 1 < len(self.steps[p]):
            self.copy(p, self.steps[p][at + 1]).start()

    def plan(self, p):
        at = self.pos[p]
        if at >= len(self.steps[p]):
            return []
        self.pos[p] = at + 1
        return [(p, at)]

    def advance(self, p):
        for q, at in self.plan(p):
            self.step(q, at)

    def plans(self, wanted):
        return {turn: [step for p in wanted[turn] for step in self.plan(p)] for turn in sorted(wanted)}

    def hook(self, turn, plans):
        for k, steps in plans.items():
            @pl.when(turn == k)
            def _():
                for p, at in steps:
                    self.step(p, at)

    def add(self, p, s, copy):
        piece = self.pieces[p]
        off, rows, slot, halved = self.geometry(p, s)
        if halved:
            copy.wait_recv()
            rows = rows // 2
            off = off + self.bit[piece["order"][s]] * rows
        else:
            copy.wait()
        recv, rel = piece["recv"], off - self.first(p)
        source, at = (piece["work"], off) if s == 0 else (piece["kept"], rel)
        dest, to = (piece["out"], off) if s == self.bits - 1 else (piece["kept"], rel)
        size = 48 if rows % 48 == 0 else 16

        def one(i, _):
            total = source[pl.ds(pl.multiple_of(at + i * size, 16), size), :].astype(F32)
            total = total + recv[pl.ds(pl.multiple_of(slot + i * size, 16), size), :].astype(F32)
            dest[pl.ds(pl.multiple_of(to + i * size, 16), size), :] = total.astype(BF16)
            return 0

        lax.fori_loop(0, rows // size, one, 0)

    def finish(self, p):
        for kind, s in self.steps[p]:
            if kind == "ag" or self.geometry(p, s)[3]:
                self.copy(p, (kind, s)).wait_send()


def halvings_of(rows, bits):
    made = 0
    while made < bits and (rows >> made) % 32 == 0:
        made += 1
    return made


def received_rows(rows, bits):
    halvings, total = halvings_of(rows, bits), 0
    for s in range(bits):
        rows = rows // 2 if s < halvings else rows
        total += rows
    return total


def part(i, size):
    return pl.ds(pl.multiple_of(i * size, size), size)


def at_turns(*groups):
    found = {}
    for turns, pieces in groups:
        for turn in turns:
            found.setdefault(turn, []).extend(pieces)
    return found


class Refs:
    pass


NAMES_IN = ("lengths", "hid_any", "wg_any", "wv_any", "ws_any", "wo_any", "cot_any",
            "gain", "wstep", "tapv", "taps", "bias", "dlog", "skip", "ggain")
NAMES_OUT = ("block_out", "grad_hidden", "ggw_any", "gow_any", "gvw_any", "gsw_any", "tiny_any")


def layer_kernel(reach, bits, names, *refs):
    r = Refs()
    for name, ref in zip(names, refs):
        setattr(r, name, ref)
    length, width = r.hid.shape
    inner = r.wo.shape[0]
    maps = r.ws.shape[1]
    both = inner + maps
    heads = r.dlog.shape[0]
    nblk, nchunk, per = length // TB, length // Q, TB // Q
    me, core, count = lax.axis_index("seq"), lax.axis_index("head"), lax.axis_size("seq")
    base = me * length

    loads = [pltpu.make_async_copy(src, dst, r.load.at[i]) for i, (src, dst) in enumerate(
        ((r.hid_any, r.hid), (r.wv_any, r.wv), (r.ws_any, r.ws), (r.wg_any, r.wg), (r.wo_any, r.wo),
         (r.cot_any, r.cot)))]
    for load in loads:
        load.start()

    swap1 = Swap(reach, r.msgs.at[0], r.msgs.at[1], r.low1, r.high1, r.up_s.at[0], r.up_r.at[0], r.dn_s.at[0], r.dn_r.at[0])
    swap2 = Swap(reach, r.msgs.at[2], r.msgs.at[3], r.low2, r.high2, r.up_s.at[1], r.up_r.at[1], r.dn_s.at[1], r.dn_r.at[1])
    plain = list(range(bits))
    turned = plain[1:2] + plain[:1] + plain[2:]
    groups = inner // 256
    first_state = 2 + groups
    sums = ["ggw", "gow"] + [f"gv{g}" for g in range(groups)] + ["gsw"]
    pieces = [
        dict(work=getattr(r, name + "_w"), kept=getattr(r, name + "_k"), recv=getattr(r, name + "_r"),
             out=getattr(r, name + "_o"), order=turned if i % 2 else plain)
        for i, name in enumerate(sums)
    ]
    red = Reduce(bits, pieces, r.rs_s, r.rs_r, r.ag_s, r.ag_r)
    first = [0, 1]
    barrier = pltpu.get_barrier_semaphore()
    near = swap1.greet(barrier)
    for mate in red.mates:
        pl.semaphore_signal(barrier, inc=1, device_id=(mate, core), device_id_type=MESH)
    pl.semaphore_signal(barrier, inc=1, device_id=(me, 1 - core), device_id_type=MESH)

    def over(src, dst, sems, k):
        return pltpu.make_async_remote_copy(
            src_ref=src, dst_ref=dst, send_sem=sems.at[0, k], recv_sem=sems.at[1, k], device_id=(me, 1 - core),
            device_id_type=MESH)

    def one_sequence(j, carry):
        start, b, off0, after = carry
        end = start + r.lengths[j]
        b = jnp.where((start > base) & (start < base + length), start - base, b)
        off0 = jnp.where((start <= base) & (base < end), base - start, off0)
        after = jnp.where(end == base + length, 0, after)
        return end, b, off0, after

    _, b, off0, after = lax.fori_loop(
        0, r.lengths.shape[0], one_sequence, (jnp.int32(0), jnp.int32(length + 1), jnp.int32(0), jnp.int32(1)))
    before_f = jnp.where(off0 > 0, 1.0, 0.0)
    after_f = after.astype(F32)

    def lanes128(x):
        return jnp.concatenate([x, jnp.zeros((x.shape[0], 128 - x.shape[1]), F32)], axis=1)

    small_cols = jnp.concatenate(
        [lanes128(r.bias[...]), lanes128(r.dlog[...].reshape(1, heads)), lanes128(r.skip[...].reshape(1, heads)),
         jnp.zeros((4, 128), F32)], axis=0).T
    bias = jnp.concatenate([small_cols[:HP, 0:1], small_cols[:HP, 1:2]], axis=0)
    dlog = jnp.concatenate([small_cols[:HP, 2:3], small_cols[:HP, 2:3]], axis=0)
    spread = spread_matrix(inner, inner // heads)
    spread_low = spread.astype(BF16)
    spread2 = jnp.concatenate([spread_low, spread_low], axis=0)
    skip = widen_col(small_cols[:HP, 3:4], spread)
    gain = r.gain[...].reshape(1, width)
    ggain = r.ggain[...].reshape(1, inner)
    r.wst[...] = jnp.zeros_like(r.wst)
    wstep = r.wstep[...].astype(F32)
    for k in range(2):
        r.wst[k * HP : (k + 1) * HP, :] = jnp.concatenate(
            [wstep[:, k, :], jnp.zeros((HP - heads, width), F32)], axis=0).astype(BF16)

    loads[0].wait()
    loads[1].wait()
    loads[2].wait()

    def normalize(x):
        x = x.astype(F32)
        scale = lax.rsqrt(jnp.mean(x * x, axis=1, keepdims=True) + EPSILON)
        return (x * scale * gain).astype(BF16)

    def project(blk, _):
        rows = part(blk, TB)
        normed = normalize(r.hid[rows, :])
        r.buf[rows, :] = normed
        r.normt[:, rows] = normed.T
        dest = pl.ds(pl.multiple_of(16 + blk * TB, 16), TB)
        r.joined[dest, :inner] = nn(normed, r.wv[...]).astype(BF16)
        r.joined[dest, inner:] = nn(normed, r.ws[...]).astype(BF16)
        r.step[:, rows] = nt(r.wst[...], normed)
        return 0

    lax.fori_loop(0, nblk, project, 0)

    pl.semaphore_wait(barrier, near + bits + 1)

    def halo_copy(to):
        return pltpu.make_async_remote_copy(
            src_ref=r.hid.at[pl.ds(length - 16, 16)], dst_ref=r.halo, send_sem=r.edge.at[0], recv_sem=r.edge.at[1],
            device_id=(to, core), device_id_type=MESH)

    @pl.when(me + 1 < count)
    def _():
        halo_copy(me + 1).start()

    @pl.when(me == 0)
    def _():
        r.halo[...] = jnp.zeros_like(r.halo)

    def conv_rows(blk, cols, c0, masks, width_now):
        r.jx[...] = r.joined[pl.ds(pl.multiple_of(blk * TB, 16), TB + 16), cols].astype(F32)
        shifted = [r.jx[16 : 16 + TB, :]]
        tap = r.tap[:, cols]
        total = shifted[0] * tap[3:4]
        for m in range(1, 4):
            shifted.append(r.jx[16 - m : 16 - m + TB, :] * masks[m])
            total = total + shifted[m] * tap[3 - m : 4 - m]
        return shifted, tap, total

    r.tap[:, :inner] = r.tapv[...]
    r.tap[:, inner:] = r.taps[...]

    def chunk_parts(chunk):
        cols = part(chunk, Q)
        return step_parts(r.step[:, cols], bias, dlog)

    def summarize(blk, _):
        rows = part(blk, TB)
        tok = iota((TB, 1), 0) + blk * TB
        masks = [conv_mask(tok, m, b, off0) for m in range(4)]
        for g in range(both // 256):
            cols = slice(g * 256, (g + 1) * 256)
            _, _, total = conv_rows(blk, cols, g * 256, masks, 256)
            r.act[rows, cols] = silu(total).astype(BF16)
        for q in range(per):
            chunk = blk * per + q
            t0 = chunk * Q
            at = part(chunk, Q)
            dt, ld, run, bef = chunk_parts(chunk)
            _, _, tf, tr = state_factors(dt, run, bef, t0, b)
            values = r.act[at, :inner].astype(F32)
            maps_t = r.act[at, inner:].astype(F32).T.astype(BF16)
            r.inc[chunk, 0:64, :] = nn(maps_t[0:64], (values * widen(tf, spread2)).astype(BF16))
            r.inc[chunk, 64:128, :] = nn(maps_t[128:192], (values * widen(tr, spread2)).astype(BF16))
            gone = jnp.exp(run[:, Q - 1 : Q])
            r.pexp[chunk, 0:1, :] = widen_col(gone[:HP], spread) * jnp.where((t0 <= b) & (b < t0 + Q), 0.0, 1.0)
            r.pexp[chunk, 1:2, :] = widen_col(gone[HP:], spread) * jnp.where((t0 < b) & (b <= t0 + Q), 0.0, 1.0)
        return 0

    lax.fori_loop(1, nblk, summarize, 0)

    @pl.when(me > 0)
    def _():
        halo_copy(me + 1).wait_recv()

    nh = normalize(r.halo[...])
    r.joined[0:16, :inner] = nn(nh, r.wv[...]).astype(BF16)
    r.joined[0:16, inner:] = nn(nh, r.ws[...]).astype(BF16)
    summarize(jnp.int32(0), 0)
    sumf, prodf = r.inc[0, 0:64, :], r.pexp[0, 0:1, :]
    sumr, prodr = r.inc[nchunk - 1, 64:128, :], r.pexp[nchunk - 1, 1:2, :]
    for c in range(1, nchunk):
        d = nchunk - 1 - c
        pf, pr = r.pexp[c, 0:1, :], r.pexp[d, 1:2, :]
        sumf, prodf = pf * sumf + r.inc[c, 0:64, :], prodf * pf
        sumr, prodr = pr * sumr + r.inc[d, 64:128, :], prodr * pr
    put_message(r.msgs.at[0], sumf, prodf * before_f)
    put_message(r.msgs.at[1], sumr, prodr * after_f)
    swap1.start()

    loads[3].wait()
    tri0, tri1 = iota((Q, Q), 0), iota((Q, Q), 1)
    lower, upper = tri0 > tri1, tri0 < tri1

    def within(blk, _):
        rows = part(blk, TB)
        r.gate[rows, :] = nn(r.buf[rows, :], r.wg[...])
        for q in range(per):
            chunk = blk * per + q
            at = part(chunk, Q)
            t0 = chunk * Q
            dt, ld, run, bef = chunk_parts(chunk)
            ldt = jnp.log(jnp.maximum(dt, 1e-37))
            rowf = ldt[:HP] - run[:HP]
            rowr = ldt[HP:] + bef[HP:]
            cols = jnp.concatenate([bef[:HP], -run[HP:]], axis=0).T
            scores = chunk_scores(r.act[at, inner:], t0, b)
            for j in range(inner // 128):
                lanes = slice(j * 128, (j + 1) * 128)
                weights = []
                for h in (2 * j, 2 * j + 1):
                    e = jnp.where(lower, cols[:, h : h + 1] + rowf[h : h + 1],
                                  cols[:, HP + h : HP + h + 1] + rowr[h : h + 1])
                    weights.append((jnp.exp(jnp.minimum(e, 60.0)) * scores).astype(BF16))
                vp = r.act[at, lanes]
                y = nn(jnp.concatenate(weights, axis=1), halves(vp))
                r.mixed[at, lanes] = y + skip[:, lanes] * vp.astype(F32)
        return 0

    lax.fori_loop(0, nblk, within, 0)
    loads[4].wait()
    loads[5].wait()
    swap1.finish()
    hf = chain(r.low1) * before_f
    hr = chain(r.high1) * after_f
    for c in range(nchunk):
        r.state[c, 0:64, :] = hf.astype(BF16)
        hf = r.pexp[c, 0:1, :] * hf + r.inc[c, 0:64, :]
        d = nchunk - 1 - c
        r.state[d, 64:128, :] = hr.astype(BF16)
        hr = r.pexp[d, 1:2, :] * hr + r.inc[d, 64:128, :]

    def enter(blk, _):
        lane = iota((Q, 128), 1)
        u_all = nt(r.cot[part(blk, TB), :], r.wo[...])
        for q in range(per):
            chunk = blk * per + q
            at = part(chunk, Q)
            dt, ld, run, bef = chunk_parts(chunk)
            ef, er, _, _ = state_factors(dt, run, bef, chunk * Q, b)
            maps_here = r.act[at, inner:]
            state = r.state[chunk]
            ys = nn(maps_here[:, 64:128], state[0:64]) * widen(ef, spread2)
            ys = ys + nn(maps_here[:, 192:256], state[64:128]) * widen(er, spread2)
            square = jnp.zeros((Q, 1), F32)
            cross = jnp.zeros((Q, 1), F32)
            for j in range(inner // 128):
                lanes = slice(j * 128, (j + 1) * 128)
                y = r.mixed[at, lanes] + ys[:, lanes]
                r.mixed[at, lanes] = y
                gated = y * silu(r.gate[at, lanes])
                square = square + jnp.sum(gated * gated, axis=1, keepdims=True)
                cross = cross + jnp.sum(
                    gated * (u_all[q * Q : (q + 1) * Q, lanes] * ggain[:, lanes]), axis=1, keepdims=True)
            two = jnp.where(lane == 0, square, jnp.where(lane == 1, cross, 0.0))
            r.mine[blk, :, q * Q : (q + 1) * Q] = two.T[0:8]
        over(r.mine.at[blk], r.other.at[blk], r.sum_sem, blk).start()
        return 0

    lax.fori_loop(0, nblk, enter, 0)
    r.small[...] = jnp.zeros_like(r.small)

    def gating(blk, _):
        rows = part(blk, TB)
        over(r.mine.at[blk], r.other.at[blk], r.sum_sem, blk).wait()
        sums = r.mine[blk] + r.other[blk]
        sums = jnp.concatenate([sums, jnp.zeros((120, TB), F32)], axis=0).T
        scale = lax.rsqrt(sums[:, 0:1] / (2 * inner) + EPSILON)
        back = scale * scale * scale * sums[:, 1:2] / (2 * inner)
        gng = nt(r.cot[rows, :], r.wo[...])
        for j in range(inner // 128):
            lanes = slice(j * 128, (j + 1) * 128)
            mixed = r.mixed[rows, lanes]
            pre = r.gate[rows, lanes]
            sig = jax.nn.sigmoid(pre)
            gated = mixed * (pre * sig)
            ng = gated * scale
            r.buf[rows, lanes] = (ng * ggain[:, lanes]).astype(BF16)
            g = gng[:, lanes]
            r.small[0:1, lanes] += jnp.sum(g * ng, axis=0, keepdims=True)
            grad_gated = scale * (g * ggain[:, lanes]) - gated * back
            dy = grad_gated * (pre * sig)
            r.small[1:2, lanes] += jnp.sum(dy * r.act[rows, lanes].astype(F32), axis=0, keepdims=True)
            r.dy[rows, lanes] = dy
            r.ggate[rows, lanes] = (grad_gated * mixed * (sig * (1.0 + pre * (1.0 - sig)))).astype(BF16)
        r.out_mine[rows, :] = nn(r.buf[rows, :], r.wo[...]).astype(BF16)
        over(r.out_mine.at[rows], r.out_other.at[rows], r.out_sem, blk).start()
        for q in range(per):
            chunk = blk * per + q
            at = part(chunk, Q)
            dt, ld, run, bef = chunk_parts(chunk)
            ef, er, _, _ = state_factors(dt, run, bef, chunk * Q, b)
            maps_t = r.act[at, inner:].astype(F32).T.astype(BF16)
            dy = r.dy[at, :]
            r.inc[chunk, 0:64, :] = nn(maps_t[64:128], (dy * widen(ef, spread2)).astype(BF16))
            r.inc[chunk, 64:128, :] = nn(maps_t[192:256], (dy * widen(er, spread2)).astype(BF16))
        return 0

    lax.fori_loop(0, nblk, gating, 0)
    sumf, sumr = r.inc[nchunk - 1, 0:64, :], r.inc[0, 64:128, :]
    for c in range(1, nchunk):
        d = nchunk - 1 - c
        sumf = r.pexp[d, 0:1, :] * sumf + r.inc[d, 0:64, :]
        sumr = r.pexp[c, 1:2, :] * sumr + r.inc[c, 64:128, :]
    put_message(r.msgs.at[2], sumr * after_f, prodr * after_f)
    put_message(r.msgs.at[3], sumf * before_f, prodf * before_f)
    swap2.start()
    r.ggw_w[...] = nn(r.normt[...], r.ggate[...]).astype(BF16)
    red.start(0)
    r.gow_w[...] = tn(r.buf[...], r.cot[...]).astype(BF16)
    red.start(1)

    sums_low = jnp.concatenate([lower, upper], axis=1).astype(BF16)
    diag = tri0 == tri1
    r.rowbuf[...] = jnp.zeros_like(r.rowbuf)

    plans_within = red.plans(at_turns((G1_WITHIN, first)))

    def back_within(blk, _):
        for q in range(per):
            chunk = blk * per + q
            at = part(chunk, Q)
            t0 = chunk * Q
            dt, ld, run, bef = chunk_parts(chunk)
            ldt = jnp.log(jnp.maximum(dt, 1e-37))
            cols = jnp.concatenate([ldt[:HP] - run[:HP], ldt[HP:] + bef[HP:]], axis=0).T
            rowf, rowr = bef[:HP], -run[HP:]
            m = r.act[at, inner:]
            entf, readf, entr, readr = m[:, 0:64], m[:, 64:128], m[:, 128:192], m[:, 192:256]
            same = (tri0 + t0 < b) == (tri1 + t0 < b)
            okf, okr = upper & same, lower & same
            scores = jnp.where(okf, nt(entf, readf), jnp.where(okr, nt(entr, readr), 0.0))
            dscore = jnp.zeros((Q, Q), F32)
            for j in range(inner // 128):
                lanes = slice(j * 128, (j + 1) * 128)
                vp = r.act[at, lanes]
                dyp32 = r.dy[at, lanes]
                dyp = dyp32.astype(BF16)
                dw = nt(halves(vp), dyp)
                weights = []
                for i, h in enumerate((2 * j, 2 * j + 1)):
                    e = jnp.where(upper, cols[:, h : h + 1] + rowf[h : h + 1],
                                  cols[:, HP + h : HP + h + 1] + rowr[h : h + 1])
                    x = jnp.exp(jnp.minimum(e, 60.0))
                    weights.append((x * scores).astype(BF16))
                    dwx = dw[i * Q : (i + 1) * Q] * x
                    dscore = dscore + dwx
                    sums = nn((dwx * scores).astype(BF16), sums_low)
                    pf, pr = sums[:, :Q], sums[:, Q:]
                    for place, kept in enumerate((jnp.where(upper, pf, 0.0), jnp.where(lower, pr, 0.0),
                                                  jnp.where(diag, pf, 0.0), jnp.where(diag, pr, 0.0))):
                        r.rowbuf[chunk, place * HP + h : place * HP + h + 1, :] = jnp.sum(kept, axis=0, keepdims=True)
                dv = nn(jnp.concatenate(weights, axis=1), halves(dyp))
                r.mixed[at, lanes] = dv + dyp32 * skip[:, lanes]
            dsf = jnp.where(okf, dscore, 0.0)
            dsr = jnp.where(okr, dscore, 0.0)
            r.mixed[at, inner:] = jnp.concatenate(
                [nn(dsf.astype(BF16), readf), nn(dsf.T.astype(BF16), entf),
                 nn(dsr.astype(BF16), readr), nn(dsr.T.astype(BF16), entr)], axis=1)

        red.hook(blk, plans_within)
        return 0

    lax.fori_loop(0, nblk, back_within, 0)
    swap2.finish()
    df = chain(r.high2)
    dr = chain(r.low2)
    for c in range(nchunk):
        d = nchunk - 1 - c
        r.dstate[d, 0:64, :] = df.astype(BF16)
        df = r.pexp[d, 0:1, :] * df + r.inc[d, 0:64, :]
        r.dstate[c, 64:128, :] = dr.astype(BF16)
        dr = r.pexp[c, 1:2, :] * dr + r.inc[c, 64:128, :]
    r.cg_mine[...] = jnp.zeros_like(r.cg_mine)
    r.hsum[...] = jnp.zeros_like(r.hsum)

    def lent_copy(to):
        return pltpu.make_async_remote_copy(
            src_ref=r.lent_mine, dst_ref=r.lent_other, send_sem=r.edge.at[2], recv_sem=r.edge.at[3],
            device_id=(to, core), device_id_type=MESH)

    lower32, upper32 = lower.astype(F32), upper.astype(F32)

    plans_states = red.plans(at_turns((G1_STATES, first)))

    def back_states(blk, _):
        for q in range(per):
            chunk = blk * per + q
            at = part(chunk, Q)
            dt, ld, run, bef = chunk_parts(chunk)
            ef, er, tf, tr = state_factors(dt, run, bef, chunk * Q, b)
            m = r.act[at, inner:]
            entf, readf, entr, readr = m[:, 0:64], m[:, 64:128], m[:, 128:192], m[:, 192:256]
            state = r.state[chunk]
            grad_state = r.dstate[chunk]
            dy = r.dy[at, :]
            values = r.act[at, :inner].astype(F32)
            dyf, dyr = dy * widen(ef, spread2), dy * widen(er, spread2)
            dreadf = nt(dyf.astype(BF16), state[0:64])
            dreadr = nt(dyr.astype(BF16), state[64:128])
            qf = nt(spread_low, (nn(readf, state[0:64]) * dyf).astype(BF16))
            qr = nt(spread_low, (nn(readr, state[64:128]) * dyr).astype(BF16))
            tfe, tre = widen(tf, spread2), widen(tr, spread2)
            dvf = nn(entf, grad_state[0:64]) * tfe
            dvr = nn(entr, grad_state[64:128]) * tre
            wf = nt(spread_low, (values * dvf).astype(BF16))
            wr = nt(spread_low, (values * dvr).astype(BF16))
            dentf = nt((values * tfe).astype(BF16), grad_state[0:64])
            dentr = nt((values * tre).astype(BF16), grad_state[64:128])
            through = state.astype(F32) * grad_state.astype(F32)
            zf = jnp.sum(through[0:64], axis=0, keepdims=True) * r.pexp[chunk, 0:1, :]
            zr = jnp.sum(through[64:128], axis=0, keepdims=True) * r.pexp[chunk, 1:2, :]
            zf = nt(spread, jnp.broadcast_to(zf, (8, inner)), HIGHEST)[:, 0:1]
            zr = nt(spread, jnp.broadcast_to(zr, (8, inner)), HIGHEST)[:, 0:1]
            r.mixed[at, :inner] = r.mixed[at, :inner] + dvf + dvr
            r.mixed[at, inner:] = r.mixed[at, inner:] + jnp.concatenate([dentf, dreadf, dentr, dreadr], axis=1)
            late = nn(jnp.concatenate([qf, wr], axis=0), lower32, HIGHEST)
            early = nn(jnp.concatenate([wf, qr], axis=0), upper32, HIGHEST)
            rowsum = r.rowbuf[chunk]
            dld = jnp.concatenate(
                [rowsum[0:HP] + late[:HP] + early[:HP] + zf, rowsum[HP : 2 * HP] + late[HP:] + early[HP:] + zr], axis=0)
            dldt = rowsum[2 * HP : 4 * HP] + jnp.concatenate([wf, wr], axis=0)
            sig = jax.nn.sigmoid(r.step[:, at] + bias)
            ratio = jnp.where(dt < 1e-30, 1.0, sig / jnp.maximum(dt, 1e-30))
            graw = dldt * ratio - jnp.exp(dlog) * sig * dld
            r.gstep[:, at] = graw.astype(BF16)
            r.hsum[:, 0:1] += jnp.sum(graw, axis=1, keepdims=True)
            r.hsum[:, 1:2] += jnp.sum(dld * ld, axis=1, keepdims=True)

        @pl.when(blk == 0)
        def _():
            tok8 = iota((8, 1), 0)
            masks = [conv_mask(tok8, m, b, off0) for m in range(4)]
            rows = r.joined[0:32, :].astype(F32)
            tap = r.tap[...]
            total = rows[16:24] * tap[3:4]
            for m in range(1, 4):
                total = total + rows[16 - m : 24 - m] * masks[m] * tap[3 - m : 4 - m]
            sig = jax.nn.sigmoid(total)
            dconv = r.mixed[0:8, :] * (sig * (1.0 + total * (1.0 - sig)))
            first = jnp.concatenate([jnp.zeros((8, both), F32), dconv], axis=0)
            lent = jnp.zeros((8, both), F32)
            for m in range(1, 4):
                lent = lent + first[m : m + 8] * conv_mask(tok8 - 8 + m, m, b, off0) * tap[3 - m : 4 - m]
            r.lent_mine[...] = lent

            @pl.when(me > 0)
            def _():
                lent_copy(me - 1).start()

        red.hook(blk, plans_states)
        return 0

    lax.fori_loop(0, nblk, back_states, 0)

    @pl.when(me + 1 < count)
    def _():
        lent_copy(me - 1).wait_recv()

    @pl.when(me + 1 == count)
    def _():
        r.lent_other[...] = jnp.zeros_like(r.lent_other)

    r.dbuf[length : length + 8, :] = jnp.zeros((8, 256), F32)

    def back_conv(g):
        cols = slice(g * 256, (g + 1) * 256)

        def one(i, _):
            blk = nblk - 1 - i
            rows = part(blk, TB)
            tok = iota((TB, 1), 0) + blk * TB
            masks = [conv_mask(tok, m, b, off0) for m in range(4)]
            later = [conv_mask(tok + m, m, b, off0) for m in range(4)]
            shifted, tap, total = conv_rows(blk, cols, g * 256, masks, 256)
            sig = jax.nn.sigmoid(total)
            dconv = r.mixed[rows, cols] * (sig * (1.0 + total * (1.0 - sig)))
            r.dbuf[rows, :] = dconv
            for m in range(4):
                r.cg_mine[3 - m : 4 - m, cols] += jnp.sum(dconv * shifted[m], axis=0, keepdims=True)
            grad = dconv * tap[3:4]
            ahead = r.dbuf[pl.ds(pl.multiple_of(blk * TB, TB), TB + 8), :]
            for m in range(1, 4):
                grad = grad + ahead[m : m + TB] * later[m] * tap[3 - m : 4 - m]
            last = jnp.where(blk == nblk - 1, 1.0, 0.0)
            grad = jnp.concatenate([grad[: TB - 8], grad[TB - 8 :] + r.lent_other[:, cols] * last], axis=0)
            if g * 256 < inner:
                r.buf[rows, cols] = grad.astype(BF16)
            else:
                r.gs_mine[rows, :] = grad.astype(BF16)
            return 0

        lax.fori_loop(0, nblk, one, 0)

    back_conv(inner // 256)
    gs_copy = over(r.gs_mine, r.gs_other, r.misc_sem, 0)
    gs_copy.start()
    cg_copy = over(r.cg_mine.at[:, pl.ds(inner, maps)], r.cg_other, r.misc_sem, 1)
    cg_copy.start()
    for g in range(inner // 256):
        cols = slice(g * 256, (g + 1) * 256)
        back_conv(g)
        pieces[2 + g]["work"][...] = nn(r.normt[...], r.buf[:, cols]).astype(BF16)
        red.start(2 + g)
        if g in G1_CONV:
            red.advance(0)
            red.advance(1)
    gs_copy.wait()
    cg_copy.wait()
    r.gs[...] = (r.gs_mine[...].astype(F32) + r.gs_other[...].astype(F32)).astype(BF16)
    r.gsw_w[:, :maps] = nn(r.normt[...], r.gs[...]).astype(BF16)
    gstep = jnp.concatenate([r.gstep[...].astype(F32), jnp.zeros((128 - 2 * HP, length), F32)], axis=0)
    r.gsw_w[:, maps:] = nt(r.normt[...], gstep.astype(BF16)).astype(BF16)
    red.start(first_state)

    later_pieces = list(range(2, len(pieces)))

    plans_down = red.plans(at_turns((G1_DOWN, first), (G2_DOWN, later_pieces)))

    def down(blk, _):
        rows = part(blk, TB)
        gn = nt(r.ggate[rows, :], r.wg[...]) + nt(r.buf[rows, :], r.wv[...]) + tn(r.gstep[:, rows], r.wst[...])
        r.gn_mine[rows, :] = gn.astype(BF16)
        over(r.gn_mine.at[rows], r.gn_other.at[rows], r.gn_sem, blk).start()
        red.hook(blk, plans_down)
        return 0

    lax.fori_loop(0, nblk, down, 0)
    tiny = r.tiny_w.at[0]
    tiny[...] = jnp.zeros((16, both), F32)
    tiny[0:2, :inner] = r.small[0:2, :]
    tiny[4:6, 0 : 2 * HP] = r.hsum[...].T[0:2]
    tiny[8:16, :inner] = r.cg_mine[:, :inner]
    tiny[8:16, inner:] = r.cg_mine[:, inner:] + r.cg_other[...]

    def out_copy(blk):
        rows = part(blk, TB)
        return (pltpu.make_async_copy(r.out_other.at[rows], r.block_out.at[rows], r.store.at[0, blk]),
                pltpu.make_async_copy(r.gate.at[rows], r.grad_hidden.at[rows], r.store.at[1, blk]))

    plans_end = red.plans(at_turns((G1_END, first), (G2_END, later_pieces)))

    def ending(blk, _):
        rows = part(blk, TB)
        over(r.out_mine.at[rows], r.out_other.at[rows], r.out_sem, blk).wait()
        over(r.gn_mine.at[rows], r.gn_other.at[rows], r.gn_sem, blk).wait()
        x = r.hid[rows, :].astype(F32)
        r.out_other[rows, :] = (
            x + (r.out_mine[rows, :].astype(F32) + r.out_other[rows, :].astype(F32))).astype(BF16)
        gn = r.gn_mine[rows, :].astype(F32) + r.gn_other[rows, :].astype(F32) + nt(r.gs[rows, :], r.ws[...])
        scale = lax.rsqrt(jnp.mean(x * x, axis=1, keepdims=True) + EPSILON)
        tiny[2:3, :width] += jnp.sum(gn * x * scale, axis=0, keepdims=True)
        v = gn * gain
        mean = jnp.mean(x * v, axis=1, keepdims=True)
        r.gate[rows, :] = r.cot[rows, :].astype(F32) + scale * v - x * (scale * scale * scale * mean)
        for copy in out_copy(blk):
            copy.start()
        red.hook(blk, plans_end)
        return 0

    lax.fori_loop(0, nblk, ending, 0)

    def tiny_copy(s):
        return pltpu.make_async_remote_copy(
            src_ref=r.tiny_w.at[s], dst_ref=r.tiny_r.at[s], send_sem=r.tiny_sem.at[0, s],
            recv_sem=r.tiny_sem.at[1, s], device_id=(red.mates[s], core), device_id_type=MESH)

    tiny_copy(0).start()
    for s in range(bits):
        tiny_copy(s).wait()
        r.tiny_w[s + 1] = r.tiny_w[s] + r.tiny_r[s]
        if s + 1 < bits:
            tiny_copy(s + 1).start()
        for p in range(len(pieces)):
            red.advance(p)
    stores = [
        pltpu.make_async_copy(src, dst, r.store.at[2, i]) for i, (src, dst) in enumerate(
            ((r.ggw_o, r.ggw_any), (r.gow_o, r.gow_any), (r.gsw_o, r.gsw_any),
             *((pieces[2 + g]["out"], r.gvw_any.at[:, pl.ds(g * 256, 256)]) for g in range(groups)),
             (r.tiny_w.at[bits], r.tiny_any)))]
    stores[-1].start()
    while any(red.pos[p] < len(red.steps[p]) for p in range(len(pieces))):
        for p in range(len(pieces)):
            red.advance(p)
    for p in range(len(pieces)):
        red.finish(p)
    for store in stores[:-1]:
        store.start()
    for store in stores:
        store.wait()
    for blk in range(nblk):
        for copy in out_copy(blk):
            copy.wait()

    @pl.when(me + 1 < count)
    def _():
        halo_copy(me + 1).wait_send()

    @pl.when(me > 0)
    def _():
        lent_copy(me - 1).wait_send()


G1_WITHIN = (2, 3)
G1_STATES = (1, 2, 3)
G1_CONV = (1, 2)
G1_DOWN = (1, 3)
G2_DOWN = (2,)
G1_END = ()
G2_END = (0, 2)


def last_kernel(heads, ggw_ref, gow_ref, gvw_ref, gsw_ref, tiny_ref,
                ngain_ref, ggwo_ref, gvwo_ref, gswo_ref, gsteo_ref, convv_ref, convs_ref, bias_ref, decay_ref,
                skip_ref, ggain_ref, gowo_ref):
    ggwo_ref[...] = ggw_ref[...].astype(F32)
    gvwo_ref[...] = gvw_ref[...].astype(F32)
    maps = gswo_ref.shape[1]
    gswo_ref[...] = gsw_ref[:, :maps].astype(F32)
    step = gsw_ref[:, maps:].astype(F32).T
    gsteo_ref[...] = jnp.stack([step[:heads], step[HP : HP + heads]], axis=1)
    gowo_ref[...] = gow_ref[...].astype(F32)

    @pl.when(pl.program_id(0) == 0)
    def _():
        width, inner = ngain_ref.shape[0], convv_ref.shape[1]
        ngain_ref[...] = tiny_ref[2, :width]
        ggain_ref[...] = tiny_ref[0, :inner]
        convv_ref[...] = tiny_ref[8:12, :inner]
        convs_ref[...] = tiny_ref[8:12, inner:]
        bias_ref[...] = jnp.concatenate([tiny_ref[4:5, 0:heads], tiny_ref[4:5, HP : HP + heads]], axis=0)
        decay_ref[...] = (tiny_ref[5:6, 0:heads] + tiny_ref[5:6, HP : HP + heads]).reshape(heads)
        spread = spread_matrix(inner, inner // heads)
        total = nt(jnp.broadcast_to(tiny_ref[1:2, :inner], (8, inner)), spread, HIGHEST)
        skip_ref[...] = total[0:1, :heads].reshape(heads)


SMEM_SPEC = pl.BlockSpec(memory_space=pltpu.SMEM)
VMEM_SPEC = pl.BlockSpec(memory_space=pltpu.VMEM)
ANY_SPEC = pl.BlockSpec(memory_space=pl.ANY)


def body(
    hidden_in, norm_gain, gate_proj, value_proj, state_proj, step_proj, conv_value, conv_state,
    step_bias, decay_log, skip_scale, gate_gain, out_proj, lengths, cotangent,
):
    length, width = hidden_in.shape
    inner = gate_proj.shape[1]
    heads = decay_log.shape[0]
    maps = state_proj.shape[1]
    both = inner + maps
    nblk, nchunk = length // TB, length // Q
    count = lax.axis_size("seq")
    bits = count.bit_length() - 1
    assert count == 1 << bits
    reach = min(1 + (LEN_MOST - 2) // length, count - 1)
    npieces = 3 + inner // 256

    def vmem(*dims, dtype=F32):
        return pltpu.VMEM(dims, dtype)

    dma = pltpu.SemaphoreType.DMA
    low = dict(dtype=BF16)
    scratch = dict(
        hid=vmem(length, width, **low), wg=vmem(width, inner, **low), wv=vmem(width, inner, **low),
        ws=vmem(width, maps, **low), wo=vmem(inner, width, **low), cot=vmem(length, width, **low),
        wst=vmem(2 * HP, width, **low), tap=vmem(4, both),
        normt=vmem(width, length, **low), buf=vmem(length, inner, **low), gate=vmem(length, inner),
        joined=vmem(16 + length, both, **low), act=vmem(length, both, **low), step=vmem(2 * HP, length),
        inc=vmem(nchunk, 128, inner), pexp=vmem(nchunk, 2, inner), mixed=vmem(length, both),
        state=vmem(nchunk, 128, inner, **low), dstate=vmem(nchunk, 128, inner, **low),
        dy=vmem(length, inner), ggate=vmem(length, inner, **low), gstep=vmem(2 * HP, length, **low),
        msgs=vmem(4, 80, inner, **low),
        low1=vmem(reach, 80, inner, **low), high1=vmem(reach, 80, inner, **low),
        low2=vmem(reach, 80, inner, **low), high2=vmem(reach, 80, inner, **low),
        rowbuf=vmem(nchunk, 4 * HP, Q), jx=vmem(TB + 16, 256), dbuf=vmem(length + 8, 256),
        halo=vmem(16, width, **low), mine=vmem(nblk, 8, TB), other=vmem(nblk, 8, TB),
        out_mine=vmem(length, width, **low), out_other=vmem(length, width, **low),
        gn_mine=vmem(length, width, **low), gn_other=vmem(length, width, **low),
        gs_mine=vmem(length, maps, **low), gs_other=vmem(length, maps, **low), gs=vmem(length, maps, **low),
        lent_mine=vmem(8, both), lent_other=vmem(8, both), cg_mine=vmem(8, both), cg_other=vmem(8, maps),
        hsum=vmem(2 * HP, 128), small=vmem(8, inner),
        tiny_w=vmem(bits + 1, 16, both), tiny_r=vmem(bits, 16, both),
    )
    for name, rows, cols in (("ggw", width, inner), ("gow", inner, width), ("gsw", width, maps + 128), *((f"gv{g}", width, 256) for g in range(inner // 256))):
        scratch[name + "_w"] = vmem(rows, cols, **low)
        scratch[name + "_k"] = vmem(rows // 2, cols, **low)
        scratch[name + "_r"] = vmem(received_rows(rows, bits), cols, **low)
        scratch[name + "_o"] = vmem(rows, cols, **low)
    scratch.update(
        load=dma((6,)), store=dma((3, max(nblk, 4 + inner // 256))), edge=dma((4,)), sum_sem=dma((2, nblk)), out_sem=dma((2, nblk)),
        gn_sem=dma((2, nblk)), misc_sem=dma((2, 2)), tiny_sem=dma((2, bits)),
        up_s=dma((2, reach)), up_r=dma((2, reach)), dn_s=dma((2, reach)), dn_r=dma((2, reach)),
        rs_s=dma((npieces, bits)), rs_r=dma((npieces, bits)), ag_s=dma((npieces, bits)), ag_r=dma((npieces, bits)),
    )

    def shape(*dims, dtype=F32):
        return jax.ShapeDtypeStruct(dims, dtype)

    outs = pl.pallas_call(
        partial(layer_kernel, reach, bits, NAMES_IN + NAMES_OUT + tuple(scratch)),
        in_specs=[SMEM_SPEC] + [ANY_SPEC] * 6 + [VMEM_SPEC] * 8,
        out_specs=[ANY_SPEC] * 7,
        out_shape=[shape(length, width, **low), shape(length, width), shape(width, inner, **low),
                   shape(inner, width, **low), shape(width, inner, **low), shape(width, maps + 128, **low),
                   shape(16, both)],
        scratch_shapes=list(scratch.values()),
        compiler_params=pltpu.CompilerParams(
            collective_id=1, has_side_effects=True, vmem_limit_bytes=VMEM_LIMIT),
    )(lengths, hidden_in, gate_proj, value_proj, state_proj, out_proj, cotangent,
      norm_gain, step_proj.transpose(2, 0, 1), conv_value, conv_state, step_bias, decay_log, skip_scale, gate_gain)
    block_out, grad_hidden, ggw, gow, gvw, gsw, tiny = outs

    rows = 128
    def tall(cols):
        return pl.BlockSpec((rows, cols), lambda i: (i, 0))

    def whole(*dims):
        return pl.BlockSpec(dims, lambda i: (0,) * len(dims))

    assert width % rows == 0 and inner % rows == 0 and inner == width
    final = pl.pallas_call(
        partial(last_kernel, heads),
        grid=(width // rows,),
        in_specs=[tall(inner), tall(width), tall(inner), tall(maps + 128), whole(16, both)],
        out_specs=[whole(width), tall(inner), tall(inner), tall(maps), pl.BlockSpec((heads, 2, rows), lambda i: (0, 0, i)), whole(4, inner),
                   whole(4, maps), whole(2, heads), whole(heads), whole(heads), whole(inner), tall(width)],
        out_shape=[shape(width), shape(width, inner), shape(width, inner), shape(width, maps),
                   shape(heads, 2, width), shape(4, inner), shape(4, maps), shape(2, heads), shape(heads),
                   shape(heads), shape(inner), shape(inner, width)],
        compiler_params=pltpu.CompilerParams(dimension_semantics=("arbitrary",), vmem_limit_bytes=60 * MIB),
    )(ggw, gow, gvw, gsw, tiny)
    ngain, ggw, gvw, gsw, gstepw, convv, convs, bias, decay, skip, ggain, gow = final
    return (block_out, grad_hidden, ngain, ggw, gvw, gsw, gstepw.transpose(1, 2, 0), convv, convs, bias, decay, skip,
            ggain, gow)


def solution(mesh):
    in_specs = (
        P("seq", None),
        P(),
        P(None, "head"),
        P(None, "head"),
        P(),
        P(None, None, "head"),
        P(None, "head"),
        P(),
        P(None, "head"),
        P("head"),
        P("head"),
        P("head"),
        P("head", None),
        P(),
        P("seq", None),
    )
    out_specs = (
        P("seq", None),
        P("seq", None),
        P(),
        P(None, "head"),
        P(None, "head"),
        P(),
        P(None, None, "head"),
        P(None, "head"),
        P(),
        P(None, "head"),
        P("head"),
        P("head"),
        P("head"),
        P("head", None),
    )
    return jax.shard_map(body, mesh=mesh, in_specs=in_specs, out_specs=out_specs, check_vma=False)
```

time: 1760 us -> 210 us (0.12); the launches traced: 1730 us -> 210 us
  local copies, waits for them, and re-layouts: 639 us -> 4.12 us
  other arithmetic: 312 us -> 0 us
  waiting for transfers between devices: 309 us -> 0 us
  matrix products: 293 us -> 0 us
  Pallas kernels: 0 us -> 205 us
  blocking collectives: 126 us -> 0 us
  loops' own time: 24.9 us -> 0 us
  between operations: 19.1 us -> 0.69 us
    dynamic_update_slice x104 -> x0, local copies, waits for them, and re-layouts: 378 us -> none  [device_local(): lax.scan(jax.checkpoint(group_step), (zero_state, seg_before), (to_blocks...]
    dot_general x133 -> x0, matrix products: 293 us -> none  [the longest x24 111 us: group_step(): inner_y = jnp.einsum('tsh,shp->thp', weight, values, precision=HIGHEST)]
    pallas_call x0 -> x2, Pallas kernels: none -> 205 us  [the longest x1 198 us: body(): pl.pallas_call(partial(layer_kernel, reach, bits, NAMES_IN + NAMES_OUT +...]
    psum x3 -> x0, waiting for transfers between devices: 187 us -> none  [the longest x1 187 us: body(): lax.psum((norm_gain_grad, gate_proj_grad, value_proj_grad, state_proj_gra...]
    all_gather x4 -> x0, waiting for transfers between devices: 117 us -> none  [the longest x2 93.6 us: prefix(): lax.all_gather(a.astype(kind), axis)]
    psum x4 -> x0, blocking collectives: 86.1 us -> none  [the longest x1 75 us: body(): lax.psum((norm_gain_grad, gate_proj_grad, value_proj_grad, state_proj_gra...]
    another operation x93 -> x0, other arithmetic: 75.1 us -> none
    convert_element_type x63 -> x0, other arithmetic: 54.3 us -> none  [the longest x32 22 us: turn(): part[at].astype(own.dtype)]
  transfers between devices with their start and end apart: 9 -> 0, of which waited for: 5 -> 0; matrix products, arithmetic and copies ran while one was open for 19% -> 0% of each run, Pallas kernels for 0% -> 0%
where the time goes in v4:
time: 210 us
  Pallas kernels  205 us (98%)
  local copies, waits for them, and re-layouts  4.12 us (2%)
    pallas_call x1, Pallas kernels, body(): pl.pallas_call(partial(layer_kernel, reach, bits, NAMES_IN + NAMES_OUT +...  198 us
    pallas_call x1, Pallas kernels, body(): pl.pallas_call(partial(last_kernel, heads), grid=(width // rows,), in_spe...  7.31 us

profile of v4, /device:TPU:0, one launch (start us, length us, event | category | flops | bytes accessed | tf_op | source)
XLA Modules:
  0.0 209.7 jit_solution(5844938371766409897)
XLA Ops:
  0.7 197.6 %shard_map.254 = (bf16[1024,768]{1,0:T(8,128)(2,1)}, f32[1024,768]{1,0:T(8,128)}, bf16[768,768]{1,0:T(8,128)(2,1)}, bf16[768,768]{1,0:T(8,128)(2,1)}, bf16[768,7...) custom-call(s32[9]{0:T(128)} %refs_0_.1, bf16[1024,768]{1,0:T(8,128)(2,1)} %refs_1_.1, ...), custom_call_target="tpu_custom_call" | custom-call | tf_op jit(solution)/shard_map/pallas_call | solution.py:1020
  198.2 0.0 copy-start.1
  198.2 7.3 %shard_map.255 = (f32[768]{0:T(1024)}, f32[768,768]{1,0:T(8,128)}, f32[768,768]{1,0:T(8,128)}, f32[768,256]{1,0:T(8,128)}, f32[12,2,768]{2,1,0:T(2,128)}, /*inde...) custom-call(bf16[768,768]{1,0:T(8,128)(2,1)} %get-tuple-element.35.g, ...), custom_call_target="tpu_custom_call" | custom-call | tf_op jit(solution)/shard_map/pallas_call | solution.py:1042
  205.6 0.0 copy-done.1
  205.6 0.0 copy-start
  205.6 1.1 copy.31
  206.7 1.3 copy-done
  208.0 1.7 copy.32
Async XLA Ops:
  198.2 7.3 %copy-start.1 = (bf16[1024,768]{1,0:T(8,128)(2,1)S(1)}, bf16[1024,768]{1,0:T(8,128)(2,1)}, u32[]{:S(2)}) copy-start(bf16[1024,768]{1,0:T(8,128)(2,1)} %get-tuple-element.66) | copy-start | bytes 4718596
  205.6 2.5 %copy-start = (f32[1024,768]{1,0:T(8,128)S(1)}, f32[1024,768]{1,0:T(8,128)}, u32[]{:S(2)}) copy-start(f32[1024,768]{1,0:T(8,128)} %get-tuple-element.67) | copy-start | bytes 9437188

commit v5 on v4

--- a/solution.py
+++ b/solution.py
@@ -248,26 +248,34 @@
         if at + 1 < len(self.steps[p]):
             self.copy(p, self.steps[p][at + 1]).start()
 
-    def plan(self, p):
-        at = self.pos[p]
-        if at >= len(self.steps[p]):
+    def take(self, name):
+        if self.bits != TABLE_BITS:
             return []
-        self.pos[p] = at + 1
-        return [(p, at)]
-
-    def advance(self, p):
-        for q, at in self.plan(p):
-            self.step(q, at)
-
-    def plans(self, wanted):
-        return {turn: [step for p in wanted[turn] for step in self.plan(p)] for turn in sorted(wanted)}
-
-    def hook(self, turn, plans):
-        for k, steps in plans.items():
-            @pl.when(turn == k)
-            def _():
-                for p, at in steps:
-                    self.step(p, at)
+        taken = TABLE.get(name, ())
+        for p, at in taken:
+            assert self.pos[p] == at
+            self.pos[p] = at + 1
+        return taken
+
+    def at(self, name):
+        for p, at in self.take(name):
+            self.step(p, at)
+
+    def takes(self, name, count):
+        return {k: self.take(name + str(k)) for k in range(count)}
+
+    def hook(self, turn, taken):
+        for k, steps in taken.items():
+            if steps:
+                @pl.when(turn == k)
+                def _():
+                    for p, at in steps:
+                        self.step(p, at)
+
+    def left(self):
+        order = list(TABLE["tail"]) if self.bits == TABLE_BITS else []
+        rest = [(p, at) for p in range(len(self.pieces)) for at in range(self.pos[p], len(self.steps[p]))]
+        return order + sorted((x for x in rest if x not in order), key=lambda x: x[::-1])
 
     def add(self, p, s, copy):
         piece = self.pieces[p]
@@ -281,7 +289,7 @@
         recv, rel = piece["recv"], off - self.first(p)
         source, at = (piece["work"], off) if s == 0 else (piece["kept"], rel)
         dest, to = (piece["out"], off) if s == self.bits - 1 else (piece["kept"], rel)
-        size = 48 if rows % 48 == 0 else 16
+        size = next(n for n in (64, 48, 32, 16) if rows % n == 0)
 
         def one(i, _):
             total = source[pl.ds(pl.multiple_of(at + i * size, 16), size), :].astype(F32)
@@ -302,6 +310,11 @@
     while made < bits and (rows >> made) % 32 == 0:
         made += 1
     return made
+
+
+def piece_names(width, inner):
+    return ([f"ggw{g}" for g in range(width // 256)] + [f"gow{g}" for g in range(inner // 256)]
+            + [f"gv{g}" for g in range(inner // 256)] + ["gsw"])
 
 
 def received_rows(rows, bits):
@@ -314,14 +327,6 @@
 
 def part(i, size):
     return pl.ds(pl.multiple_of(i * size, size), size)
-
-
-def at_turns(*groups):
-    found = {}
-    for turns, pieces in groups:
-        for turn in turns:
-            found.setdefault(turn, []).extend(pieces)
-    return found
 
 
 class Refs:
@@ -354,18 +359,16 @@
 
     swap1 = Swap(reach, r.msgs.at[0], r.msgs.at[1], r.low1, r.high1, r.up_s.at[0], r.up_r.at[0], r.dn_s.at[0], r.dn_r.at[0])
     swap2 = Swap(reach, r.msgs.at[2], r.msgs.at[3], r.low2, r.high2, r.up_s.at[1], r.up_r.at[1], r.dn_s.at[1], r.dn_r.at[1])
-    plain = list(range(bits))
-    turned = plain[1:2] + plain[:1] + plain[2:]
     groups = inner // 256
-    first_state = 2 + groups
-    sums = ["ggw", "gow"] + [f"gv{g}" for g in range(groups)] + ["gsw"]
+    names = piece_names(width, inner)
+    orders = [ORDERS[i % len(ORDERS)] if bits == TABLE_BITS else tuple(range(bits)) for i in range(len(names))]
     pieces = [
         dict(work=getattr(r, name + "_w"), kept=getattr(r, name + "_k"), recv=getattr(r, name + "_r"),
-             out=getattr(r, name + "_o"), order=turned if i % 2 else plain)
-        for i, name in enumerate(sums)
+             out=getattr(r, name + "_o"), order=order)
+        for name, order in zip(names, orders)
     ]
+    of = {name: i for i, name in enumerate(names)}
     red = Reduce(bits, pieces, r.rs_s, r.rs_r, r.ag_s, r.ag_r)
-    first = [0, 1]
     barrier = pltpu.get_barrier_semaphore()
     near = swap1.greet(barrier)
     for mate in red.mates:
@@ -410,6 +413,13 @@
         r.wst[k * HP : (k + 1) * HP, :] = jnp.concatenate(
             [wstep[:, k, :], jnp.zeros((HP - heads, width), F32)], axis=0).astype(BF16)
 
+    r.tap[:, :inner] = r.tapv[...]
+    r.tap[:, inner:] = r.taps[...]
+    for blk in range(nblk):
+        tok = iota((TB, 128), 0) + blk * TB
+        for m in range(1, 4):
+            r.valid[m - 1, blk * TB : (blk + 1) * TB, :] = conv_mask(tok, m, b, off0).astype(BF16)
+
     loads[0].wait()
     loads[1].wait()
     loads[2].wait()
@@ -447,18 +457,9 @@
     def _():
         r.halo[...] = jnp.zeros_like(r.halo)
 
-    def conv_rows(blk, cols, c0, masks, width_now):
-        r.jx[...] = r.joined[pl.ds(pl.multiple_of(blk * TB, 16), TB + 16), cols].astype(F32)
-        shifted = [r.jx[16 : 16 + TB, :]]
-        tap = r.tap[:, cols]
-        total = shifted[0] * tap[3:4]
-        for m in range(1, 4):
-            shifted.append(r.jx[16 - m : 16 - m + TB, :] * masks[m])
-            total = total + shifted[m] * tap[3 - m : 4 - m]
-        return shifted, tap, total
-
-    r.tap[:, :inner] = r.tapv[...]
-    r.tap[:, inner:] = r.taps[...]
+    def valid_of(rows, m):
+        one = r.valid[m - 1, rows, :].astype(F32)
+        return jnp.concatenate([one, one], axis=1)
 
     def chunk_parts(chunk):
         cols = part(chunk, Q)
@@ -466,12 +467,16 @@
 
     def summarize(blk, _):
         rows = part(blk, TB)
-        tok = iota((TB, 1), 0) + blk * TB
-        masks = [conv_mask(tok, m, b, off0) for m in range(4)]
         for g in range(both // 256):
             cols = slice(g * 256, (g + 1) * 256)
-            _, _, total = conv_rows(blk, cols, g * 256, masks, 256)
-            r.act[rows, cols] = silu(total).astype(BF16)
+            r.jx[...] = r.joined[pl.ds(pl.multiple_of(blk * TB, 16), TB + 16), cols].astype(F32)
+            tap = r.tap[:, cols]
+            total = r.jx[16 : 16 + TB, :] * tap[3:4]
+            for m in range(1, 4):
+                total = total + r.jx[16 - m : 16 - m + TB, :] * valid_of(rows, m) * tap[3 - m : 4 - m]
+            sig = jax.nn.sigmoid(total)
+            r.act[rows, cols] = (total * sig).astype(BF16)
+            r.slope[rows, cols] = (sig * (1.0 + total * (1.0 - sig))).astype(BF16)
         for q in range(per):
             chunk = blk * per + q
             t0 = chunk * Q
@@ -553,6 +558,7 @@
     def enter(blk, _):
         lane = iota((Q, 128), 1)
         u_all = nt(r.cot[part(blk, TB), :], r.wo[...])
+        r.dy[part(blk, TB), :] = u_all
         for q in range(per):
             chunk = blk * per + q
             at = part(chunk, Q)
@@ -587,7 +593,6 @@
         sums = jnp.concatenate([sums, jnp.zeros((120, TB), F32)], axis=0).T
         scale = lax.rsqrt(sums[:, 0:1] / (2 * inner) + EPSILON)
         back = scale * scale * scale * sums[:, 1:2] / (2 * inner)
-        gng = nt(r.cot[rows, :], r.wo[...])
         for j in range(inner // 128):
             lanes = slice(j * 128, (j + 1) * 128)
             mixed = r.mixed[rows, lanes]
@@ -596,15 +601,13 @@
             gated = mixed * (pre * sig)
             ng = gated * scale
             r.buf[rows, lanes] = (ng * ggain[:, lanes]).astype(BF16)
-            g = gng[:, lanes]
+            g = r.dy[rows, lanes]
             r.small[0:1, lanes] += jnp.sum(g * ng, axis=0, keepdims=True)
             grad_gated = scale * (g * ggain[:, lanes]) - gated * back
             dy = grad_gated * (pre * sig)
             r.small[1:2, lanes] += jnp.sum(dy * r.act[rows, lanes].astype(F32), axis=0, keepdims=True)
             r.dy[rows, lanes] = dy
             r.ggate[rows, lanes] = (grad_gated * mixed * (sig * (1.0 + pre * (1.0 - sig)))).astype(BF16)
-        r.out_mine[rows, :] = nn(r.buf[rows, :], r.wo[...]).astype(BF16)
-        over(r.out_mine.at[rows], r.out_other.at[rows], r.out_sem, blk).start()
         for q in range(per):
             chunk = blk * per + q
             at = part(chunk, Q)
@@ -625,16 +628,26 @@
     put_message(r.msgs.at[2], sumr * after_f, prodr * after_f)
     put_message(r.msgs.at[3], sumf * before_f, prodf * before_f)
     swap2.start()
-    r.ggw_w[...] = nn(r.normt[...], r.ggate[...]).astype(BF16)
-    red.start(0)
-    r.gow_w[...] = tn(r.buf[...], r.cot[...]).astype(BF16)
-    red.start(1)
+    for g in range(width // 256):
+        pieces[of[f"ggw{g}"]]["work"][...] = nn(r.normt[g * 256 : (g + 1) * 256, :], r.ggate[...]).astype(BF16)
+        red.start(of[f"ggw{g}"])
+    for g in range(groups):
+        pieces[of[f"gow{g}"]]["work"][...] = tn(r.buf[:, g * 256 : (g + 1) * 256], r.cot[...]).astype(BF16)
+        red.start(of[f"gow{g}"])
+
+    def project_out(blk, _):
+        rows = part(blk, TB)
+        r.out_mine[rows, :] = nn(r.buf[rows, :], r.wo[...]).astype(BF16)
+        over(r.out_mine.at[rows], r.out_other.at[rows], r.out_sem, blk).start()
+        return 0
+
+    lax.fori_loop(0, nblk, project_out, 0)
 
     sums_low = jnp.concatenate([lower, upper], axis=1).astype(BF16)
     diag = tri0 == tri1
     r.rowbuf[...] = jnp.zeros_like(r.rowbuf)
 
-    plans_within = red.plans(at_turns((G1_WITHIN, first)))
+    taken_within = red.takes("within", nblk)
 
     def back_within(blk, _):
         for q in range(per):
@@ -678,7 +691,7 @@
                 [nn(dsf.astype(BF16), readf), nn(dsf.T.astype(BF16), entf),
                  nn(dsr.astype(BF16), readr), nn(dsr.T.astype(BF16), entr)], axis=1)
 
-        red.hook(blk, plans_within)
+        red.hook(blk, taken_within)
         return 0
 
     lax.fori_loop(0, nblk, back_within, 0)
@@ -701,7 +714,7 @@
 
     lower32, upper32 = lower.astype(F32), upper.astype(F32)
 
-    plans_states = red.plans(at_turns((G1_STATES, first)))
+    taken_states = red.takes("states", nblk)
 
     def back_states(blk, _):
         for q in range(per):
@@ -750,25 +763,22 @@
         @pl.when(blk == 0)
         def _():
             tok8 = iota((8, 1), 0)
-            masks = [conv_mask(tok8, m, b, off0) for m in range(4)]
-            rows = r.joined[0:32, :].astype(F32)
             tap = r.tap[...]
-            total = rows[16:24] * tap[3:4]
-            for m in range(1, 4):
-                total = total + rows[16 - m : 24 - m] * masks[m] * tap[3 - m : 4 - m]
-            sig = jax.nn.sigmoid(total)
-            dconv = r.mixed[0:8, :] * (sig * (1.0 + total * (1.0 - sig)))
-            first = jnp.concatenate([jnp.zeros((8, both), F32), dconv], axis=0)
+            dconv = r.mixed[0:8, :] * r.slope[0:16, :].astype(F32)[0:8]
+            rows = r.joined[0:16, :].astype(F32)[8:16]
             lent = jnp.zeros((8, both), F32)
             for m in range(1, 4):
-                lent = lent + first[m : m + 8] * conv_mask(tok8 - 8 + m, m, b, off0) * tap[3 - m : 4 - m]
+                first = jnp.concatenate([jnp.zeros((8, both), F32), dconv * conv_mask(tok8, m, b, off0)], axis=0)
+                first = first[m : m + 8]
+                lent = lent + first * tap[3 - m : 4 - m]
+                r.cg_mine[3 - m : 4 - m, :] = jnp.sum(first * rows, axis=0, keepdims=True)
             r.lent_mine[...] = lent
 
             @pl.when(me > 0)
             def _():
                 lent_copy(me - 1).start()
 
-        red.hook(blk, plans_states)
+        red.hook(blk, taken_states)
         return 0
 
     lax.fori_loop(0, nblk, back_states, 0)
@@ -781,27 +791,24 @@
     def _():
         r.lent_other[...] = jnp.zeros_like(r.lent_other)
 
-    r.dbuf[length : length + 8, :] = jnp.zeros((8, 256), F32)
-
     def back_conv(g):
         cols = slice(g * 256, (g + 1) * 256)
+        r.ext[...] = jnp.zeros_like(r.ext)
 
         def one(i, _):
             blk = nblk - 1 - i
             rows = part(blk, TB)
-            tok = iota((TB, 1), 0) + blk * TB
-            masks = [conv_mask(tok, m, b, off0) for m in range(4)]
-            later = [conv_mask(tok + m, m, b, off0) for m in range(4)]
-            shifted, tap, total = conv_rows(blk, cols, g * 256, masks, 256)
-            sig = jax.nn.sigmoid(total)
-            dconv = r.mixed[rows, cols] * (sig * (1.0 + total * (1.0 - sig)))
-            r.dbuf[rows, :] = dconv
-            for m in range(4):
-                r.cg_mine[3 - m : 4 - m, cols] += jnp.sum(dconv * shifted[m], axis=0, keepdims=True)
+            tap = r.tap[:, cols]
+            x = r.joined[pl.ds(pl.multiple_of(16 + blk * TB, 16), TB), cols].astype(F32)
+            dconv = r.mixed[rows, cols] * r.slope[rows, cols].astype(F32)
             grad = dconv * tap[3:4]
-            ahead = r.dbuf[pl.ds(pl.multiple_of(blk * TB, TB), TB + 8), :]
+            r.cg_mine[3:4, cols] += jnp.sum(dconv * x, axis=0, keepdims=True)
             for m in range(1, 4):
-                grad = grad + ahead[m : m + TB] * later[m] * tap[3 - m : 4 - m]
+                r.ext[m - 1, TB : TB + 8, :] = r.ext[m - 1, 0:8, :]
+                r.ext[m - 1, 0:TB, :] = dconv * valid_of(rows, m)
+                moved = r.ext[m - 1, m : m + TB, :]
+                r.cg_mine[3 - m : 4 - m, cols] += jnp.sum(moved * x, axis=0, keepdims=True)
+                grad = grad + moved * tap[3 - m : 4 - m]
             last = jnp.where(blk == nblk - 1, 1.0, 0.0)
             grad = jnp.concatenate([grad[: TB - 8], grad[TB - 8 :] + r.lent_other[:, cols] * last], axis=0)
             if g * 256 < inner:
@@ -817,48 +824,53 @@
     gs_copy.start()
     cg_copy = over(r.cg_mine.at[:, pl.ds(inner, maps)], r.cg_other, r.misc_sem, 1)
     cg_copy.start()
-    for g in range(inner // 256):
+    red.at("maps")
+
+    def finish_maps():
+        gs_copy.wait()
+        cg_copy.wait()
+        r.gs_mine[...] = (r.gs_mine[...].astype(F32) + r.gs_other[...].astype(F32)).astype(BF16)
+        half = r.gs_mine[:, pl.ds(pl.multiple_of(core * 128, 128), 128)]
+        r.gsw_w[:, 0:128] = nn(r.normt[...], half).astype(BF16)
+        gstep = jnp.concatenate([r.gstep[...].astype(F32), jnp.zeros((128 - 2 * HP, length), F32)], axis=0)
+        r.gsw_w[:, 128:256] = nt(r.normt[...], gstep.astype(BF16)).astype(BF16)
+        red.start(of["gsw"])
+
+    for g in range(groups):
         cols = slice(g * 256, (g + 1) * 256)
         back_conv(g)
-        pieces[2 + g]["work"][...] = nn(r.normt[...], r.buf[:, cols]).astype(BF16)
-        red.start(2 + g)
-        if g in G1_CONV:
-            red.advance(0)
-            red.advance(1)
-    gs_copy.wait()
-    cg_copy.wait()
-    r.gs[...] = (r.gs_mine[...].astype(F32) + r.gs_other[...].astype(F32)).astype(BF16)
-    r.gsw_w[:, :maps] = nn(r.normt[...], r.gs[...]).astype(BF16)
-    gstep = jnp.concatenate([r.gstep[...].astype(F32), jnp.zeros((128 - 2 * HP, length), F32)], axis=0)
-    r.gsw_w[:, maps:] = nt(r.normt[...], gstep.astype(BF16)).astype(BF16)
-    red.start(first_state)
-
-    later_pieces = list(range(2, len(pieces)))
-
-    plans_down = red.plans(at_turns((G1_DOWN, first), (G2_DOWN, later_pieces)))
+        pieces[of[f"gv{g}"]]["work"][...] = nn(r.normt[...], r.buf[:, cols]).astype(BF16)
+        red.start(of[f"gv{g}"])
+        if g == 0:
+            finish_maps()
+        red.at("conv" + str(g))
+
+    taken_down = red.takes("down", nblk)
 
     def down(blk, _):
         rows = part(blk, TB)
         gn = nt(r.ggate[rows, :], r.wg[...]) + nt(r.buf[rows, :], r.wv[...]) + tn(r.gstep[:, rows], r.wst[...])
         r.gn_mine[rows, :] = gn.astype(BF16)
         over(r.gn_mine.at[rows], r.gn_other.at[rows], r.gn_sem, blk).start()
-        red.hook(blk, plans_down)
+        red.hook(blk, taken_down)
         return 0
 
     lax.fori_loop(0, nblk, down, 0)
     tiny = r.tiny_w.at[0]
-    tiny[...] = jnp.zeros((16, both), F32)
+    tiny[...] = jnp.zeros((8, both), F32)
     tiny[0:2, :inner] = r.small[0:2, :]
-    tiny[4:6, 0 : 2 * HP] = r.hsum[...].T[0:2]
-    tiny[8:16, :inner] = r.cg_mine[:, :inner]
-    tiny[8:16, inner:] = r.cg_mine[:, inner:] + r.cg_other[...]
+    head_sums = r.hsum[...].T
+    tiny[3:4, 0 : 2 * HP] = head_sums[0:1]
+    tiny[3:4, 128 : 128 + 2 * HP] = head_sums[1:2]
+    tiny[4:8, :inner] = r.cg_mine[0:4, :inner]
+    tiny[4:8, inner:] = r.cg_mine[0:4, inner:] + r.cg_other[0:4, :]
 
     def out_copy(blk):
         rows = part(blk, TB)
         return (pltpu.make_async_copy(r.out_other.at[rows], r.block_out.at[rows], r.store.at[0, blk]),
                 pltpu.make_async_copy(r.gate.at[rows], r.grad_hidden.at[rows], r.store.at[1, blk]))
 
-    plans_end = red.plans(at_turns((G1_END, first), (G2_END, later_pieces)))
+    taken_end = red.takes("end", nblk)
 
     def ending(blk, _):
         rows = part(blk, TB)
@@ -867,7 +879,7 @@
         x = r.hid[rows, :].astype(F32)
         r.out_other[rows, :] = (
             x + (r.out_mine[rows, :].astype(F32) + r.out_other[rows, :].astype(F32))).astype(BF16)
-        gn = r.gn_mine[rows, :].astype(F32) + r.gn_other[rows, :].astype(F32) + nt(r.gs[rows, :], r.ws[...])
+        gn = r.gn_mine[rows, :].astype(F32) + r.gn_other[rows, :].astype(F32) + nt(r.gs_mine[rows, :], r.ws[...])
         scale = lax.rsqrt(jnp.mean(x * x, axis=1, keepdims=True) + EPSILON)
         tiny[2:3, :width] += jnp.sum(gn * x * scale, axis=0, keepdims=True)
         v = gn * gain
@@ -875,7 +887,7 @@
         r.gate[rows, :] = r.cot[rows, :].astype(F32) + scale * v - x * (scale * scale * scale * mean)
         for copy in out_copy(blk):
             copy.start()
-        red.hook(blk, plans_end)
+        red.hook(blk, taken_end)
         return 0
 
     lax.fori_loop(0, nblk, ending, 0)
@@ -885,29 +897,46 @@
             src_ref=r.tiny_w.at[s], dst_ref=r.tiny_r.at[s], send_sem=r.tiny_sem.at[0, s],
             recv_sem=r.tiny_sem.at[1, s], device_id=(red.mates[s], core), device_id_type=MESH)
 
+    halves_copy = over(r.gsw_o.at[:, pl.ds(0, 128)], r.gsx, r.misc_sem, 2)
+    stores = []
+
+    def store(src, dst):
+        copy = pltpu.make_async_copy(src, dst, r.store.at[2, len(stores)])
+        copy.start()
+        stores.append(copy)
+
+    def settle(p):
+        red.finish(p)
+        name, out = names[p], pieces[p]["out"]
+        if name == "gsw":
+            halves_copy.start()
+            return
+        kind, at = name[:-1], pl.ds(int(name[-1]) * 256, 256)
+        store(out, r.ggw_any.at[at] if kind == "ggw" else r.gow_any.at[at] if kind == "gow" else r.gvw_any.at[:, at])
+
+    for p in range(len(pieces)):
+        if red.pos[p] == len(red.steps[p]):
+            settle(p)
     tiny_copy(0).start()
-    for s in range(bits):
-        tiny_copy(s).wait()
-        r.tiny_w[s + 1] = r.tiny_w[s] + r.tiny_r[s]
-        if s + 1 < bits:
-            tiny_copy(s + 1).start()
-        for p in range(len(pieces)):
-            red.advance(p)
-    stores = [
-        pltpu.make_async_copy(src, dst, r.store.at[2, i]) for i, (src, dst) in enumerate(
-            ((r.ggw_o, r.ggw_any), (r.gow_o, r.gow_any), (r.gsw_o, r.gsw_any),
-             *((pieces[2 + g]["out"], r.gvw_any.at[:, pl.ds(g * 256, 256)]) for g in range(groups)),
-             (r.tiny_w.at[bits], r.tiny_any)))]
-    stores[-1].start()
-    while any(red.pos[p] < len(red.steps[p]) for p in range(len(pieces))):
-        for p in range(len(pieces)):
-            red.advance(p)
-    for p in range(len(pieces)):
-        red.finish(p)
-    for store in stores[:-1]:
-        store.start()
-    for store in stores:
-        store.wait()
+    rest, turns = red.left(), 0
+    for i, (p, at) in enumerate(rest):
+        red.step(p, at)
+        if at == len(red.steps[p]) - 1:
+            settle(p)
+        while turns < bits and (turns + 1) * len(rest) <= (i + 1) * (bits + 1) or i + 1 == len(rest) and turns < bits:
+            tiny_copy(turns).wait()
+            r.tiny_w[turns + 1] = r.tiny_w[turns] + r.tiny_r[turns]
+            turns += 1
+            if turns < bits:
+                tiny_copy(turns).start()
+    store(r.tiny_w.at[bits], r.tiny_any)
+    halves_copy.wait()
+    mine_at, other_at = pl.multiple_of(core * 128, 128), pl.multiple_of((1 - core) * 128, 128)
+    store(r.gsw_o.at[:, pl.ds(0, 128)], r.gsw_any.at[:, pl.ds(mine_at, 128)])
+    store(r.gsx, r.gsw_any.at[:, pl.ds(other_at, 128)])
+    store(r.gsw_o.at[:, pl.ds(128, 128)], r.gsw_any.at[:, pl.ds(256, 128)])
+    for copy in stores:
+        copy.wait()
     for blk in range(nblk):
         for copy in out_copy(blk):
             copy.wait()
@@ -921,13 +950,77 @@
         lent_copy(me - 1).wait_send()
 
 
-G1_WITHIN = (2, 3)
-G1_STATES = (1, 2, 3)
-G1_CONV = (1, 2)
-G1_DOWN = (1, 3)
-G2_DOWN = (2,)
-G1_END = ()
-G2_END = (0, 2)
+TABLE_BITS = 4
+ORDERS = (
+    (1, 0, 3, 2),
+    (0, 1, 3, 2),
+    (0, 2, 1, 3),
+    (2, 3, 1, 0),
+    (1, 0, 2, 3),
+    (1, 2, 0, 3),
+    (0, 1, 2, 3),
+    (2, 1, 0, 3),
+    (1, 2, 0, 3),
+    (0, 1, 3, 2),
+)
+TABLE = {
+    "within1": (
+        (3, 0),
+    ),
+    "within2": (
+        (0, 0), (1, 0), (2, 0),
+    ),
+    "within3": (
+        (4, 0), (5, 0),
+    ),
+    "states0": (
+        (0, 1), (1, 1), (2, 1), (3, 1),
+    ),
+    "states1": (
+        (4, 1), (5, 1),
+    ),
+    "states2": (
+        (2, 2), (3, 2),
+    ),
+    "states3": (
+        (0, 2), (1, 2), (4, 2), (5, 2),
+    ),
+    "maps": (
+        (2, 3), (3, 3),
+    ),
+    "conv0": (
+        (0, 3), (1, 3), (4, 3), (5, 3),
+    ),
+    "conv1": (
+        (2, 4), (3, 4),
+    ),
+    "conv2": (
+        (0, 4), (1, 4), (4, 4), (5, 4),
+    ),
+    "down0": (
+        (2, 5), (3, 5), (6, 0),
+    ),
+    "down1": (
+        (5, 5),
+    ),
+    "down2": (
+        (4, 5), (7, 0), (8, 0),
+    ),
+    "down3": (
+        (0, 5), (1, 5), (6, 1), (9, 0),
+    ),
+    "end2": (
+        (2, 6), (3, 6), (4, 6), (7, 1),
+    ),
+    "end3": (
+        (0, 6),
+    ),
+    "tail": (
+        (5, 6), (6, 2), (8, 1), (1, 6), (9, 1), (6, 3), (7, 2), (9, 2), (8, 2), (6, 4), (7, 3), (3, 7),
+        (9, 3), (8, 3), (2, 7), (7, 4), (1, 7), (6, 5), (4, 7), (9, 4), (8, 4), (7, 5), (0, 7), (5, 7),
+        (8, 5), (9, 5), (6, 6), (7, 6), (8, 6), (9, 6), (6, 7), (7, 7), (8, 7), (9, 7),
+    ),
+}
 
 
 def last_kernel(heads, ggw_ref, gow_ref, gvw_ref, gsw_ref, tiny_ref,
@@ -946,10 +1039,10 @@
         width, inner = ngain_ref.shape[0], convv_ref.shape[1]
         ngain_ref[...] = tiny_ref[2, :width]
         ggain_ref[...] = tiny_ref[0, :inner]
-        convv_ref[...] = tiny_ref[8:12, :inner]
-        convs_ref[...] = tiny_ref[8:12, inner:]
-        bias_ref[...] = jnp.concatenate([tiny_ref[4:5, 0:heads], tiny_ref[4:5, HP : HP + heads]], axis=0)
-        decay_ref[...] = (tiny_ref[5:6, 0:heads] + tiny_ref[5:6, HP : HP + heads]).reshape(heads)
+        convv_ref[...] = tiny_ref[4:8, :inner]
+        convs_ref[...] = tiny_ref[4:8, inner:]
+        bias_ref[...] = jnp.concatenate([tiny_ref[3:4, 0:heads], tiny_ref[3:4, HP : HP + heads]], axis=0)
+        decay_ref[...] = (tiny_ref[3:4, 128 : 128 + heads] + tiny_ref[3:4, 128 + HP : 128 + HP + heads]).reshape(heads)
         spread = spread_matrix(inner, inner // heads)
         total = nt(jnp.broadcast_to(tiny_ref[1:2, :inner], (8, inner)), spread, HIGHEST)
         skip_ref[...] = total[0:1, :heads].reshape(heads)
@@ -974,7 +1067,7 @@
     bits = count.bit_length() - 1
     assert count == 1 << bits
     reach = min(1 + (LEN_MOST - 2) // length, count - 1)
-    npieces = 3 + inner // 256
+    npieces = len(piece_names(width, inner))
 
     def vmem(*dims, dtype=F32):
         return pltpu.VMEM(dims, dtype)
@@ -993,23 +1086,25 @@
         msgs=vmem(4, 80, inner, **low),
         low1=vmem(reach, 80, inner, **low), high1=vmem(reach, 80, inner, **low),
         low2=vmem(reach, 80, inner, **low), high2=vmem(reach, 80, inner, **low),
-        rowbuf=vmem(nchunk, 4 * HP, Q), jx=vmem(TB + 16, 256), dbuf=vmem(length + 8, 256),
+        rowbuf=vmem(nchunk, 4 * HP, Q), jx=vmem(TB + 16, 256), ext=vmem(3, TB + 8, 256),
+        valid=vmem(3, length, 128, **low), slope=vmem(length, both, **low), gsx=vmem(width, 128, **low),
         halo=vmem(16, width, **low), mine=vmem(nblk, 8, TB), other=vmem(nblk, 8, TB),
         out_mine=vmem(length, width, **low), out_other=vmem(length, width, **low),
         gn_mine=vmem(length, width, **low), gn_other=vmem(length, width, **low),
-        gs_mine=vmem(length, maps, **low), gs_other=vmem(length, maps, **low), gs=vmem(length, maps, **low),
+        gs_mine=vmem(length, maps, **low), gs_other=vmem(length, maps, **low),
         lent_mine=vmem(8, both), lent_other=vmem(8, both), cg_mine=vmem(8, both), cg_other=vmem(8, maps),
         hsum=vmem(2 * HP, 128), small=vmem(8, inner),
-        tiny_w=vmem(bits + 1, 16, both), tiny_r=vmem(bits, 16, both),
+        tiny_w=vmem(bits + 1, 8, both), tiny_r=vmem(bits, 8, both),
     )
-    for name, rows, cols in (("ggw", width, inner), ("gow", inner, width), ("gsw", width, maps + 128), *((f"gv{g}", width, 256) for g in range(inner // 256))):
+    for name in piece_names(width, inner):
+        rows, cols = (256, width) if name[:3] in ("ggw", "gow") else (width, 256)
         scratch[name + "_w"] = vmem(rows, cols, **low)
         scratch[name + "_k"] = vmem(rows // 2, cols, **low)
         scratch[name + "_r"] = vmem(received_rows(rows, bits), cols, **low)
         scratch[name + "_o"] = vmem(rows, cols, **low)
     scratch.update(
-        load=dma((6,)), store=dma((3, max(nblk, 4 + inner // 256))), edge=dma((4,)), sum_sem=dma((2, nblk)), out_sem=dma((2, nblk)),
-        gn_sem=dma((2, nblk)), misc_sem=dma((2, 2)), tiny_sem=dma((2, bits)),
+        load=dma((6,)), store=dma((3, npieces + nblk)), edge=dma((4,)), sum_sem=dma((2, nblk)), out_sem=dma((2, nblk)),
+        gn_sem=dma((2, nblk)), misc_sem=dma((2, 3)), tiny_sem=dma((2, bits)),
         up_s=dma((2, reach)), up_r=dma((2, reach)), dn_s=dma((2, reach)), dn_r=dma((2, reach)),
         rs_s=dma((npieces, bits)), rs_r=dma((npieces, bits)), ag_s=dma((npieces, bits)), ag_r=dma((npieces, bits)),
     )
@@ -1023,7 +1118,7 @@
         out_specs=[ANY_SPEC] * 7,
         out_shape=[shape(length, width, **low), shape(length, width), shape(width, inner, **low),
                    shape(inner, width, **low), shape(width, inner, **low), shape(width, maps + 128, **low),
-                   shape(16, both)],
+                   shape(8, both)],
         scratch_shapes=list(scratch.values()),
         compiler_params=pltpu.CompilerParams(
             collective_id=1, has_side_effects=True, vmem_limit_bytes=VMEM_LIMIT),
@@ -1042,7 +1137,7 @@
     final = pl.pallas_call(
         partial(last_kernel, heads),
         grid=(width // rows,),
-        in_specs=[tall(inner), tall(width), tall(inner), tall(maps + 128), whole(16, both)],
+        in_specs=[tall(inner), tall(width), tall(inner), tall(maps + 128), whole(8, both)],
         out_specs=[whole(width), tall(inner), tall(inner), tall(maps), pl.BlockSpec((heads, 2, rows), lambda i: (0, 0, i)), whole(4, inner),
                    whole(4, maps), whole(2, heads), whole(heads), whole(heads), whole(inner), tall(width)],
         out_shape=[shape(width), shape(width, inner), shape(width, inner), shape(width, maps),

time: 210 us -> 166 us (0.79)
  Pallas kernels: 205 us -> 161 us
    pallas_call x1, Pallas kernels: 198 us -> 153 us  [body(): pl.pallas_call(partial(layer_kernel, reach, bits, NAMES_IN + NAMES_OUT +...]
where the time goes in v5:
time: 166 us; the launch traced here: 165 us
  Pallas kernels  161 us (97%)
  local copies, waits for them, and re-layouts  4.12 us (2%)
    pallas_call x1, Pallas kernels, body(): pl.pallas_call(partial(layer_kernel, reach, bits, NAMES_IN + NAMES_OUT +...  153 us
    pallas_call x1, Pallas kernels, body(): pl.pallas_call(partial(last_kernel, heads), grid=(width // rows,), in_spe...  7.23 us
    unnamed x6, local copies, waits for them, and re-layouts  4.12 us

profile of v5, /device:TPU:0, one launch (start us, length us, event | category | flops | bytes accessed | tf_op | source)
XLA Modules:
  0.0 165.3 jit_solution(9845187286983245379)
XLA Ops:
  0.7 153.3 %shard_map.254 = (bf16[1024,768]{1,0:T(8,128)(2,1)}, f32[1024,768]{1,0:T(8,128)}, bf16[768,768]{1,0:T(8,128)(2,1)}, bf16[768,768]{1,0:T(8,128)(2,1)}, bf16[768,7...) custom-call(s32[9]{0:T(128)} %refs_0_.1, bf16[1024,768]{1,0:T(8,128)(2,1)} %refs_1_.1, ...), custom_call_target="tpu_custom_call" | custom-call | tf_op jit(solution)/shard_map/pallas_call | solution.py:1115
  154.0 0.0 copy-start.1
  154.0 7.2 %shard_map.255 = (f32[768]{0:T(1024)}, f32[768,768]{1,0:T(8,128)}, f32[768,768]{1,0:T(8,128)}, f32[768,256]{1,0:T(8,128)}, f32[12,2,768]{2,1,0:T(2,128)}, /*inde...) custom-call(bf16[768,768]{1,0:T(8,128)(2,1)} %get-tuple-element.35.g, ...), custom_call_target="tpu_custom_call" | custom-call | tf_op jit(solution)/shard_map/pallas_call | solution.py:1137
  161.2 0.0 copy-done.1
  161.2 0.0 copy-start
  161.2 1.1 copy.31
  162.4 1.3 copy-done
  163.7 1.7 %copy.32 = f32[1024,768]{1,0:T(8,128)} copy(f32[1024,768]{1,0:T(8,128)S(1)} %copy-done) | data formatting | bytes 6291456
Async XLA Ops:
  154.0 7.2 %copy-start.1 = (bf16[1024,768]{1,0:T(8,128)(2,1)S(1)}, bf16[1024,768]{1,0:T(8,128)(2,1)}, u32[]{:S(2)}) copy-start(bf16[1024,768]{1,0:T(8,128)(2,1)} %get-tuple-element.66) | copy-start | bytes 4718596
  161.2 2.5 %copy-start = (f32[1024,768]{1,0:T(8,128)S(1)}, f32[1024,768]{1,0:T(8,128)}, u32[]{:S(2)}) copy-start(f32[1024,768]{1,0:T(8,128)} %get-tuple-element.67) | copy-start | bytes 9437188

commit v6 on v5

--- a/solution.py
+++ b/solution.py
@@ -13,7 +13,7 @@
 TB = 256
 HP = 16
 MIB = 1024 * 1024
-VMEM_LIMIT = 63 * MIB
+VMEM_LIMIT = 63 * MIB + MIB // 2
 HIGHEST = lax.Precision.HIGHEST
 F32 = jnp.float32
 BF16 = jnp.bfloat16
@@ -45,13 +45,30 @@
     return hi, (x - hi.astype(F32)).astype(BF16)
 
 
-def widen(rows, spread2):
-    hi, lo = split(rows.T)
-    return nn(jnp.concatenate([hi, lo], axis=1), spread2)
-
-
-def widen_col(col, spread):
-    return tn(jnp.broadcast_to(col, (HP, 8)), spread, HIGHEST)[0:1]
+def thirds(x):
+    hi = x.astype(BF16)
+    rest = x - hi.astype(F32)
+    mid = rest.astype(BF16)
+    return jnp.concatenate([hi, mid, (rest - mid.astype(F32)).astype(BF16)], axis=0)
+
+
+def exact(product, rows):
+    return product[:rows] + product[rows : 2 * rows] + product[2 * rows :]
+
+
+def widen(spread2, *factors):
+    stacks = []
+    for rows in factors:
+        hi, lo = split(rows.T)
+        stacks.append(jnp.concatenate([hi, lo], axis=1))
+    wide = nn(jnp.concatenate(stacks, axis=0), spread2)
+    return [wide[i * Q : (i + 1) * Q] for i in range(len(factors))]
+
+
+def widen_cols(spread_low, *cols):
+    rows = jnp.concatenate([*cols, jnp.zeros((HP, 128 - len(cols)), F32)], axis=1).T[0:8]
+    wide = exact(nn(thirds(rows), spread_low), 8)
+    return [wide[i : i + 1] for i in range(len(cols))]
 
 
 def silu(x):
@@ -60,14 +77,6 @@
 
 def softplus(x):
     return jnp.maximum(x, 0.0) + jnp.log1p(jnp.exp(-jnp.abs(x)))
-
-
-def step_parts(step, bias, dlog):
-    dt = softplus(step + bias)
-    ld = -jnp.exp(dlog) * dt
-    upto = (iota((Q, Q), 0) <= iota((Q, Q), 1)).astype(F32)
-    run = nn(ld, upto, HIGHEST)
-    return dt, ld, run, run - ld
 
 
 def state_factors(dt, run, bef, t0, b):
@@ -404,7 +413,7 @@
     spread = spread_matrix(inner, inner // heads)
     spread_low = spread.astype(BF16)
     spread2 = jnp.concatenate([spread_low, spread_low], axis=0)
-    skip = widen_col(small_cols[:HP, 3:4], spread)
+    (skip,) = widen_cols(spread_low, small_cols[:HP, 3:4])
     gain = r.gain[...].reshape(1, width)
     ggain = r.ggain[...].reshape(1, inner)
     r.wst[...] = jnp.zeros_like(r.wst)
@@ -428,6 +437,8 @@
         x = x.astype(F32)
         scale = lax.rsqrt(jnp.mean(x * x, axis=1, keepdims=True) + EPSILON)
         return (x * scale * gain).astype(BF16)
+
+    upto = (iota((Q, Q), 0) <= iota((Q, Q), 1)).astype(BF16)
 
     def project(blk, _):
         rows = part(blk, TB)
@@ -437,7 +448,14 @@
         dest = pl.ds(pl.multiple_of(16 + blk * TB, 16), TB)
         r.joined[dest, :inner] = nn(normed, r.wv[...]).astype(BF16)
         r.joined[dest, inner:] = nn(normed, r.ws[...]).astype(BF16)
-        r.step[:, rows] = nt(r.wst[...], normed)
+        step = nt(r.wst[...], normed)
+        dt = softplus(step + bias)
+        ld = -jnp.exp(dlog) * dt
+        r.step[:, rows] = step
+        r.dt[:, rows] = dt
+        for q in range(per):
+            run = exact(nn(thirds(ld[:, q * Q : (q + 1) * Q]), upto), 2 * HP)
+            r.run[:, pl.ds(pl.multiple_of(blk * TB + q * Q, Q), Q)] = run
         return 0
 
     lax.fori_loop(0, nblk, project, 0)
@@ -463,7 +481,9 @@
 
     def chunk_parts(chunk):
         cols = part(chunk, Q)
-        return step_parts(r.step[:, cols], bias, dlog)
+        dt, run = r.dt[:, cols], r.run[:, cols]
+        ld = -jnp.exp(dlog) * dt
+        return dt, ld, run, run - ld
 
     def summarize(blk, _):
         rows = part(blk, TB)
@@ -485,11 +505,13 @@
             _, _, tf, tr = state_factors(dt, run, bef, t0, b)
             values = r.act[at, :inner].astype(F32)
             maps_t = r.act[at, inner:].astype(F32).T.astype(BF16)
-            r.inc[chunk, 0:64, :] = nn(maps_t[0:64], (values * widen(tf, spread2)).astype(BF16))
-            r.inc[chunk, 64:128, :] = nn(maps_t[128:192], (values * widen(tr, spread2)).astype(BF16))
+            tfe, tre = widen(spread2, tf, tr)
+            r.inc[chunk, 0:64, :] = nn(maps_t[0:64], (values * tfe).astype(BF16))
+            r.inc[chunk, 64:128, :] = nn(maps_t[128:192], (values * tre).astype(BF16))
             gone = jnp.exp(run[:, Q - 1 : Q])
-            r.pexp[chunk, 0:1, :] = widen_col(gone[:HP], spread) * jnp.where((t0 <= b) & (b < t0 + Q), 0.0, 1.0)
-            r.pexp[chunk, 1:2, :] = widen_col(gone[HP:], spread) * jnp.where((t0 < b) & (b <= t0 + Q), 0.0, 1.0)
+            pf, pr = widen_cols(spread_low, gone[:HP], gone[HP:])
+            r.pexp[chunk, 0:1, :] = pf * jnp.where((t0 <= b) & (b < t0 + Q), 0.0, 1.0)
+            r.pexp[chunk, 1:2, :] = pr * jnp.where((t0 < b) & (b <= t0 + Q), 0.0, 1.0)
         return 0
 
     lax.fori_loop(1, nblk, summarize, 0)
@@ -566,8 +588,8 @@
             ef, er, _, _ = state_factors(dt, run, bef, chunk * Q, b)
             maps_here = r.act[at, inner:]
             state = r.state[chunk]
-            ys = nn(maps_here[:, 64:128], state[0:64]) * widen(ef, spread2)
-            ys = ys + nn(maps_here[:, 192:256], state[64:128]) * widen(er, spread2)
+            efe, ere = widen(spread2, ef, er)
+            ys = nn(maps_here[:, 64:128], state[0:64]) * efe + nn(maps_here[:, 192:256], state[64:128]) * ere
             square = jnp.zeros((Q, 1), F32)
             cross = jnp.zeros((Q, 1), F32)
             for j in range(inner // 128):
@@ -615,8 +637,9 @@
             ef, er, _, _ = state_factors(dt, run, bef, chunk * Q, b)
             maps_t = r.act[at, inner:].astype(F32).T.astype(BF16)
             dy = r.dy[at, :]
-            r.inc[chunk, 0:64, :] = nn(maps_t[64:128], (dy * widen(ef, spread2)).astype(BF16))
-            r.inc[chunk, 64:128, :] = nn(maps_t[192:256], (dy * widen(er, spread2)).astype(BF16))
+            efe, ere = widen(spread2, ef, er)
+            r.inc[chunk, 0:64, :] = nn(maps_t[64:128], (dy * efe).astype(BF16))
+            r.inc[chunk, 64:128, :] = nn(maps_t[192:256], (dy * ere).astype(BF16))
         return 0
 
     lax.fori_loop(0, nblk, gating, 0)
@@ -712,7 +735,7 @@
             src_ref=r.lent_mine, dst_ref=r.lent_other, send_sem=r.edge.at[2], recv_sem=r.edge.at[3],
             device_id=(to, core), device_id_type=MESH)
 
-    lower32, upper32 = lower.astype(F32), upper.astype(F32)
+    lower_low, upper_low = lower.astype(BF16), upper.astype(BF16)
 
     taken_states = red.takes("states", nblk)
 
@@ -728,12 +751,12 @@
             grad_state = r.dstate[chunk]
             dy = r.dy[at, :]
             values = r.act[at, :inner].astype(F32)
-            dyf, dyr = dy * widen(ef, spread2), dy * widen(er, spread2)
+            efe, ere, tfe, tre = widen(spread2, ef, er, tf, tr)
+            dyf, dyr = dy * efe, dy * ere
             dreadf = nt(dyf.astype(BF16), state[0:64])
             dreadr = nt(dyr.astype(BF16), state[64:128])
             qf = nt(spread_low, (nn(readf, state[0:64]) * dyf).astype(BF16))
             qr = nt(spread_low, (nn(readr, state[64:128]) * dyr).astype(BF16))
-            tfe, tre = widen(tf, spread2), widen(tr, spread2)
             dvf = nn(entf, grad_state[0:64]) * tfe
             dvr = nn(entr, grad_state[64:128]) * tre
             wf = nt(spread_low, (values * dvf).astype(BF16))
@@ -743,12 +766,14 @@
             through = state.astype(F32) * grad_state.astype(F32)
             zf = jnp.sum(through[0:64], axis=0, keepdims=True) * r.pexp[chunk, 0:1, :]
             zr = jnp.sum(through[64:128], axis=0, keepdims=True) * r.pexp[chunk, 1:2, :]
-            zf = nt(spread, jnp.broadcast_to(zf, (8, inner)), HIGHEST)[:, 0:1]
-            zr = nt(spread, jnp.broadcast_to(zr, (8, inner)), HIGHEST)[:, 0:1]
+            through = jnp.concatenate([zf, zr, jnp.zeros((6, inner), F32)], axis=0)
+            through = exact(nt(thirds(through), spread_low), 8)
+            through = jnp.concatenate([through, jnp.zeros((120, HP), F32)], axis=0).T
+            zf, zr = through[:, 0:1], through[:, 1:2]
             r.mixed[at, :inner] = r.mixed[at, :inner] + dvf + dvr
             r.mixed[at, inner:] = r.mixed[at, inner:] + jnp.concatenate([dentf, dreadf, dentr, dreadr], axis=1)
-            late = nn(jnp.concatenate([qf, wr], axis=0), lower32, HIGHEST)
-            early = nn(jnp.concatenate([wf, qr], axis=0), upper32, HIGHEST)
+            late = exact(nn(thirds(jnp.concatenate([qf, wr], axis=0)), lower_low), 2 * HP)
+            early = exact(nn(thirds(jnp.concatenate([wf, qr], axis=0)), upper_low), 2 * HP)
             rowsum = r.rowbuf[chunk]
             dld = jnp.concatenate(
                 [rowsum[0:HP] + late[:HP] + early[:HP] + zf, rowsum[HP : 2 * HP] + late[HP:] + early[HP:] + zr], axis=0)
@@ -1079,7 +1104,7 @@
         ws=vmem(width, maps, **low), wo=vmem(inner, width, **low), cot=vmem(length, width, **low),
         wst=vmem(2 * HP, width, **low), tap=vmem(4, both),
         normt=vmem(width, length, **low), buf=vmem(length, inner, **low), gate=vmem(length, inner),
-        joined=vmem(16 + length, both, **low), act=vmem(length, both, **low), step=vmem(2 * HP, length),
+        joined=vmem(16 + length, both, **low), act=vmem(length, both, **low), step=vmem(2 * HP, length), dt=vmem(2 * HP, length), run=vmem(2 * HP, length),
         inc=vmem(nchunk, 128, inner), pexp=vmem(nchunk, 2, inner), mixed=vmem(length, both),
         state=vmem(nchunk, 128, inner, **low), dstate=vmem(nchunk, 128, inner, **low),
         dy=vmem(length, inner), ggate=vmem(length, inner, **low), gstep=vmem(2 * HP, length, **low),

time: 166 us -> 154 us (0.928)
  Pallas kernels: 161 us -> 149 us
    pallas_call x1, Pallas kernels: 153 us -> 142 us  [body(): pl.pallas_call(partial(layer_kernel, reach, bits, NAMES_IN + NAMES_OUT +...]
where the time goes in v6:
time: 154 us
  Pallas kernels  149 us (97%)
  local copies, waits for them, and re-layouts  4.12 us (3%)
    pallas_call x1, Pallas kernels, body(): pl.pallas_call(partial(layer_kernel, reach, bits, NAMES_IN + NAMES_OUT +...  142 us
    pallas_call x1, Pallas kernels, body(): pl.pallas_call(partial(last_kernel, heads), grid=(width // rows,), in_spe...  7.23 us
    unnamed x6, local copies, waits for them, and re-layouts  4.12 us

profile of v6, /device:TPU:0, one launch (start us, length us, event | category | flops | bytes accessed | tf_op | source)
XLA Modules:
  0.0 153.5 jit_solution(8610437487622491803)
XLA Ops:
  0.7 141.5 %shard_map.254 = (bf16[1024,768]{1,0:T(8,128)(2,1)}, f32[1024,768]{1,0:T(8,128)}, bf16[768,768]{1,0:T(8,128)(2,1)}, bf16[768,768]{1,0:T(8,128)(2,1)}, bf16[768,7...) custom-call(s32[9]{0:T(128)} %refs_0_.1, bf16[1024,768]{1,0:T(8,128)(2,1)} %refs_1_.1, ...), custom_call_target="tpu_custom_call" | custom-call | tf_op jit(solution)/shard_map/pallas_call | solution.py:1140
  142.2 0.0 copy-start.1
  142.2 7.2 %shard_map.255 = (f32[768]{0:T(1024)}, f32[768,768]{1,0:T(8,128)}, f32[768,768]{1,0:T(8,128)}, f32[768,256]{1,0:T(8,128)}, f32[12,2,768]{2,1,0:T(2,128)}, /*inde...) custom-call(bf16[768,768]{1,0:T(8,128)(2,1)} %get-tuple-element.35.g, ...), custom_call_target="tpu_custom_call" | custom-call | tf_op jit(solution)/shard_map/pallas_call | solution.py:1162
  149.4 0.0 copy-done.1
  149.4 0.0 copy-start
  149.4 1.1 copy.31
  150.6 1.3 copy-done
  151.9 1.7 %copy.32 = f32[1024,768]{1,0:T(8,128)} copy(f32[1024,768]{1,0:T(8,128)S(1)} %copy-done) | data formatting | bytes 6291456
Async XLA Ops:
  142.2 7.2 %copy-start.1 = (bf16[1024,768]{1,0:T(8,128)(2,1)S(1)}, bf16[1024,768]{1,0:T(8,128)(2,1)}, u32[]{:S(2)}) copy-start(bf16[1024,768]{1,0:T(8,128)(2,1)} %get-tuple-element.66) | copy-start | bytes 4718596
  149.4 2.5 %copy-start = (f32[1024,768]{1,0:T(8,128)S(1)}, f32[1024,768]{1,0:T(8,128)}, u32[]{:S(2)}) copy-start(f32[1024,768]{1,0:T(8,128)} %get-tuple-element.67) | copy-start | bytes 9437188

commit v7 on v6

--- a/solution.py
+++ b/solution.py
@@ -273,10 +273,10 @@
     def takes(self, name, count):
         return {k: self.take(name + str(k)) for k in range(count)}
 
-    def hook(self, turn, taken):
+    def hook(self, turn, taken, per=1, q=0):
         for k, steps in taken.items():
-            if steps:
-                @pl.when(turn == k)
+            if steps and k % per == q:
+                @pl.when(turn == k // per)
                 def _():
                     for p, at in steps:
                         self.step(p, at)
@@ -536,12 +536,15 @@
     swap1.start()
 
     loads[3].wait()
+    loads[4].wait()
+    loads[5].wait()
     tri0, tri1 = iota((Q, Q), 0), iota((Q, Q), 1)
     lower, upper = tri0 > tri1, tri0 < tri1
 
     def within(blk, _):
         rows = part(blk, TB)
         r.gate[rows, :] = nn(r.buf[rows, :], r.wg[...])
+        r.dy[rows, :] = nt(r.cot[rows, :], r.wo[...])
         for q in range(per):
             chunk = blk * per + q
             at = part(chunk, Q)
@@ -565,8 +568,6 @@
         return 0
 
     lax.fori_loop(0, nblk, within, 0)
-    loads[4].wait()
-    loads[5].wait()
     swap1.finish()
     hf = chain(r.low1) * before_f
     hr = chain(r.high1) * after_f
@@ -579,8 +580,7 @@
 
     def enter(blk, _):
         lane = iota((Q, 128), 1)
-        u_all = nt(r.cot[part(blk, TB), :], r.wo[...])
-        r.dy[part(blk, TB), :] = u_all
+        u_all = r.dy[part(blk, TB), :]
         for q in range(per):
             chunk = blk * per + q
             at = part(chunk, Q)
@@ -590,16 +590,17 @@
             state = r.state[chunk]
             efe, ere = widen(spread2, ef, er)
             ys = nn(maps_here[:, 64:128], state[0:64]) * efe + nn(maps_here[:, 192:256], state[64:128]) * ere
-            square = jnp.zeros((Q, 1), F32)
-            cross = jnp.zeros((Q, 1), F32)
+            square = jnp.zeros((Q, 128), F32)
+            cross = jnp.zeros((Q, 128), F32)
             for j in range(inner // 128):
                 lanes = slice(j * 128, (j + 1) * 128)
                 y = r.mixed[at, lanes] + ys[:, lanes]
                 r.mixed[at, lanes] = y
                 gated = y * silu(r.gate[at, lanes])
-                square = square + jnp.sum(gated * gated, axis=1, keepdims=True)
-                cross = cross + jnp.sum(
-                    gated * (u_all[q * Q : (q + 1) * Q, lanes] * ggain[:, lanes]), axis=1, keepdims=True)
+                square = square + gated * gated
+                cross = cross + gated * (u_all[q * Q : (q + 1) * Q, lanes] * ggain[:, lanes])
+            square = jnp.sum(square, axis=1, keepdims=True)
+            cross = jnp.sum(cross, axis=1, keepdims=True)
             two = jnp.where(lane == 0, square, jnp.where(lane == 1, cross, 0.0))
             r.mine[blk, :, q * Q : (q + 1) * Q] = two.T[0:8]
         over(r.mine.at[blk], r.other.at[blk], r.sum_sem, blk).start()
@@ -670,7 +671,7 @@
     diag = tri0 == tri1
     r.rowbuf[...] = jnp.zeros_like(r.rowbuf)
 
-    taken_within = red.takes("within", nblk)
+    taken_within = red.takes("within", nchunk)
 
     def back_within(blk, _):
         for q in range(per):
@@ -713,8 +714,7 @@
             r.mixed[at, inner:] = jnp.concatenate(
                 [nn(dsf.astype(BF16), readf), nn(dsf.T.astype(BF16), entf),
                  nn(dsr.astype(BF16), readr), nn(dsr.T.astype(BF16), entr)], axis=1)
-
-        red.hook(blk, taken_within)
+            red.hook(blk, taken_within, per, q)
         return 0
 
     lax.fori_loop(0, nblk, back_within, 0)
@@ -737,7 +737,7 @@
 
     lower_low, upper_low = lower.astype(BF16), upper.astype(BF16)
 
-    taken_states = red.takes("states", nblk)
+    taken_states = red.takes("states", nchunk)
 
     def back_states(blk, _):
         for q in range(per):
@@ -784,6 +784,7 @@
             r.gstep[:, at] = graw.astype(BF16)
             r.hsum[:, 0:1] += jnp.sum(graw, axis=1, keepdims=True)
             r.hsum[:, 1:2] += jnp.sum(dld * ld, axis=1, keepdims=True)
+            red.hook(blk, taken_states, per, q)
 
         @pl.when(blk == 0)
         def _():
@@ -803,7 +804,6 @@
             def _():
                 lent_copy(me - 1).start()
 
-        red.hook(blk, taken_states)
         return 0
 
     lax.fori_loop(0, nblk, back_states, 0)
@@ -819,6 +819,7 @@
     def back_conv(g):
         cols = slice(g * 256, (g + 1) * 256)
         r.ext[...] = jnp.zeros_like(r.ext)
+        taken = red.takes(f"conv{g}_", nblk)
 
         def one(i, _):
             blk = nblk - 1 - i
@@ -840,6 +841,7 @@
                 r.buf[rows, cols] = grad.astype(BF16)
             else:
                 r.gs_mine[rows, :] = grad.astype(BF16)
+            red.hook(i, taken)
             return 0
 
         lax.fori_loop(0, nblk, one, 0)
@@ -849,8 +851,6 @@
     gs_copy.start()
     cg_copy = over(r.cg_mine.at[:, pl.ds(inner, maps)], r.cg_other, r.misc_sem, 1)
     cg_copy.start()
-    red.at("maps")
-
     def finish_maps():
         gs_copy.wait()
         cg_copy.wait()
@@ -868,7 +868,6 @@
         red.start(of[f"gv{g}"])
         if g == 0:
             finish_maps()
-        red.at("conv" + str(g))
 
     taken_down = red.takes("down", nblk)
 
@@ -977,80 +976,91 @@
 
 TABLE_BITS = 4
 ORDERS = (
+    (0, 1, 2, 3),
+    (0, 1, 2, 3),
+    (3, 1, 0, 2),
+    (1, 2, 3, 0),
+    (2, 0, 1, 3),
     (1, 0, 3, 2),
-    (0, 1, 3, 2),
-    (0, 2, 1, 3),
-    (2, 3, 1, 0),
-    (1, 0, 2, 3),
+    (2, 0, 1, 3),
     (1, 2, 0, 3),
-    (0, 1, 2, 3),
-    (2, 1, 0, 3),
-    (1, 2, 0, 3),
+    (2, 0, 1, 3),
     (0, 1, 3, 2),
 )
 TABLE = {
-    "within1": (
-        (3, 0),
-    ),
-    "within2": (
-        (0, 0), (1, 0), (2, 0),
-    ),
     "within3": (
-        (4, 0), (5, 0),
+        (0, 0),
+    ),
+    "within4": (
+        (1, 0), (3, 0), (2, 0), (4, 0), (5, 0),
+    ),
+    "within7": (
+        (0, 1), (3, 1),
     ),
     "states0": (
-        (0, 1), (1, 1), (2, 1), (3, 1),
+        (4, 1), (5, 1), (1, 1), (2, 1),
     ),
     "states1": (
-        (4, 1), (5, 1),
+        (0, 2), (3, 2),
     ),
     "states2": (
-        (2, 2), (3, 2),
+        (2, 2), (4, 2),
     ),
     "states3": (
-        (0, 2), (1, 2), (4, 2), (5, 2),
-    ),
-    "maps": (
-        (2, 3), (3, 3),
-    ),
-    "conv0": (
-        (0, 3), (1, 3), (4, 3), (5, 3),
-    ),
-    "conv1": (
-        (2, 4), (3, 4),
-    ),
-    "conv2": (
-        (0, 4), (1, 4), (4, 4), (5, 4),
-    ),
-    "down0": (
-        (2, 5), (3, 5), (6, 0),
+        (1, 2), (3, 3), (5, 2),
+    ),
+    "states4": (
+        (0, 3), (2, 3), (4, 3),
+    ),
+    "states5": (
+        (3, 4), (1, 3), (5, 3),
+    ),
+    "states7": (
+        (2, 4), (0, 4), (4, 4),
+    ),
+    "conv3_1": (
+        (5, 4),
+    ),
+    "conv3_2": (
+        (1, 4),
+    ),
+    "conv0_0": (
+        (3, 5),
+    ),
+    "conv0_1": (
+        (2, 5), (4, 5), (0, 5),
+    ),
+    "conv1_0": (
+        (5, 5), (1, 5),
+    ),
+    "conv1_2": (
+        (4, 6),
+    ),
+    "conv1_3": (
+        (3, 6),
+    ),
+    "conv2_1": (
+        (0, 6), (2, 6),
     ),
     "down1": (
-        (5, 5),
-    ),
-    "down2": (
-        (4, 5), (7, 0), (8, 0),
+        (1, 6), (5, 6), (6, 0),
     ),
     "down3": (
-        (0, 5), (1, 5), (6, 1), (9, 0),
-    ),
-    "end2": (
-        (2, 6), (3, 6), (4, 6), (7, 1),
-    ),
-    "end3": (
-        (0, 6),
+        (9, 0),
     ),
     "tail": (
-        (5, 6), (6, 2), (8, 1), (1, 6), (9, 1), (6, 3), (7, 2), (9, 2), (8, 2), (6, 4), (7, 3), (3, 7),
-        (9, 3), (8, 3), (2, 7), (7, 4), (1, 7), (6, 5), (4, 7), (9, 4), (8, 4), (7, 5), (0, 7), (5, 7),
-        (8, 5), (9, 5), (6, 6), (7, 6), (8, 6), (9, 6), (6, 7), (7, 7), (8, 7), (9, 7),
+        (4, 7), (3, 7), (0, 7), (7, 0), (6, 1), (2, 7), (8, 0), (1, 7), (9, 1), (7, 1), (6, 2), (5, 7),
+        (8, 1), (7, 2), (9, 2), (6, 3), (8, 2), (7, 3), (9, 3), (6, 4), (8, 3), (7, 4), (9, 4), (6, 5),
+        (7, 5), (8, 4), (9, 5), (6, 6), (8, 5), (7, 6), (9, 6), (8, 6), (6, 7), (7, 7), (9, 7), (8, 7),
     ),
 }
 
 
-def last_kernel(heads, ggw_ref, gow_ref, gvw_ref, gsw_ref, tiny_ref,
+def last_kernel(heads, ggw_ref, gow_ref, gvw_ref, gsw_ref, tiny_ref, out_ref, gh_ref,
                 ngain_ref, ggwo_ref, gvwo_ref, gswo_ref, gsteo_ref, convv_ref, convs_ref, bias_ref, decay_ref,
-                skip_ref, ggain_ref, gowo_ref):
+                skip_ref, ggain_ref, gowo_ref, outo_ref, gho_ref):
+    outo_ref[...] = out_ref[...]
+    gho_ref[...] = gh_ref[...]
     ggwo_ref[...] = ggw_ref[...].astype(F32)
     gvwo_ref[...] = gvw_ref[...].astype(F32)
     maps = gswo_ref.shape[1]
@@ -1151,26 +1161,28 @@
       norm_gain, step_proj.transpose(2, 0, 1), conv_value, conv_state, step_bias, decay_log, skip_scale, gate_gain)
     block_out, grad_hidden, ggw, gow, gvw, gsw, tiny = outs
 
-    rows = 128
+    rows = 384
     def tall(cols):
         return pl.BlockSpec((rows, cols), lambda i: (i, 0))
 
     def whole(*dims):
         return pl.BlockSpec(dims, lambda i: (0,) * len(dims))
 
-    assert width % rows == 0 and inner % rows == 0 and inner == width
+    steps = width // rows
+    tokens = pl.BlockSpec((length // steps, width), lambda i: (i, 0))
+    assert width % rows == 0 and length % steps == 0 and inner % rows == 0 and inner == width
     final = pl.pallas_call(
         partial(last_kernel, heads),
         grid=(width // rows,),
-        in_specs=[tall(inner), tall(width), tall(inner), tall(maps + 128), whole(8, both)],
+        in_specs=[tall(inner), tall(width), tall(inner), tall(maps + 128), whole(8, both), tokens, tokens],
         out_specs=[whole(width), tall(inner), tall(inner), tall(maps), pl.BlockSpec((heads, 2, rows), lambda i: (0, 0, i)), whole(4, inner),
-                   whole(4, maps), whole(2, heads), whole(heads), whole(heads), whole(inner), tall(width)],
+                   whole(4, maps), whole(2, heads), whole(heads), whole(heads), whole(inner), tall(width), tokens, tokens],
         out_shape=[shape(width), shape(width, inner), shape(width, inner), shape(width, maps),
                    shape(heads, 2, width), shape(4, inner), shape(4, maps), shape(2, heads), shape(heads),
-                   shape(heads), shape(inner), shape(inner, width)],
+                   shape(heads), shape(inner), shape(inner, width), shape(length, width, **low), shape(length, width)],
         compiler_params=pltpu.CompilerParams(dimension_semantics=("arbitrary",), vmem_limit_bytes=60 * MIB),
-    )(ggw, gow, gvw, gsw, tiny)
-    ngain, ggw, gvw, gsw, gstepw, convv, convs, bias, decay, skip, ggain, gow = final
+    )(ggw, gow, gvw, gsw, tiny, block_out, grad_hidden)
+    ngain, ggw, gvw, gsw, gstepw, convv, convs, bias, decay, skip, ggain, gow, block_out, grad_hidden = final
     return (block_out, grad_hidden, ngain, ggw, gvw, gsw, gstepw.transpose(1, 2, 0), convv, convs, bias, decay, skip,
             ggain, gow)
 

time: 154 us -> 150 us (0.974)
  local copies, waits for them, and re-layouts: 4.12 us -> 0 us
    unnamed x6 -> x0, local copies, waits for them, and re-layouts: 4.12 us -> none
where the time goes in v7:
time: 150 us
  Pallas kernels  149 us (99%)
    pallas_call x1, Pallas kernels, body(): pl.pallas_call(partial(layer_kernel, reach, bits, NAMES_IN + NAMES_OUT +...  141 us
    pallas_call x1, Pallas kernels, body(): pl.pallas_call(partial(last_kernel, heads), grid=(width // rows,), in_spe...  7.79 us

profile of v7, /device:TPU:0, one launch (start us, length us, event | category | flops | bytes accessed | tf_op | source)
XLA Modules:
  0.0 149.9 jit_solution(8845601841870749688)
XLA Ops:
  0.7 141.3 %shard_map.254 = (bf16[1024,768]{1,0:T(8,128)(2,1)}, f32[1024,768]{1,0:T(8,128)}, bf16[768,768]{1,0:T(8,128)(2,1)}, bf16[768,768]{1,0:T(8,128)(2,1)}, bf16[768,7...) custom-call(s32[9]{0:T(128)} %refs_0_.1, bf16[1024,768]{1,0:T(8,128)(2,1)} %refs_1_.1, ...), custom_call_target="tpu_custom_call" | custom-call | tf_op jit(solution)/shard_map/pallas_call | solution.py:1150
  141.9 7.8 %shard_map.255 = (f32[768]{0:T(1024)}, f32[768,768]{1,0:T(8,128)}, f32[768,768]{1,0:T(8,128)}, f32[768,256]{1,0:T(8,128)}, f32[12,2,768]{2,1,0:T(2,128)}, /*inde...) custom-call(bf16[768,768]{1,0:T(8,128)(2,1)} %get-tuple-element.35.g, ...), custom_call_target="tpu_custom_call" | custom-call | tf_op jit(solution)/shard_map/pallas_call | solution.py:1174
